TPU v7x, 32 devices: a whole 2x2x4 slice. The times are simulated.
32 devices in a mesh: ctx: 8 (over z, x), grp: 4 (over y, core).
Axes of the slice: x: 2, y: 2, z: 4, core: 2. Of those that a mesh axis runs over, the one named last changes fastest.
Arguments:
- out_grad: bfloat16 [4096, 2048], P('ctx', 'grp'), may hold values from -6 to 6
- filter_mats: bfloat16 [16, 2048, 2048], P('grp', 'ctx'), may hold values from -0.125 to 0.125
- coeffs: float32 [16, 80], replicated, may hold values from -0.15625 to 0.15625
- pole_rates: float32 [80], replicated, may hold values from 4.8828124e-06 to 0.03
Outputs:
- in_grad: bfloat16 [4096, 2048], P('ctx', 'grp')
All inputs are finite; a program needn't handle non-finite values.
Results may differ from a plain program's by a relative error of at most 0.001.
Values may be sent and summed in bfloat16 or wider, within the bound.
No kernel may reach another device: no remote copies, remote signals or barrier semaphores. Data moves between devices by JAX's collectives and lax.ppermute only.
A program may use at most 128 MiB of HBM per device.

v0:
```python
import jax
import jax.numpy as jnp
from jax import lax
from jax.sharding import PartitionSpec as P

exact_prec = lax.Precision.HIGHEST


def entering(array, axis, combine, identity):
    count, here = (lax.axis_size(axis), lax.axis_index(axis))
    everything = jax.tree.map(lambda part: lax.all_gather(part, axis), array)
    start = jax.tree.map(
        lambda part, zero: jnp.broadcast_to(jnp.asarray(zero, part.dtype), part.shape),
        array,
        identity,
    )

    def step(k, before):
        at = count - 1 - k
        reached = at > here
        new = combine(before, jax.tree.map(lambda part: part[at], everything))
        return jax.tree.map(lambda a, b: jnp.where(reached, a, b), new, before)

    return lax.fori_loop(0, count, step, start)


def merge_suffix(earlier, latter):
    carried_e, factor_e = earlier
    carried_l, factor_l = latter
    return (carried_l + factor_l * carried_e, factor_l * factor_e)


def per_device(out_grad, filter_mats, coeffs, pole_rates):
    full_grad = lax.all_gather(out_grad, "grp", axis=1, tiled=True)
    length = full_grad.shape[0]
    col_width = out_grad.shape[1]
    poles = pole_rates.shape[0]
    positions = jnp.arange(length, dtype=jnp.float32)
    pole_gains = jnp.sqrt(-jnp.expm1(-2.0 * pole_rates))
    middle = float(length // 2)
    rising = jnp.exp(-(positions[:, None] - middle) * pole_rates[None, :])
    falling = jnp.exp((positions[:, None] - middle) * pole_rates[None, :])
    causal = positions[:, None] >= positions[None, :]
    decay_pos = jnp.exp(-positions[:, None] * pole_rates[None, :])
    edge_decay = pole_gains[None, :] * jnp.exp(-(length - positions)[:, None] * pole_rates[None, :])
    block_decay = jnp.exp(-length * pole_rates)[:, None]
    unit_factor = jnp.ones((poles, 1), jnp.float32)
    groups = lax.axis_size("grp")
    blocks_ctx = lax.axis_size("ctx")
    swapped = lax.all_to_all(filter_mats, "grp", split_axis=1, concat_axis=0, tiled=True)
    kernel_mat = jnp.einsum(
        "tp,kp,sp->kts", rising, coeffs * pole_gains[None, :], falling, precision=exact_prec
    )
    kernel_mat = jnp.where(causal[None], kernel_mat, 0.0)
    weights = coeffs[:, :, None] * decay_pos.T[None]
    proj_grad = jnp.einsum(
        "tj,kij->kti",
        full_grad,
        lax.all_gather(swapped, "ctx", axis=1, tiled=True),
        preferred_element_type=jnp.float32,
    )
    near_part = jnp.einsum("kts,kti->si", kernel_mat, proj_grad, precision=exact_prec)
    pole_part = jnp.einsum("kpt,kti->pi", weights, proj_grad, precision=exact_prec)
    stacked = jnp.concatenate([near_part, pole_part], axis=0)
    pole_part = stacked[length:]
    later_part = entering(
        (pole_part, block_decay), "ctx", merge_suffix, (jnp.zeros_like(pole_part), unit_factor)
    )[0]
    strided = (stacked[:length] + jnp.dot(edge_decay, later_part, precision=exact_prec)).astype(
        jnp.bfloat16
    )
    returned = lax.all_to_all(strided, "grp", split_axis=1, concat_axis=1, tiled=True)
    per_group = blocks_ctx // groups
    narrow = col_width // per_group // groups
    ordered = returned.reshape(length, groups, per_group, narrow).transpose(0, 2, 1, 3)
    return ordered.reshape(length, col_width)


def solution(mesh):
    placed = (P("ctx", "grp"), P("grp", "ctx", None), P(), P())
    return jax.shard_map(
        per_device, mesh=mesh, in_specs=placed, out_specs=P("ctx", "grp"), check_vma=False
    )
```

profile of v0, /device:TPU:4, one launch (start us, length us, event | category | flops | bytes accessed | tf_op | source)
XLA Modules:
  0.0 845.0 jit_solution(15606808902696085806)
XLA Ops:
  6.5 7.4 copy.17
  14.0 4.8 all-to-all-start
  18.9 0.7 all-gather.8.cloned.1.call-update
  19.6 56.1 %all-to-all-done = bf16[4,256,2048]{2,0,1:T(4,128)(2,1)} async-done(((bf16[4,256,2048]{2,0,1:T(4,128)(2,1)}), bf16[4,256,2048]{2,0,1:T(4,128)(2,1)}, u32[]{:S(2)}, u32[]{:S(2)}) %all-to-all-start) | async-done | bytes 4194336 | tf_op jit(solution)/shard_map/all_to_all | solution.py:50
  75.7 6.6 copy.18
  82.4 0.6 dynamic-slice
  83.7 65.8 %all-reduce = f32[640]{0:T(1024)S(1)} all-reduce(f32[640]{0:T(1024)S(1)} %get-tuple-element.166), channel_id=3, replica_groups=mesh['ctx'=8,'grp'=4] {'ctx'}, use_global_device_ids=true, to_apply=%add | all-reduce | flops 640 | bytes 5120
  150.2 573.3 %all-gather.6.cloned.1.call-done = bf16[16,512,2048]{2,1,0:T(8,128)(2,1)} async-done(((bf16[16,64,2048]{2,1,0:T(8,128)(2,1)}), bf16[16,512,2048]{2,1,0:T(8,128)(2,1)}) %all-gather.6.cloned.1.call-update) | async-done | bytes 33554448 | tf_op jit(solution)/shard_map/all_gather | solution.py:59
  723.4 27.5 %fusion.12 = f32[16,512,512]{2,1,0:T(8,128)} fusion(bf16[16,512,2048]{2,1,0:T(8,128)(2,1)} %all-gather.6.cloned.1.call-done, bf16[512,2048]{1,0:T(8,128)(2,1)} %all-gather.8.cloned.1.call-done), kind=kOutput, calls=%fused_computation.14 | convolution fusion | flops 17179869184 | bytes 52428800 | tf_op jit(solution)/shard_map/tj,kij->kti/dot_general | solution.py:56
  750.9 21.1 %fusion.24 = f32[80,512]{1,0:T(8,128)} fusion(f32[16,512,512]{2,1,0:T(8,128)} %fusion.12, f32[80,512]{1,0:T(8,128)S(1)} %multiply_exponential_fusion, f32[16,80]{1,0:T(8,128)S(1)} %copy-done), kind=kOutput, calls=%fused_computation.23 | convolution fusion | flops 4027187200 | bytes 17110016 | tf_op jit(solution)/shard_map/kpt,kti->pi/dot_general | solution.py:63
  772.0 14.7 %fusion.8 = f32[16,512,512]{2,1,0:T(8,128)S(1)} fusion(f32[80,512]{1,0:T(8,128)S(1)} %exponential_bitcast_fusion, f32[80,16]{0,1:T(8,128)S(1)} %multiply_bitcast_fusion, f32[512]{0:T(512)S(1)} %iota_add_fusion, f32[80]{0:T(128)S(1)} %copy-done.1), kind=kOutput, calls=%fused_computation.10 | convolution fusion | flops 4027228160 | bytes 16948544 | tf_op jit(solution)/shard_map/tp,kp,sp->kts/dot_general | solution.py:51
  786.8 30.6 %fusion.14 = f32[512,512]{0,1:T(8,128)S(1)} fusion(f32[16,512,512]{2,1,0:T(8,128)} %fusion.12, f32[16,512,512]{2,1,0:T(8,128)S(1)} %fusion.8, pred[512,512]{1,0:T(8,128)(4,1)S(1)} %iota_compare_fusion), kind=kOutput, calls=%fused_computation.17 | convolution fusion | flops 25773998080 | bytes 34865152 | tf_op jit(solution)/shard_map/kts,kti->si/dot_general | solution.py:62
  817.4 8.5 %while.16 = (s32[]{:T(128)}, f32[80,512]{1,0:T(8,128)S(1)}, s32[]{:T(128)}, f32[8,80,512]{2,1,0:T(8,128)}, f32[8,80,1]{1,2,0:T(1,128)S(1)}, /*index=5*/s32[]{:T(128)}, s32[]{:T(128)}, s32[]{:T(128)}, s32[]{:T(128)}) while((s32[]{:T(128)}, f32[80,512]{1,0:T(8,128)S(1)}, s32[]{:T(128)}, f32[8,80,512]{2,1,0:T(8,128)}, ...), condition=%wide.region_1.2_spmd.clone, body=%wide.region_0.1_spmd.clone.sunk | while | flops 163848 | bytes 492655 | solution.py:24
  817.4 1.0 fusion.45
  818.5 1.0 fusion.45
  819.6 1.0 fusion.45
  820.6 1.0 fusion.45
  821.7 1.0 fusion.45
  822.7 1.0 fusion.45
  823.8 1.0 fusion.45
  824.9 1.0 fusion.45
  825.9 1.1 fusion.23
  827.0 10.3 %all_to_all.27 = bf16[512,4,128]{0,2,1:T(8,128)(2,1)S(1)} all-to-all(bf16[512,4,128]{0,2,1:T(8,128)(2,1)S(1)} %bitcast.50), channel_id=1, replica_groups=mesh['ctx'=8,'grp'=4] {'grp'}, dimensions={1} | all-to-all | bytes 1048576 | tf_op jit(solution)/shard_map/all_to_all | solution.py:72
  837.3 1.0 copy.21
  (34 shorter events, 0.9 us)
Async XLA Ops:
  6.5 75.8 %copy-start.2 = (u32[32]{0:T(128)S(1)}, u32[32]{0:T(128)}, u32[]{:S(2)}) copy-start(u32[32]{0:T(128)} %constant.64) | copy-start | bytes 388
  6.5 77.1 %copy-start.1 = (f32[80]{0:T(128)S(1)}, f32[80]{0:T(128)}, u32[]{:S(2)}) copy-start(f32[80]{0:T(128)} %param.9) | copy-start | bytes 964
  6.5 143.4 %copy-start = (f32[16,80]{1,0:T(8,128)S(1)}, f32[16,80]{1,0:T(8,128)}, u32[]{:S(2)}) copy-start(f32[16,80]{1,0:T(8,128)} %param.8) | copy-start | bytes 15364
  14.0 61.7 %all-to-all-start = ((bf16[4,256,2048]{2,0,1:T(4,128)(2,1)}), bf16[4,256,2048]{2,0,1:T(4,128)(2,1)}, u32[]{:S(2)}, u32[]{:S(2)}) async-start(bf16[4,256,2048]{2,0,1:T(4,128)(2,1)} %copy.17), calls=%async_computation | async-start | bytes 8388608 | tf_op jit(solution)/shard_map/all_to_all | solution.py:50
  18.8 131.4 %all-gather.8.cloned.1.call-start = ((), (), s32[]{:S(2)}) async-start(), calls=%async_computation.3 | async-start | bytes 2621440 | tf_op jit(solution)/shard_map/all_gather | solution.py:34
  19.6 703.9 %all-gather.6.cloned.1.call-start = ((), (), s32[]{:S(2)}) async-start(), calls=%async_computation.2 | async-start | bytes 37748736 | tf_op jit(solution)/shard_map/all_gather | solution.py:59
  82.3 735.1 %all-gather.10.cloned.1.call-start = ((), (), s32[]{:S(2)}) async-start(), calls=%async_computation.4 | async-start | bytes 1474560 | tf_op jit(solution)/shard_map/all_gather | solution.py:11
Sparse Core Ops, SparseCore 0:
  21.2 34.4 all-gather.7
  82.4 641.0 all-gather.5
  772.2 42.0 all-gather.9
where the time goes:
time: 853 us; the launch traced here: 845 us
  waiting for transfers between devices  630 us (74%)
  matrix products  95 us (11%)
  blocking collectives  76.1 us (9%)
  local copies, waits for them, and re-layouts  15.8 us (2%)
  between operations  14.1 us (2%)
  other arithmetic  8.63 us (1%)
    all_gather x1, waiting for transfers between devices, per_device(): lax.all_gather(swapped, 'ctx', axis=1, tiled=True)  573 us
    unnamed x1, blocking collectives  65.8 us
    all_to_all x1, waiting for transfers between devices, per_device(): lax.all_to_all(filter_mats, 'grp', split_axis=1, concat_axis=0, tiled=True)  56.1 us
    dot_general x1, matrix products, per_device(): jnp.einsum('kts,kti->si', kernel_mat, proj_grad, precision=exact_prec)  30.6 us
    dot_general x1, matrix products, per_device(): jnp.einsum('tj,kij->kti', full_grad, lax.all_gather(swapped, 'ctx', axis=...  27.5 us
    dot_general x1, matrix products, per_device(): jnp.einsum('kpt,kti->pi', weights, proj_grad, precision=exact_prec)  21.1 us
  transfers between devices with their start and end apart: 4, of which 2 were waited for; matrix products, arithmetic and copies ran while one was open for 6% of the time, Pallas kernels for 0%

commit v1 on v0

v1 whole, which is shorter than its diff:
```python
import functools

import jax
import jax.numpy as jnp
import numpy as np
from jax import lax
from jax.experimental import pallas as pl
from jax.experimental.pallas import tpu as pltpu
from jax.sharding import PartitionSpec as P

exact_prec = lax.Precision.HIGHEST
f32, bf16 = jnp.float32, jnp.bfloat16
NT = (((1,), (1,)), ((), ()))
VM = pl.BlockSpec(memory_space=pltpu.VMEM)
ANY = pl.BlockSpec(memory_space=pl.ANY)
SM = pl.BlockSpec(memory_space=pltpu.SMEM)


def params(mib=16):
    return pltpu.CompilerParams(vmem_limit_bytes=mib * 2**20)


def split2(x):
    high = x.astype(bf16)
    return high, (x - high.astype(f32)).astype(bf16)


def tables_kernel(poles_ref, out):
    poles, height, width = poles_ref.shape[0], out.shape[1], out.shape[2] // 4
    step = width // 2
    rate, gain = poles_ref[:, 0:1], poles_ref[:, 1:2]
    lag = lax.broadcasted_iota(jnp.int32, (poles, width), 1).astype(f32)
    decay = jnp.exp(-rate * lag)
    gained = gain * decay
    columns = lax.broadcasted_iota(jnp.int32, (poles, poles_ref.shape[1]), 1)

    @pl.loop(0, out.shape[0])
    def _(pair):
        for j in range(2):
            chosen = jnp.where(columns == 2 + 2 * pair + j, poles_ref[...], 0.0)
            coef = jnp.sum(chosen, axis=1, keepdims=True)
            phi = jnp.sum(coef * gained, axis=0, keepdims=True)
            line = jnp.concatenate([phi, jnp.zeros((1, step), f32)], axis=1)
            rolled = pltpu.roll(jnp.broadcast_to(line, (step, width + step)), 0, 1, stride=1, stride_axis=0)
            high, low = split2(rolled[:, :width])
            wh, wl = split2(coef * decay)
            for at, near, weight in ((j, high, wh), (2 + j, low, wl)):
                lo = at * width
                out[pair, :step, lo : lo + width] = near
                out[pair, step:width, lo : lo + step] = jnp.zeros((step, step), bf16)
                out[pair, step:width, lo + step : lo + width] = near[:, :step]
                out[pair, width:, lo : lo + width] = weight


def tables(coeffs, rates, gains, width):
    filters, poles = coeffs.shape
    joined = jnp.concatenate([rates[:, None], gains[:, None], coeffs.T], axis=1)
    return pl.pallas_call(
        tables_kernel,
        in_specs=[VM],
        out_specs=VM,
        out_shape=jax.ShapeDtypeStruct((filters // 2, width + poles, 4 * width), bf16),
        compiler_params=params(),
        cost_estimate=pl.CostEstimate(flops=int(4e9), bytes_accessed=0, transcendentals=0),
        name="pole_tables",
    )(joined)


def cut_kernel(plan, info, mats, *refs):
    outs, sems = refs[:-1], refs[-1]
    copies = []
    for i, (lo, n) in enumerate(plan):
        half, cols = outs[i].shape[1:]
        src = mats.at[
            pl.ds(lo, n),
            pl.ds(pl.multiple_of(info[2 * i], half), half),
            pl.ds(pl.multiple_of(info[2 * i + 1], cols), cols),
        ]
        copies.append(pltpu.make_async_copy(src, outs[i], sems.at[i]))
    for c in copies:
        c.start()
    for c in copies:
        c.wait()


def cut(mats, info, plan, half, cols):
    return pl.pallas_call(
        functools.partial(cut_kernel, plan),
        in_specs=[SM, ANY],
        out_specs=[ANY] * len(plan),
        out_shape=[jax.ShapeDtypeStruct((n, half, cols), bf16) for _, n in plan],
        scratch_shapes=[pltpu.SemaphoreType.DMA((len(plan),))],
        compiler_params=params(),
        name="cut_filters",
    )(info, mats)


def blocks_kernel(blocks, sets, fresh, info, *refs):
    mine, other = refs[:blocks], refs[blocks : 2 * blocks]
    mats = refs[2 * blocks : 2 * blocks + sets]
    table = refs[2 * blocks + sets]
    rest = refs[2 * blocks + sets + 1 :]
    before, after, held = rest[:-blocks - 1], rest[-blocks - 1 : -1], rest[-1]
    wide = mine[0].shape[1]
    here = info[0]
    width = table.shape[2] // 4
    half = mats[0].shape[1]
    for b in range(blocks):
        after[b][...] = jnp.zeros_like(after[b]) if fresh else before[b][...]

    @pl.loop(0, mats[0].shape[0] // 2)
    def _(i):
        for n in range(sets):
            two = mats[n].at[pl.ds(2 * i, 2)]
            m_mine = two[:, :, pl.ds(pl.multiple_of(here * wide, wide), wide)].reshape(2 * half, wide)
            m_other = two[:, :, pl.ds(pl.multiple_of((1 - here) * wide, wide), wide)].reshape(2 * half, wide)
            for b in range(blocks):
                proj = lax.dot_general(mine[b][...], m_mine, NT, preferred_element_type=f32)
                proj += lax.dot_general(other[b][...], m_other, NT, preferred_element_type=f32)
                for at, part in enumerate(split2(proj)):
                    for j in range(2):
                        rows = pl.ds((2 * at + j) * width, width)
                        for s in range(2):
                            held[n, b, rows, s * half : (s + 1) * half] = part[
                                s * width : (s + 1) * width, j * half : (j + 1) * half
                            ]
        for n in range(sets):
            pair = info[1 + n] + i
            for b in range(blocks):
                high, low = held[n, b, : 2 * width, :], held[n, b, 2 * width :, :]
                add = jnp.dot(table[pair, :, : 2 * width], high, preferred_element_type=f32)
                add += jnp.dot(table[pair, :, 2 * width :], high, preferred_element_type=f32)
                add += jnp.dot(table[pair, :, : 2 * width], low, preferred_element_type=f32)
                after[b][...] += add


def add_blocks(info, mine, other, mats, table, totals):
    blocks, sets, fresh = len(mine), len(mats), totals is None
    half = mats[0].shape[1]
    height, tw = table.shape[1:]
    total = jax.ShapeDtypeStruct((height, 2 * half), f32)
    units = blocks * sets * mats[0].shape[0] // 2
    return pl.pallas_call(
        functools.partial(blocks_kernel, blocks, sets, fresh),
        in_specs=[SM] + [VM] * (2 * blocks + sets + 1 + (0 if fresh else blocks)),
        out_specs=[VM] * blocks,
        out_shape=[total] * blocks,
        scratch_shapes=[pltpu.VMEM((sets, blocks, tw, 2 * half), bf16)],
        input_output_aliases={} if fresh else {1 + 2 * blocks + sets + 1 + b: b for b in range(blocks)},
        compiler_params=params(),
        cost_estimate=pl.CostEstimate(flops=int(units * 0.69e9), bytes_accessed=0, transcendentals=0),
        name="add_blocks",
    )(info, *mine, *other, *mats, table, *([] if fresh else totals))


def finish_kernel(count, ways, info, *refs):
    totals, (edge, decay) = refs[:count], refs[count : count + 2]
    outs = refs[count + 2 : 2 * count + 2]
    held, entering, sems = refs[2 * count + 2 :]
    copies = [pltpu.make_async_copy(totals[s], held.at[info[s]], sems.at[s]) for s in range(count)]
    for c in copies:
        c.start()
    width, poles = edge.shape
    half = held.shape[2] // 2
    eh, el = split2(edge[...])
    left = jnp.concatenate([eh, el, eh], axis=1)
    for c in copies:
        c.wait()
    carried = jnp.zeros((poles, half), f32)
    for c in reversed(range(count)):
        state = held[c, width:, :]
        inner = state[:, half:] + decay[...] * carried
        ch, cl = split2(jnp.concatenate([inner, carried], axis=1))
        entering[c] = jnp.concatenate([ch, ch, cl], axis=0)
        carried = state[:, :half] + decay[...] * inner
    for n in range(count):
        c = info[count + n]
        value = held[c, :width, :] + jnp.dot(left, entering[c], preferred_element_type=f32)
        outs[n][:width, :] = value[:, :half]
        outs[n][width:, :] = value[:, half:]


def finish(info, totals, edge, decay, ways):
    count = len(totals)
    height, tw = totals[0].shape
    width, poles = edge.shape
    return pl.pallas_call(
        functools.partial(finish_kernel, count, ways),
        in_specs=[SM] + [ANY] * count + [VM, VM],
        out_specs=[VM] * count,
        out_shape=[jax.ShapeDtypeStruct((2 * width, tw // 2), f32)] * count,
        scratch_shapes=[
            pltpu.VMEM((count, height, tw), f32),
            pltpu.VMEM((count, 3 * poles, tw), bf16),
            pltpu.SemaphoreType.DMA((count,)),
        ],
        compiler_params=params(),
        cost_estimate=pl.CostEstimate(flops=int(3e9), bytes_accessed=0, transcendentals=0),
        name="finish_blocks",
    )(info, *totals, edge, decay)


def combine_kernel(*refs):
    value = refs[0][...]
    for r in refs[1:-1]:
        value = value + r[...]
    refs[-1][...] = value.astype(bf16)


def combine(parts):
    return pl.pallas_call(
        combine_kernel,
        in_specs=[VM] * len(parts),
        out_specs=VM,
        out_shape=jax.ShapeDtypeStruct(parts[0].shape, bf16),
        compiler_params=params(),
        name="combine_ways",
    )(*parts)


def arrange_kernel(count, info, *refs):
    out = refs[count]
    lanes = refs[0].shape[1]
    for r in range(count):
        out[:, pl.ds(pl.multiple_of(info[r] * lanes, lanes), lanes)] = refs[r][...]


def arrange(info, parts):
    rows, lanes = parts[0].shape
    return pl.pallas_call(
        functools.partial(arrange_kernel, len(parts)),
        in_specs=[SM] + [VM] * len(parts),
        out_specs=VM,
        out_shape=jax.ShapeDtypeStruct((rows, lanes * len(parts)), bf16),
        compiler_params=params(),
        name="arrange_features",
    )(info, *parts)


def plain_tables(coeffs, rates, gains, width):
    lag = jnp.arange(width, dtype=f32)
    decay = jnp.exp(-rates[:, None] * lag[None, :])
    shift = lag[None, :] - lag[:, None]
    phi = jnp.dot(coeffs * gains[None, :], decay, precision=exact_prec)
    near = jnp.where(shift >= 0, phi[:, jnp.maximum(shift, 0).astype(jnp.int32)], 0.0)
    return jnp.concatenate([near, coeffs[:, :, None] * decay[None]], axis=1)


def plain_cut(mats, info, plan, half, cols):
    return [
        lax.dynamic_slice(mats, (lo, info[2 * i], info[2 * i + 1]), (n, half, cols)) for i, (lo, n) in enumerate(plan)
    ]


def plain_add(info, mine, other, mats, table, totals):
    results = []
    wide, width = mine[0].shape[1], table.shape[2]
    for b in range(len(mine)):
        rows = jnp.concatenate([mine[b], other[b]], axis=1)
        total = 0.0 if totals is None else totals[b]
        for n in range(len(mats)):
            use = lax.dynamic_slice_in_dim(table, 2 * info[1 + n], mats[n].shape[0], 0)
            swapped = jnp.where(info[0] == 0, mats[n], jnp.roll(mats[n], wide, axis=2))
            proj = jnp.einsum("tj,kij->kti", rows, swapped, preferred_element_type=f32)
            proj = jnp.concatenate([proj[:, :width], proj[:, width:]], axis=2)
            total = total + jnp.einsum("kst,kti->si", use, proj, precision=exact_prec)
        results.append(total)
    return results


def plain_finish(info, totals, edge, decay, ways):
    count = len(totals)
    width, half = edge.shape[0], totals[0].shape[1] // 2
    held = jnp.zeros((count,) + totals[0].shape, f32)
    for s in range(count):
        held = lax.dynamic_update_slice(held, totals[s][None], (info[s], 0, 0))
    carried, values = jnp.zeros((edge.shape[1], half), f32), [None] * count
    for c in reversed(range(count)):
        state = held[c, width:]
        inner = state[:, half:] + decay * carried
        far = jnp.dot(edge, jnp.concatenate([inner, carried], axis=1), precision=exact_prec)
        value = held[c, :width] + far
        values[c] = jnp.concatenate([value[:, :half], value[:, half:]], axis=0)
        carried = state[:, :half] + decay * inner
    values = jnp.stack(values)
    return [values[info[count + n]] for n in range(count)]


def plain_combine(parts):
    return sum(parts[1:], parts[0]).astype(bf16)


def plain_arrange(info, parts):
    rows, lanes = parts[0].shape
    out = jnp.zeros((rows, lanes * len(parts)), bf16)
    for r, part in enumerate(parts):
        out = lax.dynamic_update_slice(out, part, (0, info[r] * lanes))
    return out


def per_device(out_grad, filter_mats, coeffs, pole_rates):
    count, groups = lax.axis_size("ctx"), lax.axis_size("grp")
    ways, per_grp = groups // 2, count // groups
    per = count // ways
    own_filters, features, _ = filter_mats.shape
    length, wide = out_grad.shape
    half, width = features // 2, length // 2
    kernels = half % 128 == 0 and wide % 128 == 0 and width % 256 == 0 and pole_rates.shape[0] % 16 == 0
    make, slices, add, end, both, put = (
        (tables, cut, add_blocks, finish, combine, arrange)
        if kernels
        else (plain_tables, plain_cut, plain_add, plain_finish, plain_combine, plain_arrange)
    )

    order = [*range(0, count, 2), *reversed(range(1, count, 2))]
    right = [(order[i], order[(i + 1) % count]) for i in range(count)]
    left = [(b, a) for a, b in right]
    offsets = [0]
    for step in range(1, count // 2):
        offsets += [-step, step]
    offsets.append(count // 2)
    far_ways = [(w, h) for w in range(1, ways) for h in range(2)]
    plan = [(lo, 2) for lo in range(0, own_filters, 2) for _ in far_ways] + [(0, own_filters)] * 2
    to = far_ways * (own_filters // 2) + [(0, 1), (0, 0)]

    def numbers(ctx, grp):
        way, here, at = grp // 2, grp % 2, order.index(ctx)
        cuts, firsts, near_firsts = [], [], []
        for w, h in to:
            cuts += [(here ^ h) * half, (way + w) % ways * 2 * wide]
        pair = lambda w, h, lo: (((way - w) % ways) * 2 + (here ^ h)) * (own_filters // 2) + lo // 2
        firsts = [[here] + [pair(w, h, lo) for w, h in far_ways] for lo in range(0, own_filters, 2)]
        near_firsts = [here, pair(0, 1, 0), pair(0, 0, 0)]
        turn = ctx % per_grp * 2 + here
        slots = [order[(at + o) % count] for o in offsets]
        use = [ways * ((r + turn) % per) + (way + w + ctx) % ways for w in range(ways) for r in range(per)]
        lanes = [(ctx // ways - r) % per for r in range(per)]
        return [cuts, near_firsts, *firsts, slots + use, lanes]

    rows = [numbers(c, g) for c in range(count) for g in range(groups)]
    ends = np.cumsum([len(part) for part in rows[0]])
    known = jnp.asarray(np.array([sum(r, []) for r in rows], np.int32))
    me = lax.axis_index("ctx") * groups + lax.axis_index("grp")
    row = lax.dynamic_slice(known, (me, 0), (1, known.shape[1]))[0]
    cuts, near_info, *rest = [row[e - len(part) : e] for e, part in zip(ends, rows[0])]
    far_info, finish_info, lanes_info = rest[:-2], rest[-2], rest[-1]

    def over_grp(x, by_way, by_core):
        rank = lambda w, h: (w % ways) * 2 + h
        pairs = [(rank(w, h), rank(w + by_way, h ^ by_core)) for w in range(ways) for h in range(2)]
        return lax.ppermute(x, "grp", pairs)

    swap = lambda x: over_grp(x, 0, 1)

    mine, other = [out_grad], [swap(out_grad)]
    going_right, going_left = out_grad, out_grad
    for step in range(1, count // 2):
        going_right = lax.ppermute(going_right, "ctx", right)
        going_left = lax.ppermute(going_left, "ctx", left)
        mine += [going_right, going_left]
        other += [swap(going_right), swap(going_left)]
    last = jnp.concatenate(
        [lax.ppermute(going_right[:width], "ctx", right), lax.ppermute(going_left[width:], "ctx", left)]
    )
    mine.append(last)
    other.append(swap(last))

    pieces = slices(filter_mats, cuts, plan, half, 2 * wide)
    far = [over_grp(p, w, h) for p, (w, h) in zip(pieces, to[:-2])]
    near = [swap(pieces[-2]), pieces[-1]]

    gains = jnp.sqrt(-jnp.expm1(-2.0 * pole_rates))
    table = make(coeffs, pole_rates, gains, width)
    totals = [None] * count

    def run(slots, info, mats):
        have = None if totals[slots[0]] is None else [totals[s] for s in slots]
        got = add(info, [mine[s] for s in slots], [other[s] for s in slots], mats, table, have)
        for s, t in zip(slots, got):
            totals[s] = t

    twos = [[s, s + 1] for s in range(1, count - 1, 2)]
    for slots in [[0], *twos, [count - 1]]:
        run(slots, near_info, near)
    for i, info in enumerate(far_info):
        for slots in [*twos, [0, count - 1]]:
            run(slots, info, far[i * len(far_ways) : (i + 1) * len(far_ways)])

    step_back = jnp.arange(width, dtype=f32) - width
    edge = gains[None, :] * jnp.exp(step_back[:, None] * pole_rates[None, :])
    decay = jnp.exp(-width * pole_rates)[:, None]
    partial = end(finish_info, totals, edge, decay, ways)
    arrived = [[over_grp(partial[w * per + r], w, 0) for w in range(1, ways)] for r in range(per)]
    received = []
    for r in range(per):
        result = both([partial[r], *arrived[r]])
        pairs = []
        for c in range(count):
            for g in range(groups):
                m = (r + c % per_grp * 2 + g % 2) % per
                goal = ways * m + (g // 2 + c) % ways
                pairs.append((c * groups + g, goal * groups + c // per_grp))
        received.append(lax.ppermute(result, ("ctx", "grp"), pairs))
    return put(lanes_info, received)


def solution(mesh):
    placed = (P("ctx", "grp"), P("grp", "ctx", None), P(), P())
    return jax.shard_map(
        per_device, mesh=mesh, in_specs=placed, out_specs=P("ctx", "grp"), check_vma=False
    )
```

time: 853 us -> 151 us (0.18)
  waiting for transfers between devices: 630 us -> 38.8 us
  matrix products: 95 us -> 0 us
  blocking collectives: 76.1 us -> 0 us
  Pallas kernels: 0 us -> 65 us
  starting transfers between devices: 4.95 us -> 32.2 us
  between operations: 14.1 us -> 0.33 us
    all_gather x3 -> x0, waiting for transfers between devices: 573 us -> none  [the longest x1 573 us: per_device(): lax.all_gather(swapped, 'ctx', axis=1, tiled=True)]
    dot_general x5 -> x0, matrix products: 95 us -> none  [the longest x1 30.6 us: per_device(): jnp.einsum('kts,kti->si', kernel_mat, proj_grad, precision=exact_prec)]
    unnamed x1 -> x0, blocking collectives: 65.8 us -> none
    pallas_call x0 -> x21, Pallas kernels: none -> 65 us  [the longest x13 57.1 us: add_blocks(): pl.pallas_call(functools.partial(blocks_kernel, blocks, sets, fresh), in_...]
    all_to_all x1 -> x0, waiting for transfers between devices: 56.1 us -> none  [per_device(): lax.all_to_all(filter_mats, 'grp', split_axis=1, concat_axis=0, tiled=True)]
    ppermute x0 -> x29, waiting for transfers between devices: none -> 38.8 us  [the longest x17 30.4 us: over_grp(): return lax.ppermute(x, 'grp', pairs)]
    ppermute x0 -> x29, starting transfers between devices: none -> 32.2 us  [the longest x4 14.9 us: per_device(): received.append(lax.ppermute(result, ('ctx', 'grp'), pairs))]
    all_to_all x1 -> x0, blocking collectives: 10.3 us -> none  [per_device(): lax.all_to_all(strided, 'grp', split_axis=1, concat_axis=1, tiled=True)]
  transfers between devices with their start and end apart: 4 -> 29, of which waited for: 2 -> 8; matrix products, arithmetic and copies ran while one was open for 6% -> 2% of each run, Pallas kernels for 0% -> 33%
where the time goes in v1:
time: 151 us; the launch traced here: 149 us
  Pallas kernels  65 us (43%)
  waiting for transfers between devices  38.8 us (26%)
  starting transfers between devices  32.2 us (21%)
  local copies, waits for them, and re-layouts  11 us (7%)
    pallas_call x13, Pallas kernels, add_blocks(): pl.pallas_call(functools.partial(blocks_kernel, blocks, sets, fresh), in_...  57.1 us
    ppermute x17, waiting for transfers between devices, over_grp(): return lax.ppermute(x, 'grp', pairs)  30.4 us
    ppermute x4, starting transfers between devices, per_device(): received.append(lax.ppermute(result, ('ctx', 'grp'), pairs))  14.9 us
    unnamed x19, local copies, waits for them, and re-layouts  9.8 us
    ppermute x17, starting transfers between devices, over_grp(): return lax.ppermute(x, 'grp', pairs)  8.68 us
    ppermute x4, waiting for transfers between devices, per_device(): received.append(lax.ppermute(result, ('ctx', 'grp'), pairs))  8.15 us
    ppermute x3, starting transfers between devices, per_device(): going_right = lax.ppermute(going_right, 'ctx', right)  4.98 us
  transfers between devices with their start and end apart: 29, of which 8 were waited for; matrix products, arithmetic and copies ran while one was open for 2% of the time, Pallas kernels for 33%

profile of v1, /device:TPU:4, one launch (start us, length us, event | category | flops | bytes accessed | tf_op | source)
XLA Modules:
  0.0 148.8 jit_solution(2396284787380914114)
XLA Ops:
  16.2 6.3 %collective-permute-done.12.refs_4_ = bf16[2,128,1024]{2,1,0:T(8,128)(2,1)} collective-permute-done((bf16[2,128,1024]{2,1,0:T(8,128)(2,1)}, bf16[2,128,1024]{2,1,0:T(8,128)(2,1)}, u32[]{:S(2)}, u32[]{:S(2)}) %collective-permute-start.12) | collective-permute-done | bytes 524320 | tf_op jit(solution)/shard_map/ppermute | solution.py:351
  22.5 10.5 %collective-permute-done.13.refs_5_ = bf16[2,128,1024]{2,1,0:T(8,128)(2,1)} collective-permute-done((bf16[2,128,1024]{2,1,0:T(8,128)(2,1)}, bf16[2,128,1024]{2,1,0:T(8,128)(2,1)}, u32[]{:S(2)}, u32[]{:S(2)}) %collective-permute-start.13) | collective-permute-done | bytes 524320 | tf_op jit(solution)/shard_map/ppermute | solution.py:351
  38.1 2.6 %copy-done.6 = bf16[8,336,1024]{2,1,0:T(8,128)(2,1)S(1)} copy-done((bf16[8,336,1024]{2,1,0:T(8,128)(2,1)S(1)}, bf16[8,336,1024]{2,1,0:T(8,128)(2,1)}, u32[]{:S(2)}) %copy-start.6) | copy-done | bytes 5505048
  40.6 6.4 %add_blocks.17 = (f32[336,256]{1,0:T(8,128)S(1)}, f32[336,256]{1,0:T(8,128)S(1)}) custom-call(s32[3]{0:T(128)S(1)} %get-tuple-element.79.info, bf16[512,512]{1,0:T(8,128)(2,1)} %collective-permute-done.refs_0_, bf16[512,512]{1,0:T(8,128)(2,1)} %collective-permute-done.4.refs_1_, bf16[512,512]{1,0:T(8,128)(2,1)S(1)} %copy-done.3, ...), custom_call_target="tpu_custom_call" | custom-call | flops 5520000000 | tf_op jit(solution)/shard_map/add_blocks/pallas_call | solution.py:143
  50.0 5.2 %add_blocks.13.refs_7_ = f32[336,256]{1,0:T(8,128)S(1)} custom-call(s32[3]{0:T(128)S(1)} %get-tuple-element.79.info, bf16[512,512]{1,0:T(8,128)(2,1)} %refs_0_.5, bf16[512,512]{1,0:T(8,128)(2,1)} %collective-permute-done.8.refs_1_.refs_2_, bf16[4,128,1024]{2,1,0:T(8,128)(2,1)S(1)} %collective-permute-done.14.refs_2_.refs_4_, ...), custom_call_target="tpu_custom_call" | custom-call | flops 2760000000 | tf_op jit(solution)/shard_map/add_blocks/pallas_call | solution.py:143
  55.2 4.1 %add_blocks.18 = (f32[336,256]{1,0:T(8,128)S(1)}, f32[336,256]{1,0:T(8,128)S(1)}) custom-call(s32[3]{0:T(128)S(1)} %get-tuple-element.80.info, bf16[512,512]{1,0:T(8,128)(2,1)} %collective-permute-done.refs_0_, bf16[512,512]{1,0:T(8,128)(2,1)} %collective-permute-done.4.refs_1_, ...), custom_call_target="tpu_custom_call", output_to_operand_aliasing={{0}: (8, {}), {1}: (9, {})} | custom-call | flops 2760000000 | tf_op jit(solution)/shard_map/add_blocks/pallas_call | solution.py:143
  59.3 3.9 %add_blocks.19 = (f32[336,256]{1,0:T(8,128)S(1)}, f32[336,256]{1,0:T(8,128)S(1)}) custom-call(s32[3]{0:T(128)S(1)} %get-tuple-element.81.info, bf16[512,512]{1,0:T(8,128)(2,1)} %collective-permute-done.refs_0_, bf16[512,512]{1,0:T(8,128)(2,1)} %collective-permute-done.4.refs_1_, ...), custom_call_target="tpu_custom_call", output_to_operand_aliasing={{0}: (8, {}), {1}: (9, {})} | custom-call | flops 2760000000 | tf_op jit(solution)/shard_map/add_blocks/pallas_call | solution.py:143
  66.2 5.4 %add_blocks.20 = (f32[336,256]{1,0:T(8,128)S(1)}, f32[336,256]{1,0:T(8,128)S(1)}) custom-call(s32[3]{0:T(128)S(1)} %get-tuple-element.79.info, bf16[512,512]{1,0:T(8,128)(2,1)S(1)} %collective-permute-done.1.refs_0_, bf16[512,512]{1,0:T(8,128)(2,1)S(1)} %collective-permute-done.5.refs_1_, bf16[512,512]{1,0:T(8,128)(2,1)S(1)} %collective-permute-done.17.refs_2_, ...), custom_call_target="tpu_custom_call" | custom-call | flops 5520000000 | tf_op jit(solution)/shard_map/add_blocks/pallas_call | solution.py:143
  71.6 3.6 %add_blocks.21 = (f32[336,256]{1,0:T(8,128)S(1)}, f32[336,256]{1,0:T(8,128)S(1)}) custom-call(s32[3]{0:T(128)S(1)} %get-tuple-element.80.info, bf16[512,512]{1,0:T(8,128)(2,1)S(1)} %collective-permute-done.1.refs_0_, bf16[512,512]{1,0:T(8,128)(2,1)S(1)} %collective-permute-done.5.refs_1_, ...), custom_call_target="tpu_custom_call", output_to_operand_aliasing={{0}: (8, {}), {1}: (9, {})} | custom-call | flops 2760000000 | tf_op jit(solution)/shard_map/add_blocks/pallas_call | solution.py:143
  75.2 3.5 %add_blocks.22 = (f32[336,256]{1,0:T(8,128)S(1)}, f32[336,256]{1,0:T(8,128)S(1)}) custom-call(s32[3]{0:T(128)S(1)} %get-tuple-element.81.info, bf16[512,512]{1,0:T(8,128)(2,1)S(1)} %collective-permute-done.1.refs_0_, bf16[512,512]{1,0:T(8,128)(2,1)S(1)} %collective-permute-done.5.refs_1_, ...), custom_call_target="tpu_custom_call", output_to_operand_aliasing={{0}: (8, {}), {1}: (9, {})} | custom-call | flops 2760000000 | tf_op jit(solution)/shard_map/add_blocks/pallas_call | solution.py:143
  78.9 5.4 %add_blocks.23 = (f32[336,256]{1,0:T(8,128)S(1)}, f32[336,256]{1,0:T(8,128)S(1)}) custom-call(s32[3]{0:T(128)S(1)} %get-tuple-element.79.info, bf16[512,512]{1,0:T(8,128)(2,1)S(1)} %collective-permute-done.2.refs_0_, bf16[512,512]{1,0:T(8,128)(2,1)S(1)} %collective-permute-done.6.refs_1_, bf16[512,512]{1,0:T(8,128)(2,1)S(1)} %collective-permute-done.19.refs_2_, ...), custom_call_target="tpu_custom_call" | custom-call | flops 5520000000 | tf_op jit(solution)/shard_map/add_blocks/pallas_call | solution.py:143
  84.3 3.6 %add_blocks.24 = (f32[336,256]{1,0:T(8,128)S(1)}, f32[336,256]{1,0:T(8,128)S(1)}) custom-call(s32[3]{0:T(128)S(1)} %get-tuple-element.80.info, bf16[512,512]{1,0:T(8,128)(2,1)S(1)} %collective-permute-done.2.refs_0_, bf16[512,512]{1,0:T(8,128)(2,1)S(1)} %collective-permute-done.6.refs_1_, ...), custom_call_target="tpu_custom_call", output_to_operand_aliasing={{0}: (8, {}), {1}: (9, {})} | custom-call | flops 2760000000 | tf_op jit(solution)/shard_map/add_blocks/pallas_call | solution.py:143
  87.9 3.5 %add_blocks.25 = (f32[336,256]{1,0:T(8,128)S(1)}, f32[336,256]{1,0:T(8,128)S(1)}) custom-call(s32[3]{0:T(128)S(1)} %get-tuple-element.81.info, bf16[512,512]{1,0:T(8,128)(2,1)S(1)} %collective-permute-done.2.refs_0_, bf16[512,512]{1,0:T(8,128)(2,1)S(1)} %collective-permute-done.6.refs_1_, ...), custom_call_target="tpu_custom_call", output_to_operand_aliasing={{0}: (8, {}), {1}: (9, {})} | custom-call | flops 2760000000 | tf_op jit(solution)/shard_map/add_blocks/pallas_call | solution.py:143
  91.4 4.7 %add_blocks.14.refs_8_ = f32[336,256]{1,0:T(8,128)S(1)} custom-call(s32[3]{0:T(128)S(1)} %get-tuple-element.79.info, bf16[512,512]{1,0:T(8,128)(2,1)S(1)} %constant_dynamic-update-slice_fusion.refs_0_.refs_1_, bf16[512,512]{1,0:T(8,128)(2,1)S(1)} %collective-permute-done.9.refs_1_.refs_3_, bf16[4,128,1024]{2,1,0:T(8,128)(2,1)S(1)} %collective-permute-done.14.refs_2_.refs_4_, ...), custom_call_target="tpu_custom_call" | custom-call | flops 2760000000 | tf_op jit(solution)/shard_map/add_blocks/pallas_call | solution.py:143
  96.2 4.0 %add_blocks.15 = (f32[336,256]{1,0:T(8,128)S(1)}, f32[336,256]{1,0:T(8,128)S(1)}) custom-call(s32[3]{0:T(128)S(1)} %get-tuple-element.80.info, bf16[512,512]{1,0:T(8,128)(2,1)} %refs_0_.5, bf16[512,512]{1,0:T(8,128)(2,1)S(1)} %constant_dynamic-update-slice_fusion.refs_0_.refs_1_, ...), custom_call_target="tpu_custom_call", output_to_operand_aliasing={{0}: (8, {}), {1}: (9, {})} | custom-call | flops 2760000000 | tf_op jit(solution)/shard_map/add_blocks/pallas_call | solution.py:143
  100.1 3.8 %add_blocks.16 = (f32[336,256]{1,0:T(8,128)S(1)}, f32[336,256]{1,0:T(8,128)S(1)}) custom-call(s32[3]{0:T(128)S(1)} %get-tuple-element.81.info, bf16[512,512]{1,0:T(8,128)(2,1)} %refs_0_.5, bf16[512,512]{1,0:T(8,128)(2,1)S(1)} %constant_dynamic-update-slice_fusion.refs_0_.refs_1_, ...), custom_call_target="tpu_custom_call", output_to_operand_aliasing={{0}: (8, {}), {1}: (9, {})} | custom-call | flops 2760000000 | tf_op jit(solution)/shard_map/add_blocks/pallas_call | solution.py:143
  103.9 2.4 %finish_blocks.1 = (f32[512,128]{1,0:T(8,128)S(1)}, f32[512,128]{1,0:T(8,128)S(1)}, f32[512,128]{1,0:T(8,128)S(1)}, f32[512,128]{1,0:T(8,128)S(1)}, f32[512,128]...) custom-call(s32[16]{0:T(128)S(1)} %slice_bitcast_fusion.4.info, ...), custom_call_target="tpu_custom_call" | custom-call | flops 3000000000 | tf_op jit(solution)/shard_map/finish_blocks/pallas_call | solution.py:187
  110.5 5.0 %collective-permute-done.27.refs_1_ = f32[512,128]{1,0:T(8,128)S(1)} collective-permute-done((f32[512,128]{1,0:T(8,128)S(1)}, f32[512,128]{1,0:T(8,128)S(1)}, u32[]{:S(2)}, u32[]{:S(2)}) %collective-permute-start.27) | collective-permute-done | bytes 262176 | tf_op jit(solution)/shard_map/ppermute | solution.py:351
  115.6 5.5 %collective-permute-start.28 = (bf16[512,128]{1,0:T(8,128)(2,1)S(1)}, bf16[512,128]{1,0:T(8,128)(2,1)S(1)}, u32[]{:S(2)}, u32[]{:S(2)}) collective-permute-start(bf16[512,128]{1,0:T(8,128)(2,1)S(1)} %combine_ways.7), channel_id=1, source_target_pairs={{0,24},{1,0},{2,28},{3,4},{4,12},{5,20},{6,8},{7,16},{8,25},{9,1},... | collective-permute-start | bytes 393224 | tf_op jit(solution)/shard_map/ppermute | solution.py:403
  121.1 2.9 %collective-permute-done.25.refs_1_ = f32[512,128]{1,0:T(8,128)S(1)} collective-permute-done((f32[512,128]{1,0:T(8,128)S(1)}, f32[512,128]{1,0:T(8,128)S(1)}, u32[]{:S(2)}, u32[]{:S(2)}) %collective-permute-start.25) | collective-permute-done | bytes 262176 | tf_op jit(solution)/shard_map/ppermute | solution.py:351
  124.0 3.6 %collective-permute-start.26 = (bf16[512,128]{1,0:T(8,128)(2,1)S(1)}, bf16[512,128]{1,0:T(8,128)(2,1)S(1)}, u32[]{:S(2)}, u32[]{:S(2)}) collective-permute-start(bf16[512,128]{1,0:T(8,128)(2,1)S(1)} %combine_ways.6), channel_id=1, source_target_pairs={{0,16},{1,24},{2,20},{3,28},{4,4},{5,12},{6,0},{7,8},{8,17},{9,25}... | collective-permute-start | bytes 393224 | tf_op jit(solution)/shard_map/ppermute | solution.py:403
  131.1 3.7 %collective-permute-done.21.refs_1_ = f32[512,128]{1,0:T(8,128)S(1)} collective-permute-done((f32[512,128]{1,0:T(8,128)S(1)}, f32[512,128]{1,0:T(8,128)S(1)}, u32[]{:S(2)}, u32[]{:S(2)}) %collective-permute-start.21) | collective-permute-done | bytes 262176 | tf_op jit(solution)/shard_map/ppermute | solution.py:351
  134.8 4.3 %collective-permute-start.22 = (bf16[512,128]{1,0:T(8,128)(2,1)S(1)}, bf16[512,128]{1,0:T(8,128)(2,1)S(1)}, u32[]{:S(2)}, u32[]{:S(2)}) collective-permute-start(bf16[512,128]{1,0:T(8,128)(2,1)S(1)} %combine_ways.4), channel_id=1, source_target_pairs={{0,0},{1,8},{2,4},{3,12},{4,20},{5,28},{6,16},{7,24},{8,1},{9,9},{... | collective-permute-start | bytes 393224 | tf_op jit(solution)/shard_map/ppermute | solution.py:403
  139.2 8.1 %collective-permute-done.22.refs_0_ = bf16[512,128]{1,0:T(8,128)(2,1)S(1)} collective-permute-done((bf16[512,128]{1,0:T(8,128)(2,1)S(1)}, bf16[512,128]{1,0:T(8,128)(2,1)S(1)}, u32[]{:S(2)}, u32[]{:S(2)}) %collective-permute-start.22) | collective-permute-done | bytes 131104 | tf_op jit(solution)/shard_map/ppermute | solution.py:403
  (88 shorter events, 36.5 us)
Async XLA Ops:
  0.0 15.4 %collective-permute-start = (bf16[512,512]{1,0:T(8,128)(2,1)}, bf16[512,512]{1,0:T(8,128)(2,1)}, u32[]{:S(2)}, u32[]{:S(2)}) collective-permute-start(bf16[512,512]{1,0:T(8,128)(2,1)} %refs_0_.5), channel_id=1, source_target_pairs={{0,8},{8,16},{16,24},{24,28},{28,20},{20,12},{12,4},{4,0},{1,9},{9... | collective-permute-start | bytes 1572872 | tf_op jit(solution)/shard_map/ppermute | solution.py:358
  1.6 14.2 %collective-permute-start.4 = (bf16[512,512]{1,0:T(8,128)(2,1)}, bf16[512,512]{1,0:T(8,128)(2,1)}, u32[]{:S(2)}, u32[]{:S(2)}) collective-permute-start(bf16[512,512]{1,0:T(8,128)(2,1)} %refs_0_.5), channel_id=1, source_target_pairs={{8,0},{16,8},{24,16},{28,24},{20,28},{12,20},{4,12},{0,4},{9,1},{1... | collective-permute-start | bytes 1572872 | tf_op jit(solution)/shard_map/ppermute | solution.py:359
  7.4 25.9 %collective-permute-start.14 = (bf16[4,128,1024]{2,1,0:T(8,128)(2,1)S(1)}, bf16[4,128,1024]{2,1,0:T(8,128)(2,1)S(1)}, u32[]{:S(2)}, u32[]{:S(2)}) collective-permute-start(bf16[4,128,1024]{2,1,0:T(8,128)(2,1)S(1)} %get-tuple-element.45), channel_id=1, source_target_pairs={{0,1},{1,0},{2,3},{3,2},{4,5},{5,4},{6,7},{7,6},{8,9},{9,8},{10,11... | collective-permute-start | bytes 3145736 | tf_op jit(solution)/shard_map/ppermute | solution.py:351
  7.4 15.0 %collective-permute-start.12 = (bf16[2,128,1024]{2,1,0:T(8,128)(2,1)}, bf16[2,128,1024]{2,1,0:T(8,128)(2,1)}, u32[]{:S(2)}, u32[]{:S(2)}) collective-permute-start(bf16[2,128,1024]{2,1,0:T(8,128)(2,1)} %get-tuple-element.43), channel_id=1, source_target_pairs={{0,2},{1,3},{2,0},{3,1},{4,6},{5,7},{6,4},{7,5},{8,10},{9,11},{10,... | collective-permute-start | bytes 1572872 | tf_op jit(solution)/shard_map/ppermute | solution.py:351
  7.5 25.4 %collective-permute-start.13 = (bf16[2,128,1024]{2,1,0:T(8,128)(2,1)}, bf16[2,128,1024]{2,1,0:T(8,128)(2,1)}, u32[]{:S(2)}, u32[]{:S(2)}) collective-permute-start(bf16[2,128,1024]{2,1,0:T(8,128)(2,1)} %get-tuple-element.44), channel_id=1, source_target_pairs={{0,3},{1,2},{2,1},{3,0},{4,7},{5,6},{6,5},{7,4},{8,11},{9,10},{10,... | collective-permute-start | bytes 1572872 | tf_op jit(solution)/shard_map/ppermute | solution.py:351
  15.4 19.6 %collective-permute-start.15 = (bf16[512,512]{1,0:T(8,128)(2,1)}, bf16[512,512]{1,0:T(8,128)(2,1)S(1)}, u32[]{:S(2)}, u32[]{:S(2)}) collective-permute-start(bf16[512,512]{1,0:T(8,128)(2,1)} %collective-permute-done.refs_0_), channel_id=1, source_target_pairs={{0,1},{1,0},{2,3},{3,2},{4,5},{5,4},{6,7},{7,6},{8,9},{9,8},{10,11... | collective-permute-start | bytes 1572872 | tf_op jit(solution)/shard_map/ppermute | solution.py:351
  15.8 20.6 %collective-permute-start.16 = (bf16[512,512]{1,0:T(8,128)(2,1)}, bf16[512,512]{1,0:T(8,128)(2,1)}, u32[]{:S(2)}, u32[]{:S(2)}) collective-permute-start(bf16[512,512]{1,0:T(8,128)(2,1)} %collective-permute-done.4.refs_1_), channel_id=1, source_target_pairs={{0,1},{1,0},{2,3},{3,2},{4,5},{5,4},{6,7},{7,6},{8,9},{9,8},{10,11... | collective-permute-start | bytes 1572872 | tf_op jit(solution)/shard_map/ppermute | solution.py:351
  22.5 27.5 %collective-permute-start.8 = (bf16[512,512]{1,0:T(8,128)(2,1)}, bf16[512,512]{1,0:T(8,128)(2,1)}, u32[]{:S(2)}, u32[]{:S(2)}) collective-permute-start(bf16[512,512]{1,0:T(8,128)(2,1)} %refs_0_.5), channel_id=1, source_target_pairs={{0,1},{1,0},{2,3},{3,2},{4,5},{5,4},{6,7},{7,6},{8,9},{9,8},{10,11... | collective-permute-start | bytes 1572872 | tf_op jit(solution)/shard_map/ppermute | solution.py:351
  32.9 16.1 %collective-permute-start.10 = (bf16[2,128,1024]{2,1,0:T(8,128)(2,1)}, bf16[2,128,1024]{2,1,0:T(8,128)(2,1)}, u32[]{:S(2)}, u32[]{:S(2)}) collective-permute-start(bf16[2,128,1024]{2,1,0:T(8,128)(2,1)} %get-tuple-element.41), channel_id=1, source_target_pairs={{0,2},{1,3},{2,0},{3,1},{4,6},{5,7},{6,4},{7,5},{8,10},{9,11},{10,... | collective-permute-start | bytes 1572872 | tf_op jit(solution)/shard_map/ppermute | solution.py:351
  33.4 13.9 %collective-permute-start.1 = (bf16[512,512]{1,0:T(8,128)(2,1)}, bf16[512,512]{1,0:T(8,128)(2,1)S(1)}, u32[]{:S(2)}, u32[]{:S(2)}) collective-permute-start(bf16[512,512]{1,0:T(8,128)(2,1)} %collective-permute-done.refs_0_), channel_id=1, source_target_pairs={{0,8},{8,16},{16,24},{24,28},{28,20},{20,12},{12,4},{4,0},{1,9},{9... | collective-permute-start | bytes 1572872 | tf_op jit(solution)/shard_map/ppermute | solution.py:358
  35.8 13.7 %collective-permute-start.5 = (bf16[512,512]{1,0:T(8,128)(2,1)}, bf16[512,512]{1,0:T(8,128)(2,1)S(1)}, u32[]{:S(2)}, u32[]{:S(2)}) collective-permute-start(bf16[512,512]{1,0:T(8,128)(2,1)} %collective-permute-done.4.refs_1_), channel_id=1, source_target_pairs={{8,0},{16,8},{24,16},{28,24},{20,28},{12,20},{4,12},{0,4},{9,1},{1... | collective-permute-start | bytes 1572872 | tf_op jit(solution)/shard_map/ppermute | solution.py:359
  36.4 22.9 %collective-permute-start.11 = (bf16[2,128,1024]{2,1,0:T(8,128)(2,1)}, bf16[2,128,1024]{2,1,0:T(8,128)(2,1)S(1)}, u32[]{:S(2)}, u32[]{:S(2)}) collective-permute-start(bf16[2,128,1024]{2,1,0:T(8,128)(2,1)} %copy-done.1), channel_id=1, source_target_pairs={{0,3},{1,2},{2,1},{3,0},{4,7},{5,6},{6,5},{7,4},{8,11},{9,10},{10,... | collective-permute-start | bytes 1572872 | tf_op jit(solution)/shard_map/ppermute | solution.py:351
  47.2 16.0 %collective-permute-start.2 = (bf16[512,512]{1,0:T(8,128)(2,1)S(1)}, bf16[512,512]{1,0:T(8,128)(2,1)S(1)}, u32[]{:S(2)}, u32[]{:S(2)}) collective-permute-start(bf16[512,512]{1,0:T(8,128)(2,1)S(1)} %collective-permute-done.1.refs_0_), channel_id=1, source_target_pairs={{0,8},{8,16},{16,24},{24,28},{28,20},{20,12},{12,4},{4,0},{1,9},{9... | collective-permute-start | bytes 1572872 | tf_op jit(solution)/shard_map/ppermute | solution.py:358
  49.0 16.7 %collective-permute-start.17 = (bf16[512,512]{1,0:T(8,128)(2,1)S(1)}, bf16[512,512]{1,0:T(8,128)(2,1)S(1)}, u32[]{:S(2)}, u32[]{:S(2)}) collective-permute-start(bf16[512,512]{1,0:T(8,128)(2,1)S(1)} %collective-permute-done.1.refs_0_), channel_id=1, source_target_pairs={{0,1},{1,0},{2,3},{3,2},{4,5},{5,4},{6,7},{7,6},{8,9},{9,8},{10,11... | collective-permute-start | bytes 1572872 | tf_op jit(solution)/shard_map/ppermute | solution.py:351
  49.5 15.4 %collective-permute-start.6 = (bf16[512,512]{1,0:T(8,128)(2,1)S(1)}, bf16[512,512]{1,0:T(8,128)(2,1)S(1)}, u32[]{:S(2)}, u32[]{:S(2)}) collective-permute-start(bf16[512,512]{1,0:T(8,128)(2,1)S(1)} %collective-permute-done.5.refs_1_), channel_id=1, source_target_pairs={{8,0},{16,8},{24,16},{28,24},{20,28},{12,20},{4,12},{0,4},{9,1},{1... | collective-permute-start | bytes 1572872 | tf_op jit(solution)/shard_map/ppermute | solution.py:359
  50.0 16.2 %collective-permute-start.18 = (bf16[512,512]{1,0:T(8,128)(2,1)S(1)}, bf16[512,512]{1,0:T(8,128)(2,1)S(1)}, u32[]{:S(2)}, u32[]{:S(2)}) collective-permute-start(bf16[512,512]{1,0:T(8,128)(2,1)S(1)} %collective-permute-done.5.refs_1_), channel_id=1, source_target_pairs={{0,1},{1,0},{2,3},{3,2},{4,5},{5,4},{6,7},{7,6},{8,9},{9,8},{10,11... | collective-permute-start | bytes 1572872 | tf_op jit(solution)/shard_map/ppermute | solution.py:351
  63.3 15.4 %collective-permute-start.3 = (bf16[256,512]{1,0:T(8,128)(2,1)S(1)}, bf16[256,512]{1,0:T(8,128)(2,1)S(1)}, u32[]{:S(2)}, u32[]{:S(2)}) collective-permute-start(bf16[256,512]{1,0:T(8,128)(2,1)S(1)} %slice.56), channel_id=1, source_target_pairs={{0,8},{8,16},{16,24},{24,28},{28,20},{20,12},{12,4},{4,0},{1,9},{9... | collective-permute-start | bytes 786440 | tf_op jit(solution)/shard_map/ppermute | solution.py:363
  65.0 13.8 %collective-permute-start.7 = (bf16[256,512]{1,0:T(8,128)(2,1)S(1)}, bf16[256,512]{1,0:T(8,128)(2,1)S(1)}, u32[]{:S(2)}, u32[]{:S(2)}) collective-permute-start(bf16[256,512]{1,0:T(8,128)(2,1)S(1)} %slice.57), channel_id=1, source_target_pairs={{8,0},{16,8},{24,16},{28,24},{20,28},{12,20},{4,12},{0,4},{9,1},{1... | collective-permute-start | bytes 786440 | tf_op jit(solution)/shard_map/ppermute | solution.py:363
  65.7 13.2 %collective-permute-start.20 = (bf16[512,512]{1,0:T(8,128)(2,1)S(1)}, bf16[512,512]{1,0:T(8,128)(2,1)S(1)}, u32[]{:S(2)}, u32[]{:S(2)}) collective-permute-start(bf16[512,512]{1,0:T(8,128)(2,1)S(1)} %collective-permute-done.6.refs_1_), channel_id=1, source_target_pairs={{0,1},{1,0},{2,3},{3,2},{4,5},{5,4},{6,7},{7,6},{8,9},{9,8},{10,11... | collective-permute-start | bytes 1572872 | tf_op jit(solution)/shard_map/ppermute | solution.py:351
  107.9 16.0 %collective-permute-start.25 = (f32[512,128]{1,0:T(8,128)S(1)}, f32[512,128]{1,0:T(8,128)S(1)}, u32[]{:S(2)}, u32[]{:S(2)}) collective-permute-start(f32[512,128]{1,0:T(8,128)S(1)} %get-tuple-element.74), channel_id=1, source_target_pairs={{0,2},{1,3},{2,0},{3,1},{4,6},{5,7},{6,4},{7,5},{8,10},{9,11},{10,... | collective-permute-start | bytes 786440 | tf_op jit(solution)/shard_map/ppermute | solution.py:351
  108.5 21.1 %collective-permute-start.23 = (f32[512,128]{1,0:T(8,128)S(1)}, f32[512,128]{1,0:T(8,128)S(1)}, u32[]{:S(2)}, u32[]{:S(2)}) collective-permute-start(f32[512,128]{1,0:T(8,128)S(1)} %get-tuple-element.72), channel_id=1, source_target_pairs={{0,2},{1,3},{2,0},{3,1},{4,6},{5,7},{6,4},{7,5},{8,10},{9,11},{10,... | collective-permute-start | bytes 786440 | tf_op jit(solution)/shard_map/ppermute | solution.py:351
  110.0 24.8 %collective-permute-start.21 = (f32[512,128]{1,0:T(8,128)S(1)}, f32[512,128]{1,0:T(8,128)S(1)}, u32[]{:S(2)}, u32[]{:S(2)}) collective-permute-start(f32[512,128]{1,0:T(8,128)S(1)} %get-tuple-element.70), channel_id=1, source_target_pairs={{0,2},{1,3},{2,0},{3,1},{4,6},{5,7},{6,4},{7,5},{8,10},{9,11},{10,... | collective-permute-start | bytes 786440 | tf_op jit(solution)/shard_map/ppermute | solution.py:351
  115.6 23.7 %collective-permute-start.28 = (bf16[512,128]{1,0:T(8,128)(2,1)S(1)}, bf16[512,128]{1,0:T(8,128)(2,1)S(1)}, u32[]{:S(2)}, u32[]{:S(2)}) collective-permute-start(bf16[512,128]{1,0:T(8,128)(2,1)S(1)} %combine_ways.7), channel_id=1, source_target_pairs={{0,24},{1,0},{2,28},{3,4},{4,12},{5,20},{6,8},{7,16},{8,25},{9,1},... | collective-permute-start | bytes 393224 | tf_op jit(solution)/shard_map/ppermute | solution.py:403
  124.0 15.3 %collective-permute-start.26 = (bf16[512,128]{1,0:T(8,128)(2,1)S(1)}, bf16[512,128]{1,0:T(8,128)(2,1)S(1)}, u32[]{:S(2)}, u32[]{:S(2)}) collective-permute-start(bf16[512,128]{1,0:T(8,128)(2,1)S(1)} %combine_ways.6), channel_id=1, source_target_pairs={{0,16},{1,24},{2,20},{3,28},{4,4},{5,12},{6,0},{7,8},{8,17},{9,25}... | collective-permute-start | bytes 393224 | tf_op jit(solution)/shard_map/ppermute | solution.py:403
  (14 other events, 89.9 us)

commit v2 on v1

--- a/solution.py
+++ b/solution.py
@@ -26,8 +26,7 @@
 
 
 def tables_kernel(poles_ref, out):
-    poles, height, width = poles_ref.shape[0], out.shape[1], out.shape[2] // 4
-    step = width // 2
+    poles, width = poles_ref.shape[0], out.shape[2] // 4
     rate, gain = poles_ref[:, 0:1], poles_ref[:, 1:2]
     lag = lax.broadcasted_iota(jnp.int32, (poles, width), 1).astype(f32)
     decay = jnp.exp(-rate * lag)
@@ -40,16 +39,13 @@
             chosen = jnp.where(columns == 2 + 2 * pair + j, poles_ref[...], 0.0)
             coef = jnp.sum(chosen, axis=1, keepdims=True)
             phi = jnp.sum(coef * gained, axis=0, keepdims=True)
-            line = jnp.concatenate([phi, jnp.zeros((1, step), f32)], axis=1)
-            rolled = pltpu.roll(jnp.broadcast_to(line, (step, width + step)), 0, 1, stride=1, stride_axis=0)
-            high, low = split2(rolled[:, :width])
-            wh, wl = split2(coef * decay)
-            for at, near, weight in ((j, high, wh), (2 + j, low, wl)):
-                lo = at * width
-                out[pair, :step, lo : lo + width] = near
-                out[pair, step:width, lo : lo + step] = jnp.zeros((step, step), bf16)
-                out[pair, step:width, lo + step : lo + width] = near[:, :step]
-                out[pair, width:, lo : lo + width] = weight
+            line = jnp.concatenate([phi, jnp.zeros((1, width), f32)], axis=1)
+            rolled = pltpu.roll(jnp.broadcast_to(line, (width, 2 * width)), 0, 1, stride=1, stride_axis=0)
+            near, weight = split2(rolled[:, :width]), split2(coef * decay)
+            for at in range(2):
+                lanes = slice((2 * at + j) * width, (2 * at + j + 1) * width)
+                out[pair, :width, lanes] = near[at]
+                out[pair, width:, lanes] = weight[at]
 
 
 def tables(coeffs, rates, gains, width):
@@ -87,10 +83,10 @@
     return pl.pallas_call(
         functools.partial(cut_kernel, plan),
         in_specs=[SM, ANY],
-        out_specs=[ANY] * len(plan),
+        out_specs=[VM] * len(plan),
         out_shape=[jax.ShapeDtypeStruct((n, half, cols), bf16) for _, n in plan],
         scratch_shapes=[pltpu.SemaphoreType.DMA((len(plan),))],
-        compiler_params=params(),
+        compiler_params=params(60),
         name="cut_filters",
     )(info, mats)
 
@@ -105,55 +101,57 @@
     here = info[0]
     width = table.shape[2] // 4
     half = mats[0].shape[1]
-    for b in range(blocks):
-        after[b][...] = jnp.zeros_like(after[b]) if fresh else before[b][...]
-
-    @pl.loop(0, mats[0].shape[0] // 2)
-    def _(i):
-        for n in range(sets):
-            two = mats[n].at[pl.ds(2 * i, 2)]
-            m_mine = two[:, :, pl.ds(pl.multiple_of(here * wide, wide), wide)].reshape(2 * half, wide)
-            m_other = two[:, :, pl.ds(pl.multiple_of((1 - here) * wide, wide), wide)].reshape(2 * half, wide)
-            for b in range(blocks):
-                proj = lax.dot_general(mine[b][...], m_mine, NT, preferred_element_type=f32)
-                proj += lax.dot_general(other[b][...], m_other, NT, preferred_element_type=f32)
-                for at, part in enumerate(split2(proj)):
-                    for j in range(2):
-                        rows = pl.ds((2 * at + j) * width, width)
-                        for s in range(2):
-                            held[n, b, rows, s * half : (s + 1) * half] = part[
-                                s * width : (s + 1) * width, j * half : (j + 1) * half
-                            ]
-        for n in range(sets):
-            pair = info[1 + n] + i
-            for b in range(blocks):
-                high, low = held[n, b, : 2 * width, :], held[n, b, 2 * width :, :]
-                add = jnp.dot(table[pair, :, : 2 * width], high, preferred_element_type=f32)
-                add += jnp.dot(table[pair, :, 2 * width :], high, preferred_element_type=f32)
-                add += jnp.dot(table[pair, :, : 2 * width], low, preferred_element_type=f32)
-                after[b][...] += add
+    subs = mine[0].shape[0] // width
+    pairs = mats[0].shape[0] // 2
+    units = [(i, n, b) for i in range(pairs) for n in range(sets) for b in range(blocks)]
+    for u, (i, n, b) in enumerate(units):
+        two = mats[n].at[pl.ds(2 * i, 2)]
+        m_mine = two[:, :, pl.ds(pl.multiple_of(here * wide, wide), wide)].reshape(2 * half, wide)
+        m_other = two[:, :, pl.ds(pl.multiple_of((1 - here) * wide, wide), wide)].reshape(2 * half, wide)
+        proj = lax.dot_general(mine[b][...], m_mine, NT, preferred_element_type=f32)
+        proj += lax.dot_general(other[b][...], m_other, NT, preferred_element_type=f32)
+        for at, part in enumerate(split2(proj)):
+            for j in range(2):
+                rows = pl.ds((2 * at + j) * width, width)
+                for s in range(subs):
+                    held[u, rows, s * half : (s + 1) * half] = part[
+                        s * width : (s + 1) * width, j * half : (j + 1) * half
+                    ]
+    for u, (i, n, b) in enumerate(units):
+        pair = info[1 + n] + i
+        high, low = held[u, : 2 * width, :], held[u, 2 * width :, :]
+        add = jnp.dot(table[pair, :, : 2 * width], high, preferred_element_type=f32)
+        add += jnp.dot(table[pair, :, 2 * width :], high, preferred_element_type=f32)
+        add += jnp.dot(table[pair, :, : 2 * width], low, preferred_element_type=f32)
+        if fresh and i == n == 0:
+            after[b][...] = add
+        elif i == n == 0:
+            after[b][...] = before[b][...] + add
+        else:
+            after[b][...] += add
 
 
 def add_blocks(info, mine, other, mats, table, totals):
     blocks, sets, fresh = len(mine), len(mats), totals is None
     half = mats[0].shape[1]
     height, tw = table.shape[1:]
-    total = jax.ShapeDtypeStruct((height, 2 * half), f32)
+    lanes = mine[0].shape[0] // (tw // 4) * half
+    total = jax.ShapeDtypeStruct((height, lanes), f32)
     units = blocks * sets * mats[0].shape[0] // 2
     return pl.pallas_call(
         functools.partial(blocks_kernel, blocks, sets, fresh),
         in_specs=[SM] + [VM] * (2 * blocks + sets + 1 + (0 if fresh else blocks)),
         out_specs=[VM] * blocks,
         out_shape=[total] * blocks,
-        scratch_shapes=[pltpu.VMEM((sets, blocks, tw, 2 * half), bf16)],
+        scratch_shapes=[pltpu.VMEM((units, tw, lanes), bf16)],
         input_output_aliases={} if fresh else {1 + 2 * blocks + sets + 1 + b: b for b in range(blocks)},
         compiler_params=params(),
-        cost_estimate=pl.CostEstimate(flops=int(units * 0.69e9), bytes_accessed=0, transcendentals=0),
+        cost_estimate=pl.CostEstimate(flops=int(units * 0.6e9), bytes_accessed=0, transcendentals=0),
         name="add_blocks",
     )(info, *mine, *other, *mats, table, *([] if fresh else totals))
 
 
-def finish_kernel(count, ways, info, *refs):
+def finish_kernel(count, info, *refs):
     totals, (edge, decay) = refs[:count], refs[count : count + 2]
     outs = refs[count + 2 : 2 * count + 2]
     held, entering, sems = refs[2 * count + 2 :]
@@ -161,34 +159,37 @@
     for c in copies:
         c.start()
     width, poles = edge.shape
-    half = held.shape[2] // 2
+    subs = outs[0].shape[0] // width
+    half = held.shape[2] // subs
     eh, el = split2(edge[...])
     left = jnp.concatenate([eh, el, eh], axis=1)
     for c in copies:
         c.wait()
     carried = jnp.zeros((poles, half), f32)
     for c in reversed(range(count)):
-        state = held[c, width:, :]
-        inner = state[:, half:] + decay[...] * carried
-        ch, cl = split2(jnp.concatenate([inner, carried], axis=1))
+        state, enters = held[c, width:, :], []
+        for s in reversed(range(subs)):
+            enters.append(carried)
+            carried = state[:, s * half : (s + 1) * half] + decay[...] * carried
+        ch, cl = split2(jnp.concatenate(enters[::-1], axis=1))
         entering[c] = jnp.concatenate([ch, ch, cl], axis=0)
-        carried = state[:, :half] + decay[...] * inner
     for n in range(count):
         c = info[count + n]
         value = held[c, :width, :] + jnp.dot(left, entering[c], preferred_element_type=f32)
-        outs[n][:width, :] = value[:, :half]
-        outs[n][width:, :] = value[:, half:]
-
-
-def finish(info, totals, edge, decay, ways):
+        for s in range(subs):
+            outs[n][s * width : (s + 1) * width, :] = value[:, s * half : (s + 1) * half]
+
+
+def finish(info, totals, edge, decay, length):
     count = len(totals)
     height, tw = totals[0].shape
     width, poles = edge.shape
-    return pl.pallas_call(
-        functools.partial(finish_kernel, count, ways),
+    half = tw * width // length
+    return pl.pallas_call(
+        functools.partial(finish_kernel, count),
         in_specs=[SM] + [ANY] * count + [VM, VM],
         out_specs=[VM] * count,
-        out_shape=[jax.ShapeDtypeStruct((2 * width, tw // 2), f32)] * count,
+        out_shape=[jax.ShapeDtypeStruct((length, half), f32)] * count,
         scratch_shapes=[
             pltpu.VMEM((count, height, tw), f32),
             pltpu.VMEM((count, 3 * poles, tw), bf16),
@@ -262,26 +263,26 @@
             use = lax.dynamic_slice_in_dim(table, 2 * info[1 + n], mats[n].shape[0], 0)
             swapped = jnp.where(info[0] == 0, mats[n], jnp.roll(mats[n], wide, axis=2))
             proj = jnp.einsum("tj,kij->kti", rows, swapped, preferred_element_type=f32)
-            proj = jnp.concatenate([proj[:, :width], proj[:, width:]], axis=2)
+            proj = jnp.concatenate(jnp.split(proj, rows.shape[0] // width, axis=1), axis=2)
             total = total + jnp.einsum("kst,kti->si", use, proj, precision=exact_prec)
         results.append(total)
     return results
 
 
-def plain_finish(info, totals, edge, decay, ways):
-    count = len(totals)
-    width, half = edge.shape[0], totals[0].shape[1] // 2
+def plain_finish(info, totals, edge, decay, length):
+    count, width = len(totals), edge.shape[0]
+    subs = length // width
     held = jnp.zeros((count,) + totals[0].shape, f32)
     for s in range(count):
         held = lax.dynamic_update_slice(held, totals[s][None], (info[s], 0, 0))
-    carried, values = jnp.zeros((edge.shape[1], half), f32), [None] * count
+    carried, values = jnp.zeros((edge.shape[1], totals[0].shape[1] // subs), f32), [None] * count
     for c in reversed(range(count)):
-        state = held[c, width:]
-        inner = state[:, half:] + decay * carried
-        far = jnp.dot(edge, jnp.concatenate([inner, carried], axis=1), precision=exact_prec)
-        value = held[c, :width] + far
-        values[c] = jnp.concatenate([value[:, :half], value[:, half:]], axis=0)
-        carried = state[:, :half] + decay * inner
+        enters = []
+        for state in reversed(jnp.split(held[c, width:], subs, axis=1)):
+            enters.append(carried)
+            carried = state + decay * carried
+        far = jnp.dot(edge, jnp.concatenate(enters[::-1], axis=1), precision=exact_prec)
+        values[c] = jnp.concatenate(jnp.split(held[c, :width] + far, subs, axis=1), axis=0)
     values = jnp.stack(values)
     return [values[info[count + n]] for n in range(count)]
 
@@ -304,8 +305,8 @@
     per = count // ways
     own_filters, features, _ = filter_mats.shape
     length, wide = out_grad.shape
-    half, width = features // 2, length // 2
-    kernels = half % 128 == 0 and wide % 128 == 0 and width % 256 == 0 and pole_rates.shape[0] % 16 == 0
+    half, width = features // 2, length // 4
+    kernels = half % 128 == 0 and wide % 128 == 0 and width % 128 == 0 and pole_rates.shape[0] % 16 == 0
     make, slices, add, end, both, put = (
         (tables, cut, add_blocks, finish, combine, arrange)
         if kernels
@@ -320,22 +321,23 @@
         offsets += [-step, step]
     offsets.append(count // 2)
     far_ways = [(w, h) for w in range(1, ways) for h in range(2)]
-    plan = [(lo, 2) for lo in range(0, own_filters, 2) for _ in far_ways] + [(0, own_filters)] * 2
-    to = far_ways * (own_filters // 2) + [(0, 1), (0, 0)]
+    plan = [(0, own_filters)] * (len(far_ways) + 2)
+    to = far_ways + [(0, 1), (0, 0)]
 
     def numbers(ctx, grp):
         way, here, at = grp // 2, grp % 2, order.index(ctx)
-        cuts, firsts, near_firsts = [], [], []
+        cuts = []
         for w, h in to:
             cuts += [(here ^ h) * half, (way + w) % ways * 2 * wide]
-        pair = lambda w, h, lo: (((way - w) % ways) * 2 + (here ^ h)) * (own_filters // 2) + lo // 2
-        firsts = [[here] + [pair(w, h, lo) for w, h in far_ways] for lo in range(0, own_filters, 2)]
-        near_firsts = [here, pair(0, 1, 0), pair(0, 0, 0)]
+        pair = lambda w, h: (((way - w) % ways) * 2 + (here ^ h)) * (own_filters // 2)
+        firsts = [[here, pair(w, h)] for w, h in far_ways]
+        near_firsts = [here, pair(0, 1), pair(0, 0)]
         turn = ctx % per_grp * 2 + here
         slots = [order[(at + o) % count] for o in offsets]
         use = [ways * ((r + turn) % per) + (way + w + ctx) % ways for w in range(ways) for r in range(per)]
         lanes = [(ctx // ways - r) % per for r in range(per)]
-        return [cuts, near_firsts, *firsts, slots + use, lanes]
+        every = near_firsts + [f[1] for f in firsts]
+        return [cuts, near_firsts, *firsts, every, slots + use, lanes]
 
     rows = [numbers(c, g) for c in range(count) for g in range(groups)]
     ends = np.cumsum([len(part) for part in rows[0]])
@@ -343,7 +345,7 @@
     me = lax.axis_index("ctx") * groups + lax.axis_index("grp")
     row = lax.dynamic_slice(known, (me, 0), (1, known.shape[1]))[0]
     cuts, near_info, *rest = [row[e - len(part) : e] for e, part in zip(ends, rows[0])]
-    far_info, finish_info, lanes_info = rest[:-2], rest[-2], rest[-1]
+    far_info, (every_info, finish_info, lanes_info) = rest[:-3], rest[-3:]
 
     def over_grp(x, by_way, by_core):
         rank = lambda w, h: (w % ways) * 2 + h
@@ -360,13 +362,17 @@
         mine += [going_right, going_left]
         other += [swap(going_right), swap(going_left)]
     last = jnp.concatenate(
-        [lax.ppermute(going_right[:width], "ctx", right), lax.ppermute(going_left[width:], "ctx", left)]
+        [lax.ppermute(going_right[: length // 2], "ctx", right), lax.ppermute(going_left[length // 2 :], "ctx", left)]
     )
     mine.append(last)
     other.append(swap(last))
 
     pieces = slices(filter_mats, cuts, plan, half, 2 * wide)
-    far = [over_grp(p, w, h) for p, (w, h) in zip(pieces, to[:-2])]
+    far = []
+    for p, (w, h) in zip(pieces, to[:-2]):
+        if far:
+            p, far[-1] = lax.optimization_barrier((p, far[-1]))
+        far.append(over_grp(p, w, h))
     near = [swap(pieces[-2]), pieces[-1]]
 
     gains = jnp.sqrt(-jnp.expm1(-2.0 * pole_rates))
@@ -380,16 +386,18 @@
             totals[s] = t
 
     twos = [[s, s + 1] for s in range(1, count - 1, 2)]
-    for slots in [[0], *twos, [count - 1]]:
+    for slots in [[0], *twos]:
         run(slots, near_info, near)
-    for i, info in enumerate(far_info):
-        for slots in [*twos, [0, count - 1]]:
-            run(slots, info, far[i * len(far_ways) : (i + 1) * len(far_ways)])
+    early = [0, *range(1, count - 1)]
+    for i in range(len(far)):
+        for at in range(0, count - 1, 4):
+            run(early[at : at + 4], far_info[i], [far[i]])
+    run([count - 1], every_info, [*near, *far])
 
     step_back = jnp.arange(width, dtype=f32) - width
     edge = gains[None, :] * jnp.exp(step_back[:, None] * pole_rates[None, :])
     decay = jnp.exp(-width * pole_rates)[:, None]
-    partial = end(finish_info, totals, edge, decay, ways)
+    partial = end(finish_info, totals, edge, decay, length)
     arrived = [[over_grp(partial[w * per + r], w, 0) for w in range(1, ways)] for r in range(per)]
     received = []
     for r in range(per):

time: 151 us -> 129 us (0.85)
  the two profiles are of different devices: /device:TPU:4 before, /device:TPU:9 now
where the time goes in v2:
time: 129 us
  Pallas kernels  50.4 us (39%)
  waiting for transfers between devices  46.3 us (36%)
  starting transfers between devices  30 us (23%)
  local copies, waits for them, and re-layouts  1.85 us (1%)
    pallas_call x9, Pallas kernels, add_blocks(): pl.pallas_call(functools.partial(blocks_kernel, blocks, sets, fresh), in_...  38.7 us
    ppermute x15, waiting for transfers between devices, over_grp(): return lax.ppermute(x, 'grp', pairs)  25.5 us
    ppermute x15, starting transfers between devices, over_grp(): return lax.ppermute(x, 'grp', pairs)  14.6 us
    ppermute x3, waiting for transfers between devices, per_device(): going_right = lax.ppermute(going_right, 'ctx', right)  9.6 us
    ppermute x4, waiting for transfers between devices, per_device(): received.append(lax.ppermute(result, ('ctx', 'grp'), pairs))  9.39 us
    ppermute x4, starting transfers between devices, per_device(): received.append(lax.ppermute(result, ('ctx', 'grp'), pairs))  9.28 us
    pallas_call x1, Pallas kernels, cut(): pl.pallas_call(functools.partial(cut_kernel, plan), in_specs=[SM, ANY], o...  4.89 us
    ppermute x3, starting transfers between devices, per_device(): going_right = lax.ppermute(going_right, 'ctx', right)  3.89 us
  transfers between devices with their start and end apart: 27, of which 11 were waited for; matrix products, arithmetic and copies ran while one was open for 2% of the time, Pallas kernels for 32%

profile of v2, /device:TPU:9, one launch (start us, length us, event | category | flops | bytes accessed | tf_op | source)
XLA Modules:
  0.0 129.0 jit_solution(8460780957134344573)
XLA Ops:
  3.9 4.9 %cut_filters.1 = (bf16[4,128,1024]{2,1,0:T(8,128)(2,1)}, bf16[4,128,1024]{2,1,0:T(8,128)(2,1)}, bf16[4,128,1024]{2,1,0:T(8,128)(2,1)}, bf16[4,128,1024]{2,1,0:T(8,128)(2,1)}) custom-call(s32[8]{0:T(128)} %slice_bitcast_fusion.3.info, bf16[4,256,2048]{2,1,0:T(8,128)(2,1)} %mats.1), custom_call_target="tpu_custom_call" | custom-call | tf_op jit(solution)/shard_map/cut_filters/pallas_call | solution.py:83
  10.9 2.1 %collective-permute-done.refs_0_.refs_1_ = bf16[512,512]{1,0:T(8,128)(2,1)S(1)} collective-permute-done((bf16[512,512]{1,0:T(8,128)(2,1)}, bf16[512,512]{1,0:T(8,128)(2,1)S(1)}, u32[]{:S(2)}, u32[]{:S(2)}) %collective-permute-start) | collective-permute-done | bytes 524320 | tf_op jit(solution)/shard_map/ppermute | solution.py:360
  14.3 1.9 %pole_tables.1.refs_4_.refs_6_.refs_9_.refs_7_ = bf16[8,208,512]{2,1,0:T(8,128)(2,1)S(1)} custom-call(f32[80,18]{1,0:T(8,128)S(1)} %copy.24.poles_ref), custom_call_target="tpu_custom_call" | custom-call | flops 4000000000 | tf_op jit(solution)/shard_map/pole_tables/pallas_call | solution.py:54
  16.2 1.9 %collective-permute-start.4 = (bf16[512,512]{1,0:T(8,128)(2,1)S(1)}, bf16[512,512]{1,0:T(8,128)(2,1)S(1)}, u32[]{:S(2)}, u32[]{:S(2)}) collective-permute-start(bf16[512,512]{1,0:T(8,128)(2,1)S(1)} %collective-permute-done.refs_0_.refs_1_), channel_id=1, source_target_pairs={{0,1},{1,0},{2,3},{3,2},{4,5},{5,4},{6,7},{7,6},{8,9},{9,8},{10,11... | collective-permute-start | bytes 1572872 | tf_op jit(solution)/shard_map/ppermute | solution.py:353
  18.3 6.5 %collective-permute-done.2.refs_0_.refs_3_ = bf16[512,512]{1,0:T(8,128)(2,1)S(1)} collective-permute-done((bf16[512,512]{1,0:T(8,128)(2,1)S(1)}, bf16[512,512]{1,0:T(8,128)(2,1)S(1)}, u32[]{:S(2)}, u32[]{:S(2)}) %collective-permute-start.2) | collective-permute-done | bytes 524320 | tf_op jit(solution)/shard_map/ppermute | solution.py:360
  24.9 2.5 %collective-permute-start.5 = (bf16[512,512]{1,0:T(8,128)(2,1)S(1)}, bf16[512,512]{1,0:T(8,128)(2,1)S(1)}, u32[]{:S(2)}, u32[]{:S(2)}) collective-permute-start(bf16[512,512]{1,0:T(8,128)(2,1)S(1)} %collective-permute-done.1.refs_1_.refs_2_), channel_id=1, source_target_pairs={{0,1},{1,0},{2,3},{3,2},{4,5},{5,4},{6,7},{7,6},{8,9},{9,8},{10,11... | collective-permute-start | bytes 1572872 | tf_op jit(solution)/shard_map/ppermute | solution.py:353
  27.5 6.3 %collective-permute-done.7.refs_8_.refs_6_.refs_4_ = bf16[4,128,1024]{2,1,0:T(8,128)(2,1)S(1)} collective-permute-done((bf16[4,128,1024]{2,1,0:T(8,128)(2,1)}, bf16[4,128,1024]{2,1,0:T(8,128)(2,1)S(1)}, u32[]{:S(2)}, u32[]{:S(2)}) %collective-permute-start.7) | collective-permute-done | bytes 1048608 | tf_op jit(solution)/shard_map/ppermute | solution.py:353
  36.4 3.2 %add_blocks.9.refs_10_ = f32[208,512]{1,0:T(8,128)S(1)} custom-call(s32[3]{0:T(128)S(1)} %slice_bitcast_fusion.1.info, bf16[512,512]{1,0:T(8,128)(2,1)S(1)} %copy-done.1, bf16[512,512]{1,0:T(8,128)(2,1)} %collective-permute-done.3.refs_1_.refs_4_, bf16[4,128,1024]{2,1,0:T(8,128)(2,1)S(1)} %collective-permute-done.9.refs_2_.refs_4_, ...), custom_call_target="tpu_custom_call" | custom-call | flops 2400000000 | tf_op jit(solution)/shard_map/add_blocks/pallas_call | solution.py:141
  41.2 4.4 %add_blocks.10 = (f32[208,512]{1,0:T(8,128)S(1)}, f32[208,512]{1,0:T(8,128)S(1)}) custom-call(s32[3]{0:T(128)S(1)} %slice_bitcast_fusion.1.info, bf16[512,512]{1,0:T(8,128)(2,1)S(1)} %collective-permute-done.refs_0_.refs_1_, bf16[512,512]{1,0:T(8,128)(2,1)S(1)} %collective-permute-done.1.refs_1_.refs_2_, ...), custom_call_target="tpu_custom_call" | custom-call | flops 4800000000 | tf_op jit(solution)/shard_map/add_blocks/pallas_call | solution.py:141
  47.9 1.8 %collective-permute-done.13.refs_1_.refs_2_ = bf16[512,512]{1,0:T(8,128)(2,1)S(1)} collective-permute-done((bf16[512,512]{1,0:T(8,128)(2,1)S(1)}, bf16[512,512]{1,0:T(8,128)(2,1)S(1)}, u32[]{:S(2)}, u32[]{:S(2)}) %collective-permute-start.13) | collective-permute-done | bytes 524320 | tf_op jit(solution)/shard_map/ppermute | solution.py:361
  51.4 4.4 %add_blocks.11 = (f32[208,512]{1,0:T(8,128)S(1)}, f32[208,512]{1,0:T(8,128)S(1)}) custom-call(s32[3]{0:T(128)S(1)} %slice_bitcast_fusion.1.info, bf16[512,512]{1,0:T(8,128)(2,1)S(1)} %collective-permute-done.2.refs_0_.refs_3_, bf16[512,512]{1,0:T(8,128)(2,1)S(1)} %collective-permute-done.10.refs_1_.refs_0_, ...), custom_call_target="tpu_custom_call" | custom-call | flops 4800000000 | tf_op jit(solution)/shard_map/add_blocks/pallas_call | solution.py:141
  55.8 5.1 %add_blocks.12 = (f32[208,512]{1,0:T(8,128)S(1)}, f32[208,512]{1,0:T(8,128)S(1)}, f32[208,512]{1,0:T(8,128)S(1)}, f32[208,512]{1,0:T(8,128)S(1)}) custom-call(s32[2]{0:T(128)S(1)} %get-tuple-element.75.info, bf16[512,512]{1,0:T(8,128)(2,1)S(1)} %copy-done.1, ...), custom_call_target="tpu_custom_call", output_to_operand_aliasing={{0}: (11, {}), {1}: (12, {}), {2}: (13, {}), {3}: (14, {})} | custom-call | flops 4800000000 | tf_op jit(solution)/shard_map/add_blocks/pallas_call | solution.py:141
  61.5 4.4 %add_blocks.14 = (f32[208,512]{1,0:T(8,128)S(1)}, f32[208,512]{1,0:T(8,128)S(1)}) custom-call(s32[3]{0:T(128)S(1)} %slice_bitcast_fusion.1.info, bf16[512,512]{1,0:T(8,128)(2,1)S(1)} %collective-permute-done.12.refs_0_.refs_1_, bf16[512,512]{1,0:T(8,128)(2,1)S(1)} %collective-permute-done.13.refs_1_.refs_2_, ...), custom_call_target="tpu_custom_call" | custom-call | flops 4800000000 | tf_op jit(solution)/shard_map/add_blocks/pallas_call | solution.py:141
  66.0 3.6 %add_blocks.15 = (f32[208,512]{1,0:T(8,128)S(1)}, f32[208,512]{1,0:T(8,128)S(1)}, f32[208,512]{1,0:T(8,128)S(1)}) custom-call(s32[2]{0:T(128)S(1)} %get-tuple-element.75.info, bf16[512,512]{1,0:T(8,128)(2,1)S(1)} %collective-permute-done.10.refs_1_.refs_0_, ...), custom_call_target="tpu_custom_call", output_to_operand_aliasing={{0}: (9, {}), {1}: (10, {}), {2}: (11, {})} | custom-call | flops 3600000000 | tf_op jit(solution)/shard_map/add_blocks/pallas_call | solution.py:141
  69.6 3.9 %add_blocks.16 = (f32[208,512]{1,0:T(8,128)S(1)}, f32[208,512]{1,0:T(8,128)S(1)}, f32[208,512]{1,0:T(8,128)S(1)}) custom-call(s32[2]{0:T(128)S(1)} %get-tuple-element.76.info, bf16[512,512]{1,0:T(8,128)(2,1)S(1)} %collective-permute-done.10.refs_1_.refs_0_, ...), custom_call_target="tpu_custom_call", output_to_operand_aliasing={{0}: (9, {}), {1}: (10, {}), {2}: (11, {})} | custom-call | flops 3600000000 | tf_op jit(solution)/shard_map/add_blocks/pallas_call | solution.py:141
  73.5 5.1 %add_blocks.13 = (f32[208,512]{1,0:T(8,128)S(1)}, f32[208,512]{1,0:T(8,128)S(1)}, f32[208,512]{1,0:T(8,128)S(1)}, f32[208,512]{1,0:T(8,128)S(1)}) custom-call(s32[2]{0:T(128)S(1)} %get-tuple-element.76.info, bf16[512,512]{1,0:T(8,128)(2,1)S(1)} %copy-done.1, ...), custom_call_target="tpu_custom_call", output_to_operand_aliasing={{0}: (11, {}), {1}: (12, {}), {2}: (13, {}), {3}: (14, {})} | custom-call | flops 4800000000 | tf_op jit(solution)/shard_map/add_blocks/pallas_call | solution.py:141
  78.6 4.5 %add_blocks.17.refs_7_ = f32[208,512]{1,0:T(8,128)S(1)} custom-call(s32[5]{0:T(128)S(1)} %slice_bitcast_fusion.info, bf16[512,512]{1,0:T(8,128)(2,1)S(1)} %constant_dynamic-update-slice_fusion.refs_0_, bf16[512,512]{1,0:T(8,128)(2,1)S(1)} %collective-permute-done.18.refs_1_, bf16[4,128,1024]{2,1,0:T(8,128)(2,1)S(1)} %collective-permute-done.9.refs_2_.refs_4_, ...), custom_call_target="tpu_custom_call" | custom-call | flops 4800000000 | tf_op jit(solution)/shard_map/add_blocks/pallas_call | solution.py:141
  83.1 3.4 %finish_blocks.1 = (f32[512,128]{1,0:T(8,128)S(1)}, f32[512,128]{1,0:T(8,128)S(1)}, f32[512,128]{1,0:T(8,128)S(1)}, f32[512,128]{1,0:T(8,128)S(1)}, f32[512,128]...) custom-call(s32[16]{0:T(128)S(1)} %slice_bitcast_fusion.5.info, ...), custom_call_target="tpu_custom_call" | custom-call | flops 3000000000 | tf_op jit(solution)/shard_map/finish_blocks/pallas_call | solution.py:188
  89.5 4.9 %collective-permute-done.19.refs_1_ = f32[512,128]{1,0:T(8,128)S(1)} collective-permute-done((f32[512,128]{1,0:T(8,128)S(1)}, f32[512,128]{1,0:T(8,128)S(1)}, u32[]{:S(2)}, u32[]{:S(2)}) %collective-permute-start.19) | collective-permute-done | bytes 262176 | tf_op jit(solution)/shard_map/ppermute | solution.py:353
  95.2 4.9 %collective-permute-done.21.refs_1_ = f32[512,128]{1,0:T(8,128)S(1)} collective-permute-done((f32[512,128]{1,0:T(8,128)S(1)}, f32[512,128]{1,0:T(8,128)S(1)}, u32[]{:S(2)}, u32[]{:S(2)}) %collective-permute-start.21) | collective-permute-done | bytes 262176 | tf_op jit(solution)/shard_map/ppermute | solution.py:353
  101.5 8.9 %collective-permute-done.23.refs_1_ = f32[512,128]{1,0:T(8,128)S(1)} collective-permute-done((f32[512,128]{1,0:T(8,128)S(1)}, f32[512,128]{1,0:T(8,128)S(1)}, u32[]{:S(2)}, u32[]{:S(2)}) %collective-permute-start.23) | collective-permute-done | bytes 262176 | tf_op jit(solution)/shard_map/ppermute | solution.py:353
  110.4 5.2 %collective-permute-start.24 = (bf16[512,128]{1,0:T(8,128)(2,1)S(1)}, bf16[512,128]{1,0:T(8,128)(2,1)S(1)}, u32[]{:S(2)}, u32[]{:S(2)}) collective-permute-start(bf16[512,128]{1,0:T(8,128)(2,1)S(1)} %combine_ways.6), channel_id=1, source_target_pairs={{0,16},{1,24},{2,20},{3,28},{4,4},{5,12},{6,0},{7,8},{8,17},{9,25}... | collective-permute-start | bytes 393224 | tf_op jit(solution)/shard_map/ppermute | solution.py:411
  116.0 2.1 %collective-permute-start.26 = (bf16[512,128]{1,0:T(8,128)(2,1)S(1)}, bf16[512,128]{1,0:T(8,128)(2,1)S(1)}, u32[]{:S(2)}, u32[]{:S(2)}) collective-permute-start(bf16[512,128]{1,0:T(8,128)(2,1)S(1)} %combine_ways.7), channel_id=1, source_target_pairs={{0,24},{1,0},{2,28},{3,4},{4,12},{5,20},{6,8},{7,16},{8,25},{9,1},... | collective-permute-start | bytes 393224 | tf_op jit(solution)/shard_map/ppermute | solution.py:411
  119.9 7.6 %collective-permute-done.26.refs_3_ = bf16[512,128]{1,0:T(8,128)(2,1)S(1)} collective-permute-done((bf16[512,128]{1,0:T(8,128)(2,1)S(1)}, bf16[512,128]{1,0:T(8,128)(2,1)S(1)}, u32[]{:S(2)}, u32[]{:S(2)}) %collective-permute-start.26) | collective-permute-done | bytes 131104 | tf_op jit(solution)/shard_map/ppermute | solution.py:411
  (74 shorter events, 25.0 us)
Async XLA Ops:
  0.0 13.0 %collective-permute-start = (bf16[512,512]{1,0:T(8,128)(2,1)}, bf16[512,512]{1,0:T(8,128)(2,1)S(1)}, u32[]{:S(2)}, u32[]{:S(2)}) collective-permute-start(bf16[512,512]{1,0:T(8,128)(2,1)} %refs_0_.5), channel_id=1, source_target_pairs={{0,8},{8,16},{16,24},{24,28},{28,20},{20,12},{12,4},{4,0},{1,9},{9... | collective-permute-start | bytes 1572872 | tf_op jit(solution)/shard_map/ppermute | solution.py:360
  1.3 14.9 %collective-permute-start.1 = (bf16[512,512]{1,0:T(8,128)(2,1)}, bf16[512,512]{1,0:T(8,128)(2,1)S(1)}, u32[]{:S(2)}, u32[]{:S(2)}) collective-permute-start(bf16[512,512]{1,0:T(8,128)(2,1)} %refs_0_.5), channel_id=1, source_target_pairs={{8,0},{16,8},{24,16},{28,24},{20,28},{12,20},{4,12},{0,4},{9,1},{1... | collective-permute-start | bytes 1572872 | tf_op jit(solution)/shard_map/ppermute | solution.py:361
  1.5 16.6 %collective-permute-start.3 = (bf16[512,512]{1,0:T(8,128)(2,1)}, bf16[512,512]{1,0:T(8,128)(2,1)}, u32[]{:S(2)}, u32[]{:S(2)}) collective-permute-start(bf16[512,512]{1,0:T(8,128)(2,1)} %refs_0_.5), channel_id=1, source_target_pairs={{0,1},{1,0},{2,3},{3,2},{4,5},{5,4},{6,7},{7,6},{8,9},{9,8},{10,11... | collective-permute-start | bytes 1572872 | tf_op jit(solution)/shard_map/ppermute | solution.py:353
  8.8 25.1 %collective-permute-start.7 = (bf16[4,128,1024]{2,1,0:T(8,128)(2,1)}, bf16[4,128,1024]{2,1,0:T(8,128)(2,1)S(1)}, u32[]{:S(2)}, u32[]{:S(2)}) collective-permute-start(bf16[4,128,1024]{2,1,0:T(8,128)(2,1)} %get-tuple-element.40), channel_id=1, source_target_pairs={{0,2},{1,3},{2,0},{3,1},{4,6},{5,7},{6,4},{7,5},{8,10},{9,11},{10,... | collective-permute-start | bytes 3145736 | tf_op jit(solution)/shard_map/ppermute | solution.py:353
  10.1 26.1 %collective-permute-start.9 = (bf16[4,128,1024]{2,1,0:T(8,128)(2,1)}, bf16[4,128,1024]{2,1,0:T(8,128)(2,1)S(1)}, u32[]{:S(2)}, u32[]{:S(2)}) collective-permute-start(bf16[4,128,1024]{2,1,0:T(8,128)(2,1)} %get-tuple-element.43), channel_id=1, source_target_pairs={{0,1},{1,0},{2,3},{3,2},{4,5},{5,4},{6,7},{7,6},{8,9},{9,8},{10,11... | collective-permute-start | bytes 3145736 | tf_op jit(solution)/shard_map/ppermute | solution.py:353
  13.0 11.9 %collective-permute-start.2 = (bf16[512,512]{1,0:T(8,128)(2,1)S(1)}, bf16[512,512]{1,0:T(8,128)(2,1)S(1)}, u32[]{:S(2)}, u32[]{:S(2)}) collective-permute-start(bf16[512,512]{1,0:T(8,128)(2,1)S(1)} %collective-permute-done.refs_0_.refs_1_), channel_id=1, source_target_pairs={{0,8},{8,16},{16,24},{24,28},{28,20},{20,12},{12,4},{4,0},{1,9},{9... | collective-permute-start | bytes 1572872 | tf_op jit(solution)/shard_map/ppermute | solution.py:360
  16.2 11.2 %collective-permute-start.4 = (bf16[512,512]{1,0:T(8,128)(2,1)S(1)}, bf16[512,512]{1,0:T(8,128)(2,1)S(1)}, u32[]{:S(2)}, u32[]{:S(2)}) collective-permute-start(bf16[512,512]{1,0:T(8,128)(2,1)S(1)} %collective-permute-done.refs_0_.refs_1_), channel_id=1, source_target_pairs={{0,1},{1,0},{2,3},{3,2},{4,5},{5,4},{6,7},{7,6},{8,9},{9,8},{10,11... | collective-permute-start | bytes 1572872 | tf_op jit(solution)/shard_map/ppermute | solution.py:353
  18.1 17.1 %collective-permute-start.10 = (bf16[512,512]{1,0:T(8,128)(2,1)S(1)}, bf16[512,512]{1,0:T(8,128)(2,1)S(1)}, u32[]{:S(2)}, u32[]{:S(2)}) collective-permute-start(bf16[512,512]{1,0:T(8,128)(2,1)S(1)} %collective-permute-done.1.refs_1_.refs_2_), channel_id=1, source_target_pairs={{8,0},{16,8},{24,16},{28,24},{20,28},{12,20},{4,12},{0,4},{9,1},{1... | collective-permute-start | bytes 1572872 | tf_op jit(solution)/shard_map/ppermute | solution.py:361
  24.9 14.7 %collective-permute-start.5 = (bf16[512,512]{1,0:T(8,128)(2,1)S(1)}, bf16[512,512]{1,0:T(8,128)(2,1)S(1)}, u32[]{:S(2)}, u32[]{:S(2)}) collective-permute-start(bf16[512,512]{1,0:T(8,128)(2,1)S(1)} %collective-permute-done.1.refs_1_.refs_2_), channel_id=1, source_target_pairs={{0,1},{1,0},{2,3},{3,2},{4,5},{5,4},{6,7},{7,6},{8,9},{9,8},{10,11... | collective-permute-start | bytes 1572872 | tf_op jit(solution)/shard_map/ppermute | solution.py:353
  27.5 22.7 %collective-permute-start.6 = (bf16[512,512]{1,0:T(8,128)(2,1)S(1)}, bf16[512,512]{1,0:T(8,128)(2,1)S(1)}, u32[]{:S(2)}, u32[]{:S(2)}) collective-permute-start(bf16[512,512]{1,0:T(8,128)(2,1)S(1)} %collective-permute-done.2.refs_0_.refs_3_), channel_id=1, source_target_pairs={{0,1},{1,0},{2,3},{3,2},{4,5},{5,4},{6,7},{7,6},{8,9},{9,8},{10,11... | collective-permute-start | bytes 1572872 | tf_op jit(solution)/shard_map/ppermute | solution.py:353
  33.9 12.7 %collective-permute-start.12 = (bf16[512,512]{1,0:T(8,128)(2,1)S(1)}, bf16[512,512]{1,0:T(8,128)(2,1)S(1)}, u32[]{:S(2)}, u32[]{:S(2)}) collective-permute-start(bf16[512,512]{1,0:T(8,128)(2,1)S(1)} %collective-permute-done.2.refs_0_.refs_3_), channel_id=1, source_target_pairs={{0,8},{8,16},{16,24},{24,28},{28,20},{20,12},{12,4},{4,0},{1,9},{9... | collective-permute-start | bytes 1572872 | tf_op jit(solution)/shard_map/ppermute | solution.py:360
  35.2 16.1 %collective-permute-start.11 = (bf16[512,512]{1,0:T(8,128)(2,1)S(1)}, bf16[512,512]{1,0:T(8,128)(2,1)S(1)}, u32[]{:S(2)}, u32[]{:S(2)}) collective-permute-start(bf16[512,512]{1,0:T(8,128)(2,1)S(1)} %collective-permute-done.10.refs_1_.refs_0_), channel_id=1, source_target_pairs={{0,1},{1,0},{2,3},{3,2},{4,5},{5,4},{6,7},{7,6},{8,9},{9,8},{10,11... | collective-permute-start | bytes 1572872 | tf_op jit(solution)/shard_map/ppermute | solution.py:353
  36.2 13.5 %collective-permute-start.13 = (bf16[512,512]{1,0:T(8,128)(2,1)S(1)}, bf16[512,512]{1,0:T(8,128)(2,1)S(1)}, u32[]{:S(2)}, u32[]{:S(2)}) collective-permute-start(bf16[512,512]{1,0:T(8,128)(2,1)S(1)} %collective-permute-done.10.refs_1_.refs_0_), channel_id=1, source_target_pairs={{8,0},{16,8},{24,16},{28,24},{20,28},{12,20},{4,12},{0,4},{9,1},{1... | collective-permute-start | bytes 1572872 | tf_op jit(solution)/shard_map/ppermute | solution.py:361
  39.6 30.0 %collective-permute-start.8 = (bf16[4,128,1024]{2,1,0:T(8,128)(2,1)S(1)}, bf16[4,128,1024]{2,1,0:T(8,128)(2,1)S(1)}, u32[]{:S(2)}, u32[]{:S(2)}) collective-permute-start(bf16[4,128,1024]{2,1,0:T(8,128)(2,1)S(1)} %copy-done.4), channel_id=1, source_target_pairs={{0,3},{1,2},{2,1},{3,0},{4,7},{5,6},{6,5},{7,4},{8,11},{9,10},{10,... | collective-permute-start | bytes 3145736 | tf_op jit(solution)/shard_map/ppermute | solution.py:353
  46.6 14.4 %collective-permute-start.16 = (bf16[256,512]{1,0:T(8,128)(2,1)S(1)}, bf16[256,512]{1,0:T(8,128)(2,1)S(1)}, u32[]{:S(2)}, u32[]{:S(2)}) collective-permute-start(bf16[256,512]{1,0:T(8,128)(2,1)S(1)} %slice.64), channel_id=1, source_target_pairs={{0,8},{8,16},{16,24},{24,28},{28,20},{20,12},{12,4},{4,0},{1,9},{9... | collective-permute-start | bytes 786440 | tf_op jit(solution)/shard_map/ppermute | solution.py:365
  49.8 11.2 %collective-permute-start.17 = (bf16[256,512]{1,0:T(8,128)(2,1)S(1)}, bf16[256,512]{1,0:T(8,128)(2,1)S(1)}, u32[]{:S(2)}, u32[]{:S(2)}) collective-permute-start(bf16[256,512]{1,0:T(8,128)(2,1)S(1)} %slice.65), channel_id=1, source_target_pairs={{8,0},{16,8},{24,16},{28,24},{20,28},{12,20},{4,12},{0,4},{9,1},{1... | collective-permute-start | bytes 786440 | tf_op jit(solution)/shard_map/ppermute | solution.py:365
  50.2 11.4 %collective-permute-start.14 = (bf16[512,512]{1,0:T(8,128)(2,1)S(1)}, bf16[512,512]{1,0:T(8,128)(2,1)S(1)}, u32[]{:S(2)}, u32[]{:S(2)}) collective-permute-start(bf16[512,512]{1,0:T(8,128)(2,1)S(1)} %collective-permute-done.12.refs_0_.refs_1_), channel_id=1, source_target_pairs={{0,1},{1,0},{2,3},{3,2},{4,5},{5,4},{6,7},{7,6},{8,9},{9,8},{10,11... | collective-permute-start | bytes 1572872 | tf_op jit(solution)/shard_map/ppermute | solution.py:353
  61.0 17.6 %collective-permute-start.18 = (bf16[512,512]{1,0:T(8,128)(2,1)S(1)}, bf16[512,512]{1,0:T(8,128)(2,1)S(1)}, u32[]{:S(2)}, u32[]{:S(2)}) collective-permute-start(bf16[512,512]{1,0:T(8,128)(2,1)S(1)} %constant_dynamic-update-slice_fusion.refs_0_), channel_id=1, source_target_pairs={{0,1},{1,0},{2,3},{3,2},{4,5},{5,4},{6,7},{7,6},{8,9},{9,8},{10,11... | collective-permute-start | bytes 1572872 | tf_op jit(solution)/shard_map/ppermute | solution.py:353
  87.8 12.2 %collective-permute-start.21 = (f32[512,128]{1,0:T(8,128)S(1)}, f32[512,128]{1,0:T(8,128)S(1)}, u32[]{:S(2)}, u32[]{:S(2)}) collective-permute-start(f32[512,128]{1,0:T(8,128)S(1)} %get-tuple-element.68), channel_id=1, source_target_pairs={{0,2},{1,3},{2,0},{3,1},{4,6},{5,7},{6,4},{7,5},{8,10},{9,11},{10,... | collective-permute-start | bytes 786440 | tf_op jit(solution)/shard_map/ppermute | solution.py:353
  88.1 22.3 %collective-permute-start.23 = (f32[512,128]{1,0:T(8,128)S(1)}, f32[512,128]{1,0:T(8,128)S(1)}, u32[]{:S(2)}, u32[]{:S(2)}) collective-permute-start(f32[512,128]{1,0:T(8,128)S(1)} %get-tuple-element.70), channel_id=1, source_target_pairs={{0,2},{1,3},{2,0},{3,1},{4,6},{5,7},{6,4},{7,5},{8,10},{9,11},{10,... | collective-permute-start | bytes 786440 | tf_op jit(solution)/shard_map/ppermute | solution.py:353
  89.3 26.7 %collective-permute-start.25 = (f32[512,128]{1,0:T(8,128)S(1)}, f32[512,128]{1,0:T(8,128)S(1)}, u32[]{:S(2)}, u32[]{:S(2)}) collective-permute-start(f32[512,128]{1,0:T(8,128)S(1)} %get-tuple-element.72), channel_id=1, source_target_pairs={{0,2},{1,3},{2,0},{3,1},{4,6},{5,7},{6,4},{7,5},{8,10},{9,11},{10,... | collective-permute-start | bytes 786440 | tf_op jit(solution)/shard_map/ppermute | solution.py:353
  94.5 23.6 %collective-permute-start.20 = (bf16[512,128]{1,0:T(8,128)(2,1)S(1)}, bf16[512,128]{1,0:T(8,128)(2,1)S(1)}, u32[]{:S(2)}, u32[]{:S(2)}) collective-permute-start(bf16[512,128]{1,0:T(8,128)(2,1)S(1)} %combine_ways.4), channel_id=1, source_target_pairs={{0,0},{1,8},{2,4},{3,12},{4,20},{5,28},{6,16},{7,24},{8,1},{9,9},{... | collective-permute-start | bytes 393224 | tf_op jit(solution)/shard_map/ppermute | solution.py:411
  100.1 18.0 %collective-permute-start.22 = (bf16[512,128]{1,0:T(8,128)(2,1)S(1)}, bf16[512,128]{1,0:T(8,128)(2,1)S(1)}, u32[]{:S(2)}, u32[]{:S(2)}) collective-permute-start(bf16[512,128]{1,0:T(8,128)(2,1)S(1)} %combine_ways.5), channel_id=1, source_target_pairs={{0,8},{1,16},{2,12},{3,20},{4,28},{5,4},{6,24},{7,0},{8,9},{9,17},... | collective-permute-start | bytes 393224 | tf_op jit(solution)/shard_map/ppermute | solution.py:411
  116.0 11.5 %collective-permute-start.26 = (bf16[512,128]{1,0:T(8,128)(2,1)S(1)}, bf16[512,128]{1,0:T(8,128)(2,1)S(1)}, u32[]{:S(2)}, u32[]{:S(2)}) collective-permute-start(bf16[512,128]{1,0:T(8,128)(2,1)S(1)} %combine_ways.7), channel_id=1, source_target_pairs={{0,24},{1,0},{2,28},{3,4},{4,12},{5,20},{6,8},{7,16},{8,25},{9,1},... | collective-permute-start | bytes 393224 | tf_op jit(solution)/shard_map/ppermute | solution.py:411
  (8 other events, 103.3 us)

commit v3 on v2

v3 whole, which is shorter than its diff:
```python
import functools
import random

import jax
import jax.numpy as jnp
import numpy as np
from jax import lax
from jax.experimental import pallas as pl
from jax.experimental.pallas import tpu as pltpu
from jax.sharding import PartitionSpec as P

exact_prec = lax.Precision.HIGHEST
f32, bf16 = jnp.float32, jnp.bfloat16
NT = (((1,), (1,)), ((), ()))
VM = pl.BlockSpec(memory_space=pltpu.VMEM)
ANY = pl.BlockSpec(memory_space=pl.ANY)
SM = pl.BlockSpec(memory_space=pltpu.SMEM)


def params(mib=16):
    return pltpu.CompilerParams(vmem_limit_bytes=mib * 2**20)


def split2(x):
    high = x.astype(bf16)
    return high, (x - high.astype(f32)).astype(bf16)


def tables_kernel(poles_ref, out):
    poles, width = poles_ref.shape[0], out.shape[2] // 4
    rate, gain = poles_ref[:, 0:1], poles_ref[:, 1:2]
    lag = lax.broadcasted_iota(jnp.int32, (poles, width), 1).astype(f32)
    decay = jnp.exp(-rate * lag)
    gained = gain * decay
    columns = lax.broadcasted_iota(jnp.int32, (poles, poles_ref.shape[1]), 1)

    @pl.loop(0, out.shape[0])
    def _(pair):
        for j in range(2):
            chosen = jnp.where(columns == 2 + 2 * pair + j, poles_ref[...], 0.0)
            coef = jnp.sum(chosen, axis=1, keepdims=True)
            phi = jnp.sum(coef * gained, axis=0, keepdims=True)
            line = jnp.concatenate([phi, jnp.zeros((1, width), f32)], axis=1)
            rolled = pltpu.roll(jnp.broadcast_to(line, (width, 2 * width)), 0, 1, stride=1, stride_axis=0)
            near, weight = split2(rolled[:, :width]), split2(coef * decay)
            for at in range(2):
                lanes = slice((2 * at + j) * width, (2 * at + j + 1) * width)
                out[pair, :width, lanes] = near[at]
                out[pair, width:, lanes] = weight[at]


def tables(coeffs, rates, gains, width):
    filters, poles = coeffs.shape
    joined = jnp.concatenate([rates[:, None], gains[:, None], coeffs.T], axis=1)
    return pl.pallas_call(
        tables_kernel,
        in_specs=[VM],
        out_specs=VM,
        out_shape=jax.ShapeDtypeStruct((filters // 2, width + poles, 4 * width), bf16),
        compiler_params=params(),
        cost_estimate=pl.CostEstimate(flops=int(4e9), bytes_accessed=0, transcendentals=0),
        name="pole_tables",
    )(joined)


def cut_kernel(to, mats, *refs):
    outs, sems = refs[:-1], refs[-1]
    way, here = lax.axis_index("grp") // 2, lax.axis_index("grp") % 2
    copies = []
    for i, (by_way, by_core) in enumerate(to):
        _, half, cols = outs[i].shape
        row = (1 - here if by_core else here) * half
        col = (1 - way if by_way else way) * cols
        src = mats.at[:, pl.ds(pl.multiple_of(row, half), half), pl.ds(pl.multiple_of(col, cols), cols)]
        copies.append(pltpu.make_async_copy(src, outs[i], sems.at[i]))
    for c in copies:
        c.start()
    for c in copies:
        c.wait()


def cut(mats, to, half, cols):
    return pl.pallas_call(
        functools.partial(cut_kernel, to),
        in_specs=[ANY],
        out_specs=[VM] * len(to),
        out_shape=[jax.ShapeDtypeStruct((mats.shape[0], half, cols), bf16)] * len(to),
        scratch_shapes=[pltpu.SemaphoreType.DMA((len(to),))],
        compiler_params=params(60),
        name="cut_filters",
    )(mats)


def products(work, info_at, info, mine, other, mats, table, before, after, held):
    wide = mine[0].shape[1]
    here = info[info_at[0]]
    width = table.shape[2] // 4
    half = mats[0].shape[1]
    subs = mine[0].shape[0] // width
    units = [(i, n, b) for i in range(mats[0].shape[0] // 2) for n, b in work]
    for u, (i, n, b) in enumerate(units):
        two = mats[n].at[pl.ds(2 * i, 2)]
        m_mine = two[:, :, pl.ds(pl.multiple_of(here * wide, wide), wide)].reshape(2 * half, wide)
        m_other = two[:, :, pl.ds(pl.multiple_of((1 - here) * wide, wide), wide)].reshape(2 * half, wide)
        proj = lax.dot_general(mine[b][...], m_mine, NT, preferred_element_type=f32)
        proj += lax.dot_general(other[b][...], m_other, NT, preferred_element_type=f32)
        for at, part in enumerate(split2(proj)):
            for j in range(2):
                rows = pl.ds((2 * at + j) * width, width)
                for s in range(subs):
                    held[u, rows, s * half : (s + 1) * half] = part[
                        s * width : (s + 1) * width, j * half : (j + 1) * half
                    ]
    begun = set()
    for u, (i, n, b) in enumerate(units):
        pair = info[info_at[1 + n]] + i
        high, low = held[u, : 2 * width, :], held[u, 2 * width :, :]
        add = jnp.dot(table[pair, :, : 2 * width], high, preferred_element_type=f32)
        add += jnp.dot(table[pair, :, 2 * width :], high, preferred_element_type=f32)
        add += jnp.dot(table[pair, :, : 2 * width], low, preferred_element_type=f32)
        if b in begun:
            after[b][...] += add
        else:
            after[b][...] = add if before[b] is None else before[b][...] + add
            begun.add(b)


def blocks_kernel(blocks, sets, work, info_at, fresh, closing, info, *refs):
    refs = list(refs)
    take = lambda n: [refs.pop(0) for _ in range(n)]
    mine, other, mats, (table,) = take(blocks), take(blocks), take(sets), take(1)
    before = [None if new else refs.pop(0) for new in fresh]
    if not closing:
        after, (held,) = take(blocks), take(1)
        products(work, info_at, info, mine, other, mats, table, before, after, held)
        return
    edge, decay, kept, sent, *states = take(4 + blocks)
    held, after = refs
    after = [after.at[b] for b in range(blocks)]
    products(work, info_at, info, mine, other, mats, table, before, after, held)
    width, poles = edge.shape
    half = mats[0].shape[1]
    subs = mine[0].shape[0] // width
    eh, el = split2(edge[...])
    left = jnp.concatenate([eh, el, eh], axis=1)
    values = []
    for b in range(blocks):
        state, enters, carried = after[b][width:, :], [], jnp.zeros((poles, half), f32)
        for s in reversed(range(subs)):
            enters.append(carried)
            carried = state[:, s * half : (s + 1) * half] + decay[...] * carried
        states[b][...] = carried
        ch, cl = split2(jnp.concatenate(enters[::-1], axis=1))
        far = jnp.dot(left, jnp.concatenate([ch, ch, cl], axis=0), preferred_element_type=f32)
        values.append(after[b][:width, :] + far)
    first = info[closing] == 0
    for ref, one, two in ((kept, *values), (sent, *reversed(values))):
        value = jnp.where(first, one, two)
        for s in range(subs):
            ref[s * width : (s + 1) * width, :] = value[:, s * half : (s + 1) * half]


def add_blocks(info, info_at, mine, other, mats, table, totals, work, ends=None, closing=0):
    blocks, sets = len(mine), len(mats)
    fresh = [t is None for t in totals]
    old = [t for t in totals if t is not None]
    half, length = mats[0].shape[1], mine[0].shape[0]
    height, tw = table.shape[1:]
    lanes = length // (tw // 4) * half
    units = len(work) * mats[0].shape[0] // 2
    first = 1 + 2 * blocks + sets + 1
    scratch = [pltpu.VMEM((units, tw, lanes), bf16)]
    if ends is None:
        ends, aliases = (), {first + i: b for i, b in enumerate(b for b in range(blocks) if not fresh[b])}
        shapes = [jax.ShapeDtypeStruct((height, lanes), f32)] * blocks
    else:
        aliases = {}
        shapes = [jax.ShapeDtypeStruct((length, half), f32)] * 2
        shapes += [jax.ShapeDtypeStruct((height - tw // 4, half), f32)] * blocks
        scratch.append(pltpu.VMEM((blocks, height, lanes), f32))
    return pl.pallas_call(
        functools.partial(blocks_kernel, blocks, sets, work, info_at, fresh, closing),
        in_specs=[SM] + [VM] * (2 * blocks + sets + 1 + len(old) + len(ends)),
        out_specs=[VM] * len(shapes),
        out_shape=shapes,
        scratch_shapes=scratch,
        input_output_aliases=aliases,
        compiler_params=params(24 if closing else 16),
        cost_estimate=pl.CostEstimate(flops=int(units * 0.6e9), bytes_accessed=0, transcendentals=0),
        name="close_blocks" if closing else "add_blocks",
    )(info, *mine, *other, *mats, table, *old, *ends)


def carry_kernel(count, slots_at, use_at, info, *refs):
    states, decay, (kept, sent), (held, entering) = refs[:count], refs[count], refs[count + 1 : count + 3], refs[count + 3 :]
    for s in range(count):
        held[info[slots_at + s]] = states[s][...]
    carried = jnp.zeros_like(states[0])
    for c in reversed(range(count)):
        entering[c] = carried
        carried = held[c] + decay[...] * carried
    per = kept.shape[0]
    for r in range(per):
        kept[r] = entering[info[use_at + r]]
        sent[r] = entering[info[use_at + per + r]]


def carry(info, slots_at, use_at, states, decay):
    count, shape = len(states), states[0].shape
    return pl.pallas_call(
        functools.partial(carry_kernel, count, slots_at, use_at),
        in_specs=[SM] + [VM] * (count + 1),
        out_specs=[VM] * 2,
        out_shape=[jax.ShapeDtypeStruct((count // 2, *shape), f32)] * 2,
        scratch_shapes=[pltpu.VMEM((count, *shape), f32)] * 2,
        compiler_params=params(),
        name="carry_states",
    )(info, *states, decay)


def result_kernel(pairs, here_at, info, *refs):
    kept, arrived = refs[: len(pairs)], refs[len(pairs) : 2 * len(pairs)]
    carry_kept, carry_arrived, edge, *outs = refs[2 * len(pairs) :]
    eh, el = split2(edge[...])
    left = jnp.concatenate([eh, el, eh], axis=1)
    values = []
    for n, r in enumerate(pairs):
        ch, cl = split2(carry_kept[r] + carry_arrived[r])
        far = jnp.dot(left, jnp.concatenate([ch, ch, cl], axis=0), preferred_element_type=f32)
        values.append((kept[n][...] + arrived[n][...] + far).astype(bf16))
    first = info[here_at] == 0
    outs[0][...] = jnp.where(first, values[0], values[1])
    outs[1][...] = jnp.where(first, values[1], values[0])


def results(info, here_at, pairs, kept, arrived, carries, edge):
    return pl.pallas_call(
        functools.partial(result_kernel, pairs, here_at),
        in_specs=[SM] + [VM] * (2 * len(pairs) + 3),
        out_specs=[VM] * len(pairs),
        out_shape=[jax.ShapeDtypeStruct(kept[0].shape, bf16)] * len(pairs),
        compiler_params=params(),
        name="finish_blocks",
    )(info, *kept, *arrived, *carries, edge)


def arrange_kernel(count, lanes_at, info, *refs):
    out = refs[count]
    lanes = refs[0].shape[1]
    for r in range(count):
        out[:, pl.ds(pl.multiple_of(info[lanes_at + r] * lanes, lanes), lanes)] = refs[r][...]


def arrange(info, lanes_at, parts):
    rows, lanes = parts[0].shape
    return pl.pallas_call(
        functools.partial(arrange_kernel, len(parts), lanes_at),
        in_specs=[SM] + [VM] * len(parts),
        out_specs=VM,
        out_shape=jax.ShapeDtypeStruct((rows, lanes * len(parts)), bf16),
        compiler_params=params(),
        name="arrange_features",
    )(info, *parts)


def plain_tables(coeffs, rates, gains, width):
    lag = jnp.arange(width, dtype=f32)
    decay = jnp.exp(-rates[:, None] * lag[None, :])
    shift = lag[None, :] - lag[:, None]
    phi = jnp.dot(coeffs * gains[None, :], decay, precision=exact_prec)
    near = jnp.where(shift >= 0, phi[:, jnp.maximum(shift, 0).astype(jnp.int32)], 0.0)
    return jnp.concatenate([near, coeffs[:, :, None] * decay[None]], axis=1)


def plain_cut(mats, info, plan, half, cols):
    return [
        lax.dynamic_slice(mats, (lo, info[2 * i], info[2 * i + 1]), (n, half, cols)) for i, (lo, n) in enumerate(plan)
    ]


def plain_add(info, mine, other, mats, table, totals, work):
    results = []
    wide, width = mine[0].shape[1], table.shape[2]
    for b in range(len(mine)):
        rows = jnp.concatenate([mine[b], other[b]], axis=1)
        total = 0.0 if totals[b] is None else totals[b]
        for n in [n for n, at in work if at == b]:
            use = lax.dynamic_slice_in_dim(table, 2 * info[1 + n], mats[n].shape[0], 0)
            swapped = jnp.where(info[0] == 0, mats[n], jnp.roll(mats[n], wide, axis=2))
            proj = jnp.einsum("tj,kij->kti", rows, swapped, preferred_element_type=f32)
            proj = jnp.concatenate(jnp.split(proj, rows.shape[0] // width, axis=1), axis=2)
            total = total + jnp.einsum("kst,kti->si", use, proj, precision=exact_prec)
        results.append(total)
    return results


def plain_finish(info, totals, edge, decay, length):
    count, width = len(totals), edge.shape[0]
    subs = length // width
    held = jnp.zeros((count,) + totals[0].shape, f32)
    for s in range(count):
        held = lax.dynamic_update_slice(held, totals[s][None], (info[s], 0, 0))
    carried, values = jnp.zeros((edge.shape[1], totals[0].shape[1] // subs), f32), [None] * count
    for c in reversed(range(count)):
        enters = []
        for state in reversed(jnp.split(held[c, width:], subs, axis=1)):
            enters.append(carried)
            carried = state + decay * carried
        far = jnp.dot(edge, jnp.concatenate(enters[::-1], axis=1), precision=exact_prec)
        values[c] = jnp.concatenate(jnp.split(held[c, :width] + far, subs, axis=1), axis=0)
    values = jnp.stack(values)
    return [values[info[count + n]] for n in range(count)]


def plain_combine(parts):
    return sum(parts[1:], parts[0]).astype(bf16)


def plain_arrange(info, parts):
    rows, lanes = parts[0].shape
    out = jnp.zeros((rows, lanes * len(parts)), bf16)
    for r, part in enumerate(parts):
        out = lax.dynamic_update_slice(out, part, (0, info[r] * lanes))
    return out


def ring_of(count):
    order = [*range(0, count, 2), *reversed(range(1, count, 2))]
    offsets = [0]
    for step in range(1, count // 2):
        offsets += [-step, step]
    return order, [*offsets, count // 2]


def shift_of(x, ways, by_way, by_core):
    rank = lambda w, h: (w % ways) * 2 + h
    return lax.ppermute(x, "grp", [(rank(w, h), rank(w + by_way, h ^ by_core)) for w in range(ways) for h in range(2)])


def my_row(count, groups, numbers):
    rows = [numbers(c, g) for c in range(count) for g in range(groups)]
    ends = np.cumsum([len(part) for part in rows[0]])
    known = jnp.asarray(np.array([sum(r, []) for r in rows], np.int32))
    me = lax.axis_index("ctx") * groups + lax.axis_index("grp")
    row = lax.dynamic_slice(known, (me, 0), (1, known.shape[1]))[0]
    return row, [int(e) - len(part) for e, part in zip(ends, rows[0])], [int(e) for e in ends]


def plain_device(out_grad, filter_mats, coeffs, pole_rates):
    count, groups = lax.axis_size("ctx"), lax.axis_size("grp")
    ways, per_grp = groups // 2, count // groups
    per = count // ways
    own_filters, features, _ = filter_mats.shape
    length, wide = out_grad.shape
    half, width = features // 2, length // 4
    order, offsets = ring_of(count)
    right = [(order[i], order[(i + 1) % count]) for i in range(count)]
    left = [(b, a) for a, b in right]
    to = [(w, h) for w in range(1, ways) for h in range(2)] + [(0, 1), (0, 0)]
    plan = [(0, own_filters)] * len(to)

    def numbers(ctx, grp):
        way, here, at = grp // 2, grp % 2, order.index(ctx)
        cuts = []
        for w, h in to:
            cuts += [(here ^ h) * half, (way + w) % ways * 2 * wide]
        firsts = [(((way - w) % ways) * 2 + (here ^ h)) * (own_filters // 2) for w, h in to]
        turn = ctx % per_grp * 2 + here
        slots = [order[(at + o) % count] for o in offsets]
        use = [ways * ((r + turn) % per) + (way + w + ctx) % ways for w in range(ways) for r in range(per)]
        return [cuts, [here] + firsts, slots + use, [(ctx // ways - r) % per for r in range(per)]]

    row, begins, ends = my_row(count, groups, numbers)
    cuts, firsts, finish_info, lanes_info = [row[b:e] for b, e in zip(begins, ends)]
    swap = lambda x: shift_of(x, ways, 0, 1)
    mine, other = [out_grad], [swap(out_grad)]
    going_right, going_left = out_grad, out_grad
    for step in range(1, count // 2):
        going_right = lax.ppermute(going_right, "ctx", right)
        going_left = lax.ppermute(going_left, "ctx", left)
        mine += [going_right, going_left]
        other += [swap(going_right), swap(going_left)]
    mine.append(lax.ppermute(going_right, "ctx", right))
    other.append(swap(mine[-1]))
    pieces = plain_cut(filter_mats, cuts, plan, half, 2 * wide)
    mats = [shift_of(p, ways, w, h) for p, (w, h) in zip(pieces[:-1], to[:-1])] + pieces[-1:]
    gains = jnp.sqrt(-jnp.expm1(-2.0 * pole_rates))
    table = plain_tables(coeffs, pole_rates, gains, width)
    work = [(n, 0) for n in range(len(mats))]
    totals = [plain_add(firsts, [m], [o], mats, table, [None], work)[0] for m, o in zip(mine, other)]
    step_back = jnp.arange(width, dtype=f32) - width
    edge = gains[None, :] * jnp.exp(step_back[:, None] * pole_rates[None, :])
    decay = jnp.exp(-width * pole_rates)[:, None]
    partial = plain_finish(finish_info, totals, edge, decay, length)
    received = []
    for r in range(per):
        result = plain_combine([partial[r], *[shift_of(partial[w * per + r], ways, w, 0) for w in range(1, ways)]])
        pairs = []
        for c in range(count):
            for g in range(groups):
                m = (r + c % per_grp * 2 + g % 2) % per
                goal = ways * m + (g // 2 + c) % ways
                pairs.append((c * groups + g, goal * groups + c // per_grp))
        received.append(lax.ppermute(result, ("ctx", "grp"), pairs))
    return plain_arrange(lanes_info, received)


def spread(count, pairs, order, offsets):
    rand, best = random.Random(1), None

    def cost(flips):
        loads = {}
        for c in range(count):
            for r, pair in enumerate(pairs):
                for way in range(2):
                    goal = order[(order.index(c) + offsets[pair[way ^ flips[c][r]]]) % count]
                    lo, hi = sorted((c // 2, goal // 2))
                    keys = [(z, c % 2, way, goal > c) for z in range(lo, hi)]
                    if way != 2 * c // count:
                        keys.append((goal // 2, c % 2, way))
                    for key in keys:
                        loads[key] = loads.get(key, 0) + 1
        return max(loads.values()), sum(v * v for v in loads.values())

    for _ in range(20):
        flips = [[rand.randint(0, 1) for _ in pairs] for _ in range(count)]
        now, better = cost(flips), True
        while better:
            better = False
            for c in range(count):
                for r in range(len(pairs)):
                    flips[c][r] ^= 1
                    new = cost(flips)
                    if new < now:
                        now, better = new, True
                    else:
                        flips[c][r] ^= 1
        if best is None or now < best[0]:
            best = now, flips
    return best[1]


def final_rounds(count, groups):
    order, offsets = ring_of(count)
    if groups != 4 or count != 2 * groups:
        return None
    twos = [(s, s + 1) for s in range(1, count - 1, 2)] + [(0, count - 1)]
    pairs = twos[0::2] + twos[1::2]
    flips = spread(count, pairs, order, offsets)
    rounds = []
    for first in range(0, len(pairs), 2):
        for t in range(2):
            moves = []
            for c in range(count):
                for g in range(groups):
                    r = first + (t + g % 2) % 2
                    slot = pairs[r][g // 2 ^ flips[c][r]]
                    goal = order[(order.index(c) + offsets[slot]) % count]
                    moves.append((c * groups + g, goal * groups + c * groups // count))
            if len({b for _, b in moves}) != len(moves):
                return None
            rounds.append(moves)
    return pairs, flips, rounds


def per_device(out_grad, filter_mats, coeffs, pole_rates):
    count, groups = lax.axis_size("ctx"), lax.axis_size("grp")
    own_filters, features, _ = filter_mats.shape
    length, wide = out_grad.shape
    half, width = features // 2, length // 4
    tiled = half % 128 == 0 and wide % 128 == 0 and width % 128 == 0 and pole_rates.shape[0] % 16 == 0
    found = final_rounds(count, groups)
    if not tiled or own_filters % 2 or found is None:
        return plain_device(out_grad, filter_mats, coeffs, pole_rates)
    pairs, flips, rounds = found
    ways, per_grp = groups // 2, count // groups
    order, offsets = ring_of(count)
    right = [(order[i], order[(i + 1) % count]) for i in range(count)]
    left = [(b, a) for a, b in right]
    to = [(1, 0), (1, 1), (0, 1), (0, 0)]
    sources = [(0, 1), (0, 0), (1, 0), (1, 1)]

    def numbers(ctx, grp):
        way, here, at = grp // 2, grp % 2, order.index(ctx)
        firsts = [((way ^ w) * 2 + (here ^ h)) * (own_filters // 2) for w, h in sources]
        slots = [order[(at + o) % count] for o in offsets]
        second = [way ^ flip for flip in flips[ctx]]
        use = [slots[p[t]] for p, t in zip(pairs, second)] + [slots[p[1 - t]] for p, t in zip(pairs, second)]
        senders = [next(a for a, b in moves if b == ctx * groups + grp) for moves in rounds]
        lanes = [a // groups % per_grp * 2 + a % 2 for a in senders]
        return [[here], second, firsts, slots, use, lanes]

    row, (core_at, second_at, firsts_at, slots_at, use_at, lanes_at), _ = my_row(count, groups, numbers)
    swap = lambda x: shift_of(x, ways, 0, 1)
    together = lambda *x: lax.optimization_barrier(x)

    pieces = cut(filter_mats, to[:1], half, 2 * wide)
    gains = jnp.sqrt(-jnp.expm1(-2.0 * pole_rates))
    table = tables(coeffs, pole_rates, gains, width)
    mats = [None, None, shift_of(pieces[0], ways, *to[0])]
    going_right, going_left = out_grad, out_grad
    mine, other, totals = [out_grad], [swap(out_grad)], [None] * count
    back = lambda n: gains[None, :] * jnp.exp((jnp.arange(n, dtype=f32) - n)[:, None] * pole_rates[None, :])
    ahead = lambda n: jnp.exp(-n * pole_rates)[:, None]
    ends, far_ends = (back(width), ahead(width)), (back(length), ahead(length))

    def run(slots, use, closing=None):
        chosen = sorted({n for s in slots for n in use[s]})
        info_at = [core_at] + [firsts_at + n for n in chosen]
        work = [(chosen.index(n), b) for n in chosen for b, s in enumerate(slots) if n in use[s]]
        got = add_blocks(
            row, info_at, [mine[s] for s in slots], [other[s] for s in slots], [mats[n] for n in chosen], table,
            [totals[s] for s in slots], work, *(() if closing is None else (ends, second_at + closing)),
        )
        if closing is not None:
            return got
        for s, t in zip(slots, got):
            totals[s] = t

    for step in range(1, count // 2 + 1):
        arrived = [0] if step == 1 else [2 * step - 3, 2 * step - 2]
        if step > 1:
            other += [swap(mine[s]) for s in arrived]
        if step < count // 2:
            coming = [lax.ppermute(going_right, "ctx", right), lax.ppermute(going_left, "ctx", left)]
        else:
            coming = [
                lax.ppermute(going_right[: length // 2], "ctx", right),
                lax.ppermute(going_left[length // 2 :], "ctx", left),
            ]
        if step == 3:
            piece, mats[2] = together(pieces[1], mats[2])
            mats.append(shift_of(piece, ways, *to[1]))
        if step == 2:
            pieces += cut(filter_mats, to[1:], half, 2 * wide)
            mats[:2] = [swap(pieces[2]), pieces[3]]
        elif step > 2:
            slots = ([0] if step == 3 else []) + [2 * step - 5, 2 * step - 4]
            run(slots, {s: [0, 1, 2] for s in slots})
        done = [s for s in range(count) if totals[s] is not None]
        coming, swapped, table, sums, early, filter_mats = together(
            coming, other[-len(arrived) :], table, [totals[s] for s in done], mats[:3] if step > 1 else [], filter_mats
        )
        other[-len(arrived) :] = swapped
        mats[: len(early)] = early
        for s, t in zip(done, sums):
            totals[s] = t
        if step < count // 2:
            going_right, going_left = coming
            mine += coming
        else:
            mine.append(jnp.concatenate(coming))
    other.append(swap(mine[-1]))

    kept, sent, states = [None] * len(pairs), [None] * len(pairs), [None] * count
    for pair in [*sorted(pairs)[1:], sorted(pairs)[0]]:
        use = {s: [n for n in range(4) if totals[s] is None or n == 3] for s in pair}
        keep, send, *state = run(list(pair), use, pairs.index(pair))
        for s, st in zip(pair, state):
            states[s] = st
        kept[pairs.index(pair)], sent[pairs.index(pair)] = keep, send
    carry_kept, carry_sent = carry(row, slots_at, use_at, states, far_ends[1])
    sent[-1], carry_sent = together(sent[-1], carry_sent)
    carries = [carry_kept, shift_of(carry_sent, ways, 1, 0)]
    arrived = [shift_of(x, ways, 1, 0) for x in sent]
    received = []
    for first in range(0, len(pairs), 2):
        both = [first, first + 1]
        got = results(row, core_at, both, [kept[r] for r in both], [arrived[r] for r in both], carries, far_ends[0])
        received += [lax.ppermute(v, ("ctx", "grp"), moves) for v, moves in zip(got, rounds[first : first + 2])]
    return arrange(row, lanes_at, received)


def solution(mesh):
    placed = (P("ctx", "grp"), P("grp", "ctx", None), P(), P())
    return jax.shard_map(
        per_device, mesh=mesh, in_specs=placed, out_specs=P("ctx", "grp"), check_vma=False
    )
```

time: 129 us -> 121 us (0.938)
  the two profiles are of different devices: /device:TPU:9 before, /device:TPU:4 now
where the time goes in v3:
time: 121 us; the launch traced here: 120 us
  Pallas kernels  49.6 us (41%)
  waiting for transfers between devices  36.8 us (30%)
  starting transfers between devices  27.3 us (23%)
  local copies, waits for them, and re-layouts  6.02 us (5%)
    pallas_call x6, Pallas kernels, add_blocks(): pl.pallas_call(functools.partial(blocks_kernel, blocks, sets, work, info_...  38 us
    ppermute x3, waiting for transfers between devices, per_device(): lax.ppermute(going_right, 'ctx', right)  13.1 us
    ppermute x4, starting transfers between devices, per_device(): lax.ppermute(v, ('ctx', 'grp'), moves)  11.9 us
    ppermute x16, waiting for transfers between devices, shift_of(): lax.ppermute(x, 'grp', [(rank(w, h), rank(w + by_way, h ^ by_core)) for w...  10.1 us
    ppermute x16, starting transfers between devices, shift_of(): lax.ppermute(x, 'grp', [(rank(w, h), rank(w + by_way, h ^ by_core)) for w...  7.29 us
    ppermute x3, waiting for transfers between devices, per_device(): lax.ppermute(going_left, 'ctx', left)  7.25 us
    pallas_call x2, Pallas kernels, cut(): pl.pallas_call(functools.partial(cut_kernel, to), in_specs=[ANY], out_spe...  5.77 us
    ppermute x4, waiting for transfers between devices, per_device(): lax.ppermute(v, ('ctx', 'grp'), moves)  5.56 us
  transfers between devices with their start and end apart: 28, of which 9 were waited for; matrix products, arithmetic and copies ran while one was open for 1% of the time, Pallas kernels for 37%

profile of v3, /device:TPU:4, one launch (start us, length us, event | category | flops | bytes accessed | tf_op | source)
XLA Modules:
  0.0 120.3 jit_solution(8070280629551226964)
XLA Ops:
  0.0 1.6 %collective-permute-start = (bf16[512,512]{1,0:T(8,128)(2,1)}, bf16[512,512]{1,0:T(8,128)(2,1)}, u32[]{:S(2)}, u32[]{:S(2)}) collective-permute-start(bf16[512,512]{1,0:T(8,128)(2,1)} %refs_0_.3), channel_id=1, source_target_pairs={{0,8},{8,16},{16,24},{24,28},{28,20},{20,12},{12,4},{4,0},{1,9},{9... | collective-permute-start | bytes 1572872 | tf_op jit(solution)/shard_map/ppermute | solution.py:525
  2.0 2.2 %cut_filters.3 = bf16[4,128,1024]{2,1,0:T(8,128)(2,1)} custom-call(bf16[4,256,2048]{2,1,0:T(8,128)(2,1)} %mats.2), custom_call_target="tpu_custom_call" | custom-call | tf_op jit(solution)/shard_map/cut_filters/pallas_call | solution.py:83
  4.5 1.9 %pole_tables.1.refs_9_.refs_7_.refs_5_.refs_8_ = bf16[8,208,512]{2,1,0:T(8,128)(2,1)S(1)} custom-call(f32[80,18]{1,0:T(8,128)S(1)} %copy.14.poles_ref), custom_call_target="tpu_custom_call" | custom-call | flops 4000000000 | tf_op jit(solution)/shard_map/pole_tables/pallas_call | solution.py:55
  7.6 6.3 %collective-permute-done.refs_1_.refs_0_ = bf16[512,512]{1,0:T(8,128)(2,1)} collective-permute-done((bf16[512,512]{1,0:T(8,128)(2,1)}, bf16[512,512]{1,0:T(8,128)(2,1)}, u32[]{:S(2)}, u32[]{:S(2)}) %collective-permute-start) | collective-permute-done | bytes 524320 | tf_op jit(solution)/shard_map/ppermute | solution.py:525
  15.2 1.6 %collective-permute-start.3 = (bf16[512,512]{1,0:T(8,128)(2,1)}, bf16[512,512]{1,0:T(8,128)(2,1)}, u32[]{:S(2)}, u32[]{:S(2)}) collective-permute-start(bf16[512,512]{1,0:T(8,128)(2,1)} %collective-permute-done.refs_1_.refs_0_), channel_id=1, source_target_pairs={{0,8},{8,16},{16,24},{24,28},{28,20},{20,12},{12,4},{4,0},{1,9},{9... | collective-permute-start | bytes 1572872 | tf_op jit(solution)/shard_map/ppermute | solution.py:525
  16.8 3.6 %cut_filters.2 = (bf16[4,128,1024]{2,1,0:T(8,128)(2,1)}, bf16[4,128,1024]{2,1,0:T(8,128)(2,1)}, bf16[4,128,1024]{2,1,0:T(8,128)(2,1)}) custom-call(bf16[4,256,2048]{2,1,0:T(8,128)(2,1)} %mats.2), custom_call_target="tpu_custom_call" | custom-call | tf_op jit(solution)/shard_map/cut_filters/pallas_call | solution.py:83
  21.4 6.7 %collective-permute-done.3.refs_0_ = bf16[512,512]{1,0:T(8,128)(2,1)} collective-permute-done((bf16[512,512]{1,0:T(8,128)(2,1)}, bf16[512,512]{1,0:T(8,128)(2,1)}, u32[]{:S(2)}, u32[]{:S(2)}) %collective-permute-start.3) | collective-permute-done | bytes 524320 | tf_op jit(solution)/shard_map/ppermute | solution.py:525
  29.1 6.1 %collective-permute-done.4.refs_1_ = bf16[512,512]{1,0:T(8,128)(2,1)} collective-permute-done((bf16[512,512]{1,0:T(8,128)(2,1)}, bf16[512,512]{1,0:T(8,128)(2,1)}, u32[]{:S(2)}, u32[]{:S(2)}) %collective-permute-start.4) | collective-permute-done | bytes 524320 | tf_op jit(solution)/shard_map/ppermute | solution.py:525
  35.2 1.6 %collective-permute-start.10 = (bf16[512,512]{1,0:T(8,128)(2,1)}, bf16[512,512]{1,0:T(8,128)(2,1)S(1)}, u32[]{:S(2)}, u32[]{:S(2)}) collective-permute-start(bf16[512,512]{1,0:T(8,128)(2,1)} %collective-permute-done.3.refs_0_), channel_id=1, source_target_pairs={{0,8},{8,16},{16,24},{24,28},{28,20},{20,12},{12,4},{4,0},{1,9},{9... | collective-permute-start | bytes 1572872 | tf_op jit(solution)/shard_map/ppermute | solution.py:525
  40.1 1.5 %copy-done.7 = bf16[8,208,512]{2,1,0:T(8,128)(2,1)S(1)} copy-done((bf16[8,208,512]{2,1,0:T(8,128)(2,1)S(1)}, bf16[8,208,512]{2,1,0:T(8,128)(2,1)}, u32[]{:S(2)}) %copy-start.7) | copy-done | bytes 1703960
  41.6 10.0 %add_blocks.2 = (f32[208,512]{1,0:T(8,128)S(1)}, f32[208,512]{1,0:T(8,128)S(1)}, f32[208,512]{1,0:T(8,128)S(1)}) custom-call(s32[29]{0:T(128)S(1)} %dynamic-slice_bitcast_fusion.info, bf16[512,512]{1,0:T(8,128)(2,1)S(1)} %copy-done.2, bf16[512,512]{1,0:T(8,128)(2,1)} %collective-permute-done.refs_1_.refs_0_, bf16[512,512]{1,0:T(8,128)(2,1)S(1)} %copy-done.4, ...), custom_call_target="tpu_custom_call" | custom-call | flops 10800000000 | tf_op jit(solution)/shard_map/add_blocks/pallas_call | solution.py:181
  52.3 1.6 %collective-permute-start.14 = (bf16[256,512]{1,0:T(8,128)(2,1)S(1)}, bf16[256,512]{1,0:T(8,128)(2,1)S(1)}, u32[]{:S(2)}, u32[]{:S(2)}) collective-permute-start(bf16[256,512]{1,0:T(8,128)(2,1)S(1)} %slice.6), channel_id=1, source_target_pairs={{0,8},{8,16},{16,24},{24,28},{28,20},{20,12},{12,4},{4,0},{1,9},{9... | collective-permute-start | bytes 786440 | tf_op jit(solution)/shard_map/ppermute | solution.py:528
  54.4 6.9 %add_blocks.3 = (f32[208,512]{1,0:T(8,128)S(1)}, f32[208,512]{1,0:T(8,128)S(1)}) custom-call(s32[29]{0:T(128)S(1)} %dynamic-slice_bitcast_fusion.info, bf16[512,512]{1,0:T(8,128)(2,1)} %collective-permute-done.3.refs_0_, bf16[512,512]{1,0:T(8,128)(2,1)} %collective-permute-done.4.refs_1_, bf16[512,512]{1,0:T(8,128)(2,1)S(1)} %collective-permute-done.12.refs_2_, ...), custom_call_target="tpu_custom_call" | custom-call | flops 7200000000 | tf_op jit(solution)/shard_map/add_blocks/pallas_call | solution.py:181
  62.8 3.6 %close_blocks.4 = (f32[512,128]{1,0:T(8,128)S(1)}, f32[512,128]{1,0:T(8,128)S(1)}, f32[80,128]{1,0:T(8,128)S(1)}, f32[80,128]{1,0:T(8,128)S(1)}) custom-call(s32[29]{0:T(128)S(1)} %dynamic-slice_bitcast_fusion.info, bf16[512,512]{1,0:T(8,128)(2,1)} %collective-permute-done.refs_1_.refs_0_, bf16[512,512]{1,0:T(8,128)(2,1)S(1)} %copy-done.5, ...), custom_call_target="tpu_custom_call" | custom-call | flops 2400000000 | tf_op jit(solution)/shard_map/close_blocks/pallas_call | solution.py:181
  67.5 8.3 %close_blocks.5 = (f32[512,128]{1,0:T(8,128)S(1)}, f32[512,128]{1,0:T(8,128)S(1)}, f32[80,128]{1,0:T(8,128)S(1)}, f32[80,128]{1,0:T(8,128)S(1)}) custom-call(s32[29]{0:T(128)S(1)} %dynamic-slice_bitcast_fusion.info, bf16[512,512]{1,0:T(8,128)(2,1)S(1)} %collective-permute-done.10.refs_0_, bf16[512,512]{1,0:T(8,128)(2,1)S(1)} %collective-permute-done.11.refs_1_, ...), custom_call_target="tpu_custom_call" | custom-call | flops 9600000000 | tf_op jit(solution)/shard_map/close_blocks/pallas_call | solution.py:181
  77.0 3.7 %close_blocks.7 = (f32[512,128]{1,0:T(8,128)S(1)}, f32[512,128]{1,0:T(8,128)S(1)}, f32[80,128]{1,0:T(8,128)S(1)}, f32[80,128]{1,0:T(8,128)S(1)}) custom-call(s32[29]{0:T(128)S(1)} %dynamic-slice_bitcast_fusion.info, bf16[512,512]{1,0:T(8,128)(2,1)} %collective-permute-done.3.refs_0_, bf16[512,512]{1,0:T(8,128)(2,1)} %collective-permute-done.4.refs_1_, ...), custom_call_target="tpu_custom_call" | custom-call | flops 2400000000 | tf_op jit(solution)/shard_map/close_blocks/pallas_call | solution.py:181
  81.7 5.5 %close_blocks.6 = (f32[512,128]{1,0:T(8,128)S(1)}, f32[512,128]{1,0:T(8,128)S(1)}, f32[80,128]{1,0:T(8,128)S(1)}, f32[80,128]{1,0:T(8,128)S(1)}) custom-call(s32[29]{0:T(128)S(1)} %dynamic-slice_bitcast_fusion.info, bf16[512,512]{1,0:T(8,128)(2,1)S(1)} %copy-done.2, bf16[512,512]{1,0:T(8,128)(2,1)S(1)} %constant_dynamic-update-slice_fusion.refs_1_, ...), custom_call_target="tpu_custom_call" | custom-call | flops 6000000000 | tf_op jit(solution)/shard_map/close_blocks/pallas_call | solution.py:181
  90.2 9.4 %collective-permute-done.21.refs_5_ = f32[4,80,128]{2,1,0:T(8,128)S(1)} collective-permute-done((f32[4,80,128]{2,1,0:T(8,128)S(1)}, f32[4,80,128]{2,1,0:T(8,128)S(1)}, u32[]{:S(2)}, u32[]{:S(2)}) %collective-permute-start.21) | collective-permute-done | bytes 163872 | tf_op jit(solution)/shard_map/ppermute | solution.py:337
  101.5 2.0 %collective-permute-start.23 = (bf16[512,128]{1,0:T(8,128)(2,1)S(1)}, bf16[512,128]{1,0:T(8,128)(2,1)S(1)}, u32[]{:S(2)}, u32[]{:S(2)}) collective-permute-start(bf16[512,128]{1,0:T(8,128)(2,1)S(1)} %get-tuple-element.140), channel_id=1, source_target_pairs={{0,20},{1,8},{2,24},{3,4},{4,16},{5,12},{6,28},{7,0},{8,29},{9,1},... | collective-permute-start | bytes 393224 | tf_op jit(solution)/shard_map/ppermute | solution.py:570
  104.5 2.3 %collective-permute-start.26 = (bf16[512,128]{1,0:T(8,128)(2,1)S(1)}, bf16[512,128]{1,0:T(8,128)(2,1)S(1)}, u32[]{:S(2)}, u32[]{:S(2)}) collective-permute-start(bf16[512,128]{1,0:T(8,128)(2,1)S(1)} %get-tuple-element.145), channel_id=1, source_target_pairs={{0,12},{1,0},{2,16},{3,28},{4,8},{5,4},{6,20},{7,24},{8,25},{9,21}... | collective-permute-start | bytes 393224 | tf_op jit(solution)/shard_map/ppermute | solution.py:570
  106.8 6.5 %collective-permute-start.27 = (bf16[512,128]{1,0:T(8,128)(2,1)S(1)}, bf16[512,128]{1,0:T(8,128)(2,1)S(1)}, u32[]{:S(2)}, u32[]{:S(2)}) collective-permute-start(bf16[512,128]{1,0:T(8,128)(2,1)S(1)} %get-tuple-element.146), channel_id=1, source_target_pairs={{0,0},{1,12},{2,28},{3,16},{4,4},{5,8},{6,24},{7,20},{8,21},{9,25}... | collective-permute-start | bytes 393224 | tf_op jit(solution)/shard_map/ppermute | solution.py:570
  113.3 3.5 %collective-permute-done.26.refs_2_ = bf16[512,128]{1,0:T(8,128)(2,1)S(1)} collective-permute-done((bf16[512,128]{1,0:T(8,128)(2,1)S(1)}, bf16[512,128]{1,0:T(8,128)(2,1)S(1)}, u32[]{:S(2)}, u32[]{:S(2)}) %collective-permute-start.26) | collective-permute-done | bytes 131104 | tf_op jit(solution)/shard_map/ppermute | solution.py:570
  116.8 2.1 %collective-permute-done.27.refs_3_ = bf16[512,128]{1,0:T(8,128)(2,1)S(1)} collective-permute-done((bf16[512,128]{1,0:T(8,128)(2,1)S(1)}, bf16[512,128]{1,0:T(8,128)(2,1)S(1)}, u32[]{:S(2)}, u32[]{:S(2)}) %collective-permute-start.27) | collective-permute-done | bytes 131104 | tf_op jit(solution)/shard_map/ppermute | solution.py:570
  118.9 1.4 %arrange_features.1 = bf16[512,512]{1,0:T(8,128)(2,1)} custom-call(s32[29]{0:T(128)S(1)} %dynamic-slice_bitcast_fusion.info, bf16[512,128]{1,0:T(8,128)(2,1)S(1)} %collective-permute-done.22.refs_0_, bf16[512,128]{1,0:T(8,128)(2,1)S(1)} %collective-permute-done.23.refs_1_, bf16[512,128]{1,0:T(8,128)(2,1)S(1)} %collective-permute-done.26.refs_2_, ...), custom_call_target="tpu_custom_call" | custom-call | tf_op jit(solution)/shard_map/arrange_features/pallas_call | solution.py:256
  (81 shorter events, 20.1 us)
Async XLA Ops:
  0.0 14.0 %collective-permute-start = (bf16[512,512]{1,0:T(8,128)(2,1)}, bf16[512,512]{1,0:T(8,128)(2,1)}, u32[]{:S(2)}, u32[]{:S(2)}) collective-permute-start(bf16[512,512]{1,0:T(8,128)(2,1)} %refs_0_.3), channel_id=1, source_target_pairs={{0,8},{8,16},{16,24},{24,28},{28,20},{20,12},{12,4},{4,0},{1,9},{9... | collective-permute-start | bytes 1572872 | tf_op jit(solution)/shard_map/ppermute | solution.py:525
  1.6 13.6 %collective-permute-start.1 = (bf16[512,512]{1,0:T(8,128)(2,1)}, bf16[512,512]{1,0:T(8,128)(2,1)S(1)}, u32[]{:S(2)}, u32[]{:S(2)}) collective-permute-start(bf16[512,512]{1,0:T(8,128)(2,1)} %refs_0_.3), channel_id=1, source_target_pairs={{8,0},{16,8},{24,16},{28,24},{20,28},{12,20},{4,12},{0,4},{9,1},{1... | collective-permute-start | bytes 1572872 | tf_op jit(solution)/shard_map/ppermute | solution.py:525
  2.0 13.1 %collective-permute-start.2 = (bf16[512,512]{1,0:T(8,128)(2,1)}, bf16[512,512]{1,0:T(8,128)(2,1)S(1)}, u32[]{:S(2)}, u32[]{:S(2)}) collective-permute-start(bf16[512,512]{1,0:T(8,128)(2,1)} %refs_0_.3), channel_id=1, source_target_pairs={{0,1},{1,0},{2,3},{3,2},{4,5},{5,4},{6,7},{7,6},{8,9},{9,8},{10,11... | collective-permute-start | bytes 1572872 | tf_op jit(solution)/shard_map/ppermute | solution.py:337
  4.2 30.9 %collective-permute-start.8 = (bf16[4,128,1024]{2,1,0:T(8,128)(2,1)}, bf16[4,128,1024]{2,1,0:T(8,128)(2,1)S(1)}, u32[]{:S(2)}, u32[]{:S(2)}) collective-permute-start(bf16[4,128,1024]{2,1,0:T(8,128)(2,1)} %cut_filters.3), channel_id=1, source_target_pairs={{0,2},{1,3},{2,0},{3,1},{4,6},{5,7},{6,4},{7,5},{8,10},{9,11},{10,... | collective-permute-start | bytes 3145736 | tf_op jit(solution)/shard_map/ppermute | solution.py:337
  15.2 12.9 %collective-permute-start.3 = (bf16[512,512]{1,0:T(8,128)(2,1)}, bf16[512,512]{1,0:T(8,128)(2,1)}, u32[]{:S(2)}, u32[]{:S(2)}) collective-permute-start(bf16[512,512]{1,0:T(8,128)(2,1)} %collective-permute-done.refs_1_.refs_0_), channel_id=1, source_target_pairs={{0,8},{8,16},{16,24},{24,28},{28,20},{20,12},{12,4},{4,0},{1,9},{9... | collective-permute-start | bytes 1572872 | tf_op jit(solution)/shard_map/ppermute | solution.py:525
  20.3 14.8 %collective-permute-start.7 = (bf16[4,128,1024]{2,1,0:T(8,128)(2,1)}, bf16[4,128,1024]{2,1,0:T(8,128)(2,1)S(1)}, u32[]{:S(2)}, u32[]{:S(2)}) collective-permute-start(bf16[4,128,1024]{2,1,0:T(8,128)(2,1)} %get-tuple-element.80), channel_id=1, source_target_pairs={{0,1},{1,0},{2,3},{3,2},{4,5},{5,4},{6,7},{7,6},{8,9},{9,8},{10,11... | collective-permute-start | bytes 3145736 | tf_op jit(solution)/shard_map/ppermute | solution.py:337
  20.4 14.7 %collective-permute-start.5 = (bf16[512,512]{1,0:T(8,128)(2,1)}, bf16[512,512]{1,0:T(8,128)(2,1)}, u32[]{:S(2)}, u32[]{:S(2)}) collective-permute-start(bf16[512,512]{1,0:T(8,128)(2,1)} %collective-permute-done.refs_1_.refs_0_), channel_id=1, source_target_pairs={{0,1},{1,0},{2,3},{3,2},{4,5},{5,4},{6,7},{7,6},{8,9},{9,8},{10,11... | collective-permute-start | bytes 1572872 | tf_op jit(solution)/shard_map/ppermute | solution.py:337
  20.9 14.2 %collective-permute-start.4 = (bf16[512,512]{1,0:T(8,128)(2,1)}, bf16[512,512]{1,0:T(8,128)(2,1)}, u32[]{:S(2)}, u32[]{:S(2)}) collective-permute-start(bf16[512,512]{1,0:T(8,128)(2,1)} %copy-done.3), channel_id=1, source_target_pairs={{8,0},{16,8},{24,16},{28,24},{20,28},{12,20},{4,12},{0,4},{9,1},{1... | collective-permute-start | bytes 1572872 | tf_op jit(solution)/shard_map/ppermute | solution.py:525
  35.2 16.4 %collective-permute-start.10 = (bf16[512,512]{1,0:T(8,128)(2,1)}, bf16[512,512]{1,0:T(8,128)(2,1)S(1)}, u32[]{:S(2)}, u32[]{:S(2)}) collective-permute-start(bf16[512,512]{1,0:T(8,128)(2,1)} %collective-permute-done.3.refs_0_), channel_id=1, source_target_pairs={{0,8},{8,16},{16,24},{24,28},{28,20},{20,12},{12,4},{4,0},{1,9},{9... | collective-permute-start | bytes 1572872 | tf_op jit(solution)/shard_map/ppermute | solution.py:525
  36.8 14.8 %collective-permute-start.12 = (bf16[512,512]{1,0:T(8,128)(2,1)}, bf16[512,512]{1,0:T(8,128)(2,1)S(1)}, u32[]{:S(2)}, u32[]{:S(2)}) collective-permute-start(bf16[512,512]{1,0:T(8,128)(2,1)} %collective-permute-done.3.refs_0_), channel_id=1, source_target_pairs={{0,1},{1,0},{2,3},{3,2},{4,5},{5,4},{6,7},{7,6},{8,9},{9,8},{10,11... | collective-permute-start | bytes 1572872 | tf_op jit(solution)/shard_map/ppermute | solution.py:337
  36.8 14.8 %collective-permute-start.11 = (bf16[512,512]{1,0:T(8,128)(2,1)}, bf16[512,512]{1,0:T(8,128)(2,1)S(1)}, u32[]{:S(2)}, u32[]{:S(2)}) collective-permute-start(bf16[512,512]{1,0:T(8,128)(2,1)} %collective-permute-done.4.refs_1_), channel_id=1, source_target_pairs={{8,0},{16,8},{24,16},{28,24},{20,28},{12,20},{4,12},{0,4},{9,1},{1... | collective-permute-start | bytes 1572872 | tf_op jit(solution)/shard_map/ppermute | solution.py:525
  37.2 14.4 %collective-permute-start.13 = (bf16[512,512]{1,0:T(8,128)(2,1)}, bf16[512,512]{1,0:T(8,128)(2,1)S(1)}, u32[]{:S(2)}, u32[]{:S(2)}) collective-permute-start(bf16[512,512]{1,0:T(8,128)(2,1)} %collective-permute-done.4.refs_1_), channel_id=1, source_target_pairs={{0,1},{1,0},{2,3},{3,2},{4,5},{5,4},{6,7},{7,6},{8,9},{9,8},{10,11... | collective-permute-start | bytes 1572872 | tf_op jit(solution)/shard_map/ppermute | solution.py:337
  37.5 25.3 %collective-permute-start.9 = (bf16[4,128,1024]{2,1,0:T(8,128)(2,1)}, bf16[4,128,1024]{2,1,0:T(8,128)(2,1)S(1)}, u32[]{:S(2)}, u32[]{:S(2)}) collective-permute-start(bf16[4,128,1024]{2,1,0:T(8,128)(2,1)} %get-tuple-element.86), channel_id=1, source_target_pairs={{0,3},{1,2},{2,1},{3,0},{4,7},{5,6},{6,5},{7,4},{8,11},{9,10},{10,... | collective-permute-start | bytes 3145736 | tf_op jit(solution)/shard_map/ppermute | solution.py:337
  51.7 10.4 %collective-permute-start.16 = (bf16[512,512]{1,0:T(8,128)(2,1)S(1)}, bf16[512,512]{1,0:T(8,128)(2,1)S(1)}, u32[]{:S(2)}, u32[]{:S(2)}) collective-permute-start(bf16[512,512]{1,0:T(8,128)(2,1)S(1)} %collective-permute-done.10.refs_0_), channel_id=1, source_target_pairs={{0,1},{1,0},{2,3},{3,2},{4,5},{5,4},{6,7},{7,6},{8,9},{9,8},{10,11... | collective-permute-start | bytes 1572872 | tf_op jit(solution)/shard_map/ppermute | solution.py:337
  66.4 23.8 %collective-permute-start.18 = (f32[512,128]{1,0:T(8,128)S(1)}, f32[512,128]{1,0:T(8,128)S(1)}, u32[]{:S(2)}, u32[]{:S(2)}) collective-permute-start(f32[512,128]{1,0:T(8,128)S(1)} %get-tuple-element.120), channel_id=1, source_target_pairs={{0,2},{1,3},{2,0},{3,1},{4,6},{5,7},{6,4},{7,5},{8,10},{9,11},{10,... | collective-permute-start | bytes 786440 | tf_op jit(solution)/shard_map/ppermute | solution.py:337
  67.5 14.2 %collective-permute-start.20 = (bf16[512,512]{1,0:T(8,128)(2,1)S(1)}, bf16[512,512]{1,0:T(8,128)(2,1)S(1)}, u32[]{:S(2)}, u32[]{:S(2)}) collective-permute-start(bf16[512,512]{1,0:T(8,128)(2,1)S(1)} %constant_dynamic-update-slice_fusion.refs_1_), channel_id=1, source_target_pairs={{0,1},{1,0},{2,3},{3,2},{4,5},{5,4},{6,7},{7,6},{8,9},{9,8},{10,11... | collective-permute-start | bytes 1572872 | tf_op jit(solution)/shard_map/ppermute | solution.py:337
  75.8 14.4 %collective-permute-start.19 = (f32[512,128]{1,0:T(8,128)S(1)}, f32[512,128]{1,0:T(8,128)S(1)}, u32[]{:S(2)}, u32[]{:S(2)}) collective-permute-start(f32[512,128]{1,0:T(8,128)S(1)} %get-tuple-element.121), channel_id=1, source_target_pairs={{0,2},{1,3},{2,0},{3,1},{4,6},{5,7},{6,4},{7,5},{8,10},{9,11},{10,... | collective-permute-start | bytes 786440 | tf_op jit(solution)/shard_map/ppermute | solution.py:337
  80.7 22.9 %collective-permute-start.24 = (f32[512,128]{1,0:T(8,128)S(1)}, f32[512,128]{1,0:T(8,128)S(1)}, u32[]{:S(2)}, u32[]{:S(2)}) collective-permute-start(f32[512,128]{1,0:T(8,128)S(1)} %get-tuple-element.143), channel_id=1, source_target_pairs={{0,2},{1,3},{2,0},{3,1},{4,6},{5,7},{6,4},{7,5},{8,10},{9,11},{10,... | collective-permute-start | bytes 786440 | tf_op jit(solution)/shard_map/ppermute | solution.py:337
  87.9 15.6 %collective-permute-start.25 = (f32[512,128]{1,0:T(8,128)S(1)}, f32[512,128]{1,0:T(8,128)S(1)}, u32[]{:S(2)}, u32[]{:S(2)}) collective-permute-start(f32[512,128]{1,0:T(8,128)S(1)} %get-tuple-element.144), channel_id=1, source_target_pairs={{0,2},{1,3},{2,0},{3,1},{4,6},{5,7},{6,4},{7,5},{8,10},{9,11},{10,... | collective-permute-start | bytes 786440 | tf_op jit(solution)/shard_map/ppermute | solution.py:337
  89.1 10.5 %collective-permute-start.21 = (f32[4,80,128]{2,1,0:T(8,128)S(1)}, f32[4,80,128]{2,1,0:T(8,128)S(1)}, u32[]{:S(2)}, u32[]{:S(2)}) collective-permute-start(f32[4,80,128]{2,1,0:T(8,128)S(1)} %get-tuple-element.138), channel_id=1, source_target_pairs={{0,2},{1,3},{2,0},{3,1},{4,6},{5,7},{6,4},{7,5},{8,10},{9,11},{10,... | collective-permute-start | bytes 491528 | tf_op jit(solution)/shard_map/ppermute | solution.py:337
  100.5 12.8 %collective-permute-start.22 = (bf16[512,128]{1,0:T(8,128)(2,1)S(1)}, bf16[512,128]{1,0:T(8,128)(2,1)S(1)}, u32[]{:S(2)}, u32[]{:S(2)}) collective-permute-start(bf16[512,128]{1,0:T(8,128)(2,1)S(1)} %get-tuple-element.139), channel_id=1, source_target_pairs={{0,8},{1,20},{2,4},{3,24},{4,12},{5,16},{6,0},{7,28},{8,1},{9,29},... | collective-permute-start | bytes 393224 | tf_op jit(solution)/shard_map/ppermute | solution.py:570
  101.5 11.8 %collective-permute-start.23 = (bf16[512,128]{1,0:T(8,128)(2,1)S(1)}, bf16[512,128]{1,0:T(8,128)(2,1)S(1)}, u32[]{:S(2)}, u32[]{:S(2)}) collective-permute-start(bf16[512,128]{1,0:T(8,128)(2,1)S(1)} %get-tuple-element.140), channel_id=1, source_target_pairs={{0,20},{1,8},{2,24},{3,4},{4,16},{5,12},{6,28},{7,0},{8,29},{9,1},... | collective-permute-start | bytes 393224 | tf_op jit(solution)/shard_map/ppermute | solution.py:570
  104.5 12.4 %collective-permute-start.26 = (bf16[512,128]{1,0:T(8,128)(2,1)S(1)}, bf16[512,128]{1,0:T(8,128)(2,1)S(1)}, u32[]{:S(2)}, u32[]{:S(2)}) collective-permute-start(bf16[512,128]{1,0:T(8,128)(2,1)S(1)} %get-tuple-element.145), channel_id=1, source_target_pairs={{0,12},{1,0},{2,16},{3,28},{4,8},{5,4},{6,20},{7,24},{8,25},{9,21}... | collective-permute-start | bytes 393224 | tf_op jit(solution)/shard_map/ppermute | solution.py:570
  106.8 12.1 %collective-permute-start.27 = (bf16[512,128]{1,0:T(8,128)(2,1)S(1)}, bf16[512,128]{1,0:T(8,128)(2,1)S(1)}, u32[]{:S(2)}, u32[]{:S(2)}) collective-permute-start(bf16[512,128]{1,0:T(8,128)(2,1)S(1)} %get-tuple-element.146), channel_id=1, source_target_pairs={{0,0},{1,12},{2,28},{3,16},{4,4},{5,8},{6,24},{7,20},{8,21},{9,25}... | collective-permute-start | bytes 393224 | tf_op jit(solution)/shard_map/ppermute | solution.py:570
  (15 other events, 110.4 us)

commit v4 on v3

--- a/solution.py
+++ b/solution.py
@@ -67,11 +67,11 @@
     outs, sems = refs[:-1], refs[-1]
     way, here = lax.axis_index("grp") // 2, lax.axis_index("grp") % 2
     copies = []
-    for i, (by_way, by_core) in enumerate(to):
+    for i, (by_way, by_core, lo, n) in enumerate(to):
         _, half, cols = outs[i].shape
         row = (1 - here if by_core else here) * half
         col = (1 - way if by_way else way) * cols
-        src = mats.at[:, pl.ds(pl.multiple_of(row, half), half), pl.ds(pl.multiple_of(col, cols), cols)]
+        src = mats.at[pl.ds(lo, n), pl.ds(pl.multiple_of(row, half), half), pl.ds(pl.multiple_of(col, cols), cols)]
         copies.append(pltpu.make_async_copy(src, outs[i], sems.at[i]))
     for c in copies:
         c.start()
@@ -84,7 +84,7 @@
         functools.partial(cut_kernel, to),
         in_specs=[ANY],
         out_specs=[VM] * len(to),
-        out_shape=[jax.ShapeDtypeStruct((mats.shape[0], half, cols), bf16)] * len(to),
+        out_shape=[jax.ShapeDtypeStruct((n, half, cols), bf16) for *_, n in to],
         scratch_shapes=[pltpu.SemaphoreType.DMA((len(to),))],
         compiler_params=params(60),
         name="cut_filters",
@@ -97,7 +97,7 @@
     width = table.shape[2] // 4
     half = mats[0].shape[1]
     subs = mine[0].shape[0] // width
-    units = [(i, n, b) for i in range(mats[0].shape[0] // 2) for n, b in work]
+    units = [(i, n, b) for n, b in work for i in range(mats[n].shape[0] // 2)]
     for u, (i, n, b) in enumerate(units):
         two = mats[n].at[pl.ds(2 * i, 2)]
         m_mine = two[:, :, pl.ds(pl.multiple_of(here * wide, wide), wide)].reshape(2 * half, wide)
@@ -125,7 +125,7 @@
             begun.add(b)
 
 
-def blocks_kernel(blocks, sets, work, info_at, fresh, closing, info, *refs):
+def blocks_kernel(blocks, sets, work, info_at, fresh, closing, splits, info, *refs):
     refs = list(refs)
     take = lambda n: [refs.pop(0) for _ in range(n)]
     mine, other, mats, (table,) = take(blocks), take(blocks), take(sets), take(1)
@@ -134,7 +134,8 @@
         after, (held,) = take(blocks), take(1)
         products(work, info_at, info, mine, other, mats, table, before, after, held)
         return
-    edge, decay, kept, sent, *states = take(4 + blocks)
+    edge, decay, kept, *sent = take(3 + splits)
+    states = take(blocks)
     held, after = refs
     after = [after.at[b] for b in range(blocks)]
     products(work, info_at, info, mine, other, mats, table, before, after, held)
@@ -154,20 +155,22 @@
         far = jnp.dot(left, jnp.concatenate([ch, ch, cl], axis=0), preferred_element_type=f32)
         values.append(after[b][:width, :] + far)
     first = info[closing] == 0
-    for ref, one, two in ((kept, *values), (sent, *reversed(values))):
-        value = jnp.where(first, one, two)
-        for s in range(subs):
-            ref[s * width : (s + 1) * width, :] = value[:, s * half : (s + 1) * half]
-
-
-def add_blocks(info, info_at, mine, other, mats, table, totals, work, ends=None, closing=0):
+    rows = sent[0].shape[0]
+    for s in range(subs):
+        lanes, at = slice(s * half, (s + 1) * half), s * width
+        one, two = [value[:, lanes] for value in values]
+        kept[at : at + width, :] = jnp.where(first, one, two)
+        sent[at // rows][at % rows : at % rows + width, :] = jnp.where(first, two, one)
+
+
+def add_blocks(info, info_at, mine, other, mats, table, totals, work, ends=None, closing=0, splits=1):
     blocks, sets = len(mine), len(mats)
     fresh = [t is None for t in totals]
     old = [t for t in totals if t is not None]
     half, length = mats[0].shape[1], mine[0].shape[0]
     height, tw = table.shape[1:]
     lanes = length // (tw // 4) * half
-    units = len(work) * mats[0].shape[0] // 2
+    units = sum(mats[n].shape[0] // 2 for n, _ in work)
     first = 1 + 2 * blocks + sets + 1
     scratch = [pltpu.VMEM((units, tw, lanes), bf16)]
     if ends is None:
@@ -175,11 +178,12 @@
         shapes = [jax.ShapeDtypeStruct((height, lanes), f32)] * blocks
     else:
         aliases = {}
-        shapes = [jax.ShapeDtypeStruct((length, half), f32)] * 2
+        shapes = [jax.ShapeDtypeStruct((length, half), f32)]
+        shapes += [jax.ShapeDtypeStruct((length // splits, half), f32)] * splits
         shapes += [jax.ShapeDtypeStruct((height - tw // 4, half), f32)] * blocks
         scratch.append(pltpu.VMEM((blocks, height, lanes), f32))
     return pl.pallas_call(
-        functools.partial(blocks_kernel, blocks, sets, work, info_at, fresh, closing),
+        functools.partial(blocks_kernel, blocks, sets, work, info_at, fresh, closing, splits),
         in_specs=[SM] + [VM] * (2 * blocks + sets + 1 + len(old) + len(ends)),
         out_specs=[VM] * len(shapes),
         out_shape=shapes,
@@ -218,16 +222,19 @@
     )(info, *states, decay)
 
 
-def result_kernel(pairs, here_at, info, *refs):
-    kept, arrived = refs[: len(pairs)], refs[len(pairs) : 2 * len(pairs)]
-    carry_kept, carry_arrived, edge, *outs = refs[2 * len(pairs) :]
+def result_kernel(pairs, splits, here_at, info, *refs):
+    refs = list(refs)
+    take = lambda n: [refs.pop(0) for _ in range(n)]
+    kept, arrived = take(len(pairs)), [take(n) for n in splits]
+    carry_kept, carry_arrived, edge, *outs = refs
     eh, el = split2(edge[...])
     left = jnp.concatenate([eh, el, eh], axis=1)
     values = []
     for n, r in enumerate(pairs):
         ch, cl = split2(carry_kept[r] + carry_arrived[r])
         far = jnp.dot(left, jnp.concatenate([ch, ch, cl], axis=0), preferred_element_type=f32)
-        values.append((kept[n][...] + arrived[n][...] + far).astype(bf16))
+        other = jnp.concatenate([part[...] for part in arrived[n]], axis=0)
+        values.append((kept[n][...] + other + far).astype(bf16))
     first = info[here_at] == 0
     outs[0][...] = jnp.where(first, values[0], values[1])
     outs[1][...] = jnp.where(first, values[1], values[0])
@@ -235,13 +242,13 @@
 
 def results(info, here_at, pairs, kept, arrived, carries, edge):
     return pl.pallas_call(
-        functools.partial(result_kernel, pairs, here_at),
-        in_specs=[SM] + [VM] * (2 * len(pairs) + 3),
+        functools.partial(result_kernel, pairs, [len(parts) for parts in arrived], here_at),
+        in_specs=[SM] + [VM] * (len(pairs) + sum(len(parts) for parts in arrived) + 3),
         out_specs=[VM] * len(pairs),
         out_shape=[jax.ShapeDtypeStruct(kept[0].shape, bf16)] * len(pairs),
         compiler_params=params(),
         name="finish_blocks",
-    )(info, *kept, *arrived, *carries, edge)
+    )(info, *kept, *[part for parts in arrived for part in parts], *carries, edge)
 
 
 def arrange_kernel(count, lanes_at, info, *refs):
@@ -470,19 +477,21 @@
     half, width = features // 2, length // 4
     tiled = half % 128 == 0 and wide % 128 == 0 and width % 128 == 0 and pole_rates.shape[0] % 16 == 0
     found = final_rounds(count, groups)
-    if not tiled or own_filters % 2 or found is None:
+    if not tiled or own_filters % 4 or found is None:
         return plain_device(out_grad, filter_mats, coeffs, pole_rates)
     pairs, flips, rounds = found
     ways, per_grp = groups // 2, count // groups
     order, offsets = ring_of(count)
     right = [(order[i], order[(i + 1) % count]) for i in range(count)]
     left = [(b, a) for a, b in right]
-    to = [(1, 0), (1, 1), (0, 1), (0, 0)]
-    sources = [(0, 1), (0, 0), (1, 0), (1, 1)]
+    some = own_filters // 2
+    far_to = [(1, h, 0, own_filters) for h in range(2)]
+    swap_to = [(0, 1, lo, some) for lo in (0, some)]
+    own_to = (0, 0, 0, own_filters)
 
     def numbers(ctx, grp):
         way, here, at = grp // 2, grp % 2, order.index(ctx)
-        firsts = [((way ^ w) * 2 + (here ^ h)) * (own_filters // 2) for w, h in sources]
+        firsts = [(((way ^ w) * 2 + (here ^ h)) * own_filters + lo) // 2 for w, h, lo, _ in [*swap_to, own_to, *far_to]]
         slots = [order[(at + o) % count] for o in offsets]
         second = [way ^ flip for flip in flips[ctx]]
         use = [slots[p[t]] for p, t in zip(pairs, second)] + [slots[p[1 - t]] for p, t in zip(pairs, second)]
@@ -494,23 +503,28 @@
     swap = lambda x: shift_of(x, ways, 0, 1)
     together = lambda *x: lax.optimization_barrier(x)
 
-    pieces = cut(filter_mats, to[:1], half, 2 * wide)
+    pieces = cut(filter_mats, far_to[:1], half, 2 * wide)
     gains = jnp.sqrt(-jnp.expm1(-2.0 * pole_rates))
-    table = tables(coeffs, pole_rates, gains, width)
-    mats = [None, None, shift_of(pieces[0], ways, *to[0])]
+    table = ()
+    cut_early = cut(filter_mats, [*swap_to, own_to, far_to[1]], half, 2 * wide)
+    mats = [None, None, None, shift_of(pieces[0], ways, *far_to[0][:2])]
     going_right, going_left = out_grad, out_grad
     mine, other, totals = [out_grad], [swap(out_grad)], [None] * count
     back = lambda n: gains[None, :] * jnp.exp((jnp.arange(n, dtype=f32) - n)[:, None] * pole_rates[None, :])
     ahead = lambda n: jnp.exp(-n * pole_rates)[:, None]
     ends, far_ends = (back(width), ahead(width)), (back(length), ahead(length))
 
+    done_sets, splits = {}, [1] * (len(pairs) - 1) + [2]
+
     def run(slots, use, closing=None):
+        for s in slots:
+            done_sets.setdefault(s, set()).update(use[s])
         chosen = sorted({n for s in slots for n in use[s]})
         info_at = [core_at] + [firsts_at + n for n in chosen]
         work = [(chosen.index(n), b) for n in chosen for b, s in enumerate(slots) if n in use[s]]
         got = add_blocks(
             row, info_at, [mine[s] for s in slots], [other[s] for s in slots], [mats[n] for n in chosen], table,
-            [totals[s] for s in slots], work, *(() if closing is None else (ends, second_at + closing)),
+            [totals[s] for s in slots], work, *(() if closing is None else (ends, second_at + closing, splits[closing])),
         )
         if closing is not None:
             return got
@@ -529,18 +543,26 @@
                 lax.ppermute(going_left[length // 2 :], "ctx", left),
             ]
         if step == 3:
-            piece, mats[2] = together(pieces[1], mats[2])
-            mats.append(shift_of(piece, ways, *to[1]))
+            piece, mats[3] = together(next_piece, mats[3])
+            mats.append(shift_of(piece, ways, *far_to[1][:2]))
         if step == 2:
-            pieces += cut(filter_mats, to[1:], half, 2 * wide)
-            mats[:2] = [swap(pieces[2]), pieces[3]]
+            table = tables(coeffs, later_rates, gains, width)
+            mats[:2] = [swap(p) for p in pieces[:2]]
+            mats[2], next_piece = pieces[2:]
         elif step > 2:
             slots = ([0] if step == 3 else []) + [2 * step - 5, 2 * step - 4]
-            run(slots, {s: [0, 1, 2] for s in slots})
+            run(slots, {s: [0, 1, 2, 3] for s in slots})
+        if step == count // 2:
+            slots = [2 * step - 3, 2 * step - 2]
+            run(slots, {s: [2] for s in slots})
         done = [s for s in range(count) if totals[s] is not None]
-        coming, swapped, table, sums, early, filter_mats = together(
-            coming, other[-len(arrived) :], table, [totals[s] for s in done], mats[:3] if step > 1 else [], filter_mats
+        coming, swapped, table, sums, early, filter_mats, cut_early = together(
+            coming, other[-len(arrived) :], table, [totals[s] for s in done], mats[:4] if step > 1 else [], filter_mats, cut_early
         )
+        if step == 1:
+            pieces, row, coming = together(cut_early, row, coming)
+        if step == 1:
+            later_rates, coming = together(pole_rates, coming)
         other[-len(arrived) :] = swapped
         mats[: len(early)] = early
         for s, t in zip(done, sums):
@@ -554,15 +576,15 @@
 
     kept, sent, states = [None] * len(pairs), [None] * len(pairs), [None] * count
     for pair in [*sorted(pairs)[1:], sorted(pairs)[0]]:
-        use = {s: [n for n in range(4) if totals[s] is None or n == 3] for s in pair}
-        keep, send, *state = run(list(pair), use, pairs.index(pair))
+        use = {s: [n for n in range(5) if n not in done_sets.get(s, ())] for s in pair}
+        keep, *send = run(list(pair), use, pairs.index(pair))
+        send, state = send[:-2], send[-2:]
         for s, st in zip(pair, state):
             states[s] = st
         kept[pairs.index(pair)], sent[pairs.index(pair)] = keep, send
     carry_kept, carry_sent = carry(row, slots_at, use_at, states, far_ends[1])
-    sent[-1], carry_sent = together(sent[-1], carry_sent)
     carries = [carry_kept, shift_of(carry_sent, ways, 1, 0)]
-    arrived = [shift_of(x, ways, 1, 0) for x in sent]
+    arrived = [[shift_of(x, ways, 1, 0) for x in parts] for parts in sent]
     received = []
     for first in range(0, len(pairs), 2):
         both = [first, first + 1]

time: 121 us -> 114 us (0.942)
  local copies, waits for them, and re-layouts: 6.02 us -> 1.89 us
  waiting for transfers between devices: 36.8 us -> 32.9 us
  Pallas kernels: 49.6 us -> 50.9 us
    ppermute x16 -> x18, waiting for transfers between devices: 10.1 us -> 4.3 us  [shift_of(): lax.ppermute(x, 'grp', [(rank(w, h), rank(w + by_way, h ^ by_core)) for w...]
    unnamed x23 -> x15, local copies, waits for them, and re-layouts: 4.97 us -> 0.84 us
    ppermute x3, waiting for transfers between devices: 13.1 us -> 15.7 us  [per_device(): lax.ppermute(going_right, 'ctx', right)]
    ppermute x4, waiting for transfers between devices: 5.56 us -> 7.9 us  [per_device(): lax.ppermute(v, ('ctx', 'grp'), moves)]
    ppermute x3, waiting for transfers between devices: 7.25 us -> 4.96 us  [per_device(): lax.ppermute(going_left, 'ctx', left)]
    pallas_call x6 -> x7, Pallas kernels: 38 us -> 39.3 us  [add_blocks(): pl.pallas_call(functools.partial(blocks_kernel, blocks, sets, work, info_...]
    ppermute x16 -> x18, starting transfers between devices: 7.29 us -> 8.36 us  [shift_of(): lax.ppermute(x, 'grp', [(rank(w, h), rank(w + by_way, h ^ by_core)) for w...]
  transfers between devices with their start and end apart: 28 -> 30, of which waited for: 9 -> 10; matrix products, arithmetic and copies ran while one was open for 1% -> 1% of each run, Pallas kernels for 37% -> 40%
where the time goes in v4:
time: 114 us
  Pallas kernels  50.9 us (45%)
  waiting for transfers between devices  32.9 us (29%)
  starting transfers between devices  27.7 us (24%)
  local copies, waits for them, and re-layouts  1.89 us (2%)
    pallas_call x7, Pallas kernels, add_blocks(): pl.pallas_call(functools.partial(blocks_kernel, blocks, sets, work, info_...  39.3 us
    ppermute x3, waiting for transfers between devices, per_device(): lax.ppermute(going_right, 'ctx', right)  15.7 us
    ppermute x4, starting transfers between devices, per_device(): lax.ppermute(v, ('ctx', 'grp'), moves)  11.2 us
    ppermute x18, starting transfers between devices, shift_of(): lax.ppermute(x, 'grp', [(rank(w, h), rank(w + by_way, h ^ by_core)) for w...  8.36 us
    ppermute x4, waiting for transfers between devices, per_device(): lax.ppermute(v, ('ctx', 'grp'), moves)  7.9 us
    pallas_call x2, Pallas kernels, cut(): pl.pallas_call(functools.partial(cut_kernel, to), in_specs=[ANY], out_spe...  5.82 us
    ppermute x3, waiting for transfers between devices, per_device(): lax.ppermute(going_left, 'ctx', left)  4.96 us
    ppermute x3, starting transfers between devices, per_device(): lax.ppermute(going_right, 'ctx', right)  4.78 us
  transfers between devices with their start and end apart: 30, of which 10 were waited for; matrix products, arithmetic and copies ran while one was open for 1% of the time, Pallas kernels for 40%

profile of v4, /device:TPU:4, one launch (start us, length us, event | category | flops | bytes accessed | tf_op | source)
XLA Modules:
  0.0 114.0 jit_solution(11129534503526875651)
XLA Ops:
  0.0 1.6 %collective-permute-start = (bf16[512,512]{1,0:T(8,128)(2,1)}, bf16[512,512]{1,0:T(8,128)(2,1)S(1)}, u32[]{:S(2)}, u32[]{:S(2)}) collective-permute-start(bf16[512,512]{1,0:T(8,128)(2,1)} %refs_0_.3), channel_id=1, source_target_pairs={{0,8},{8,16},{16,24},{24,28},{28,20},{20,12},{12,4},{4,0},{1,9},{9... | collective-permute-start | bytes 1572872 | tf_op jit(solution)/shard_map/ppermute | solution.py:539
  2.0 2.2 %cut_filters.3 = bf16[4,128,1024]{2,1,0:T(8,128)(2,1)} custom-call(bf16[4,256,2048]{2,1,0:T(8,128)(2,1)} %mats.3), custom_call_target="tpu_custom_call" | custom-call | tf_op jit(solution)/shard_map/cut_filters/pallas_call | solution.py:83
  4.4 3.6 %cut_filters.2 = (bf16[2,128,1024]{2,1,0:T(8,128)(2,1)}, bf16[2,128,1024]{2,1,0:T(8,128)(2,1)}, bf16[4,128,1024]{2,1,0:T(8,128)(2,1)}, bf16[4,128,1024]{2,1,0:T(8,128)(2,1)}) custom-call(bf16[4,256,2048]{2,1,0:T(8,128)(2,1)} %mats.3), custom_call_target="tpu_custom_call" | custom-call | tf_op jit(solution)/shard_map/cut_filters/pallas_call | solution.py:83
  8.7 5.2 %collective-permute-done.refs_1_.refs_0_ = bf16[512,512]{1,0:T(8,128)(2,1)S(1)} collective-permute-done((bf16[512,512]{1,0:T(8,128)(2,1)}, bf16[512,512]{1,0:T(8,128)(2,1)S(1)}, u32[]{:S(2)}, u32[]{:S(2)}) %collective-permute-start) | collective-permute-done | bytes 524320 | tf_op jit(solution)/shard_map/ppermute | solution.py:539
  15.2 1.6 %collective-permute-start.3 = (bf16[512,512]{1,0:T(8,128)(2,1)S(1)}, bf16[512,512]{1,0:T(8,128)(2,1)S(1)}, u32[]{:S(2)}, u32[]{:S(2)}) collective-permute-start(bf16[512,512]{1,0:T(8,128)(2,1)S(1)} %collective-permute-done.refs_1_.refs_0_), channel_id=1, source_target_pairs={{0,8},{8,16},{16,24},{24,28},{28,20},{20,12},{12,4},{4,0},{1,9},{9... | collective-permute-start | bytes 1572872 | tf_op jit(solution)/shard_map/ppermute | solution.py:539
  17.9 9.7 %collective-permute-done.3.refs_0_ = bf16[512,512]{1,0:T(8,128)(2,1)S(1)} collective-permute-done((bf16[512,512]{1,0:T(8,128)(2,1)S(1)}, bf16[512,512]{1,0:T(8,128)(2,1)S(1)}, u32[]{:S(2)}, u32[]{:S(2)}) %collective-permute-start.3) | collective-permute-done | bytes 524320 | tf_op jit(solution)/shard_map/ppermute | solution.py:539
  30.1 1.9 %pole_tables.1.refs_10_.refs_8_.refs_5_.refs_9_ = bf16[8,208,512]{2,1,0:T(8,128)(2,1)S(1)} custom-call(f32[80,18]{1,0:T(8,128)S(1)} %copy.14.poles_ref), custom_call_target="tpu_custom_call" | custom-call | flops 4000000000 | tf_op jit(solution)/shard_map/pole_tables/pallas_call | solution.py:55
  32.1 1.6 %collective-permute-start.11 = (bf16[512,512]{1,0:T(8,128)(2,1)S(1)}, bf16[512,512]{1,0:T(8,128)(2,1)S(1)}, u32[]{:S(2)}, u32[]{:S(2)}) collective-permute-start(bf16[512,512]{1,0:T(8,128)(2,1)S(1)} %collective-permute-done.3.refs_0_), channel_id=1, source_target_pairs={{0,8},{8,16},{16,24},{24,28},{28,20},{20,12},{12,4},{4,0},{1,9},{9... | collective-permute-start | bytes 1572872 | tf_op jit(solution)/shard_map/ppermute | solution.py:539
  34.8 10.1 %add_blocks.3 = (f32[208,512]{1,0:T(8,128)S(1)}, f32[208,512]{1,0:T(8,128)S(1)}, f32[208,512]{1,0:T(8,128)S(1)}) custom-call(s32[30]{0:T(128)S(1)} %dynamic-slice_bitcast_fusion.info, bf16[512,512]{1,0:T(8,128)(2,1)S(1)} %copy-done.1, bf16[512,512]{1,0:T(8,128)(2,1)S(1)} %collective-permute-done.refs_1_.refs_0_, ...), custom_call_target="tpu_custom_call" | custom-call | flops 10800000000 | tf_op jit(solution)/shard_map/add_blocks/pallas_call | solution.py:185
  45.7 2.4 %collective-permute-done.12.refs_1_ = bf16[512,512]{1,0:T(8,128)(2,1)S(1)} collective-permute-done((bf16[512,512]{1,0:T(8,128)(2,1)S(1)}, bf16[512,512]{1,0:T(8,128)(2,1)S(1)}, u32[]{:S(2)}, u32[]{:S(2)}) %collective-permute-start.12) | collective-permute-done | bytes 524320 | tf_op jit(solution)/shard_map/ppermute | solution.py:539
  50.8 6.9 %add_blocks.4 = (f32[208,512]{1,0:T(8,128)S(1)}, f32[208,512]{1,0:T(8,128)S(1)}) custom-call(s32[30]{0:T(128)S(1)} %dynamic-slice_bitcast_fusion.info, bf16[512,512]{1,0:T(8,128)(2,1)S(1)} %collective-permute-done.3.refs_0_, bf16[512,512]{1,0:T(8,128)(2,1)S(1)} %copy-done.3, bf16[512,512]{1,0:T(8,128)(2,1)S(1)} %collective-permute-done.13.refs_2_, ...), custom_call_target="tpu_custom_call" | custom-call | flops 7200000000 | tf_op jit(solution)/shard_map/add_blocks/pallas_call | solution.py:185
  57.7 2.6 %add_blocks.5 = (f32[208,512]{1,0:T(8,128)S(1)}, f32[208,512]{1,0:T(8,128)S(1)}) custom-call(s32[30]{0:T(128)S(1)} %dynamic-slice_bitcast_fusion.info, bf16[512,512]{1,0:T(8,128)(2,1)S(1)} %collective-permute-done.11.refs_0_, bf16[512,512]{1,0:T(8,128)(2,1)S(1)} %collective-permute-done.12.refs_1_, bf16[512,512]{1,0:T(8,128)(2,1)S(1)} %collective-permute-done.17.refs_2_, ...), custom_call_target="tpu_custom_call" | custom-call | flops 2400000000 | tf_op jit(solution)/shard_map/add_blocks/pallas_call | solution.py:185
  60.3 3.4 %close_blocks.4 = (f32[512,128]{1,0:T(8,128)S(1)}, f32[512,128]{1,0:T(8,128)S(1)}, f32[80,128]{1,0:T(8,128)S(1)}, f32[80,128]{1,0:T(8,128)S(1)}) custom-call(s32[30]{0:T(128)S(1)} %dynamic-slice_bitcast_fusion.info, bf16[512,512]{1,0:T(8,128)(2,1)S(1)} %collective-permute-done.refs_1_.refs_0_, bf16[512,512]{1,0:T(8,128)(2,1)S(1)} %collective-permute-done.1.refs_2_.refs_1_, ...), custom_call_target="tpu_custom_call" | custom-call | flops 2400000000 | tf_op jit(solution)/shard_map/close_blocks/pallas_call | solution.py:185
  64.5 7.1 %close_blocks.5 = (f32[512,128]{1,0:T(8,128)S(1)}, f32[512,128]{1,0:T(8,128)S(1)}, f32[80,128]{1,0:T(8,128)S(1)}, f32[80,128]{1,0:T(8,128)S(1)}) custom-call(s32[30]{0:T(128)S(1)} %dynamic-slice_bitcast_fusion.info, bf16[512,512]{1,0:T(8,128)(2,1)S(1)} %collective-permute-done.11.refs_0_, bf16[512,512]{1,0:T(8,128)(2,1)S(1)} %collective-permute-done.12.refs_1_, ...), custom_call_target="tpu_custom_call" | custom-call | flops 7200000000 | tf_op jit(solution)/shard_map/close_blocks/pallas_call | solution.py:185
  71.6 1.6 %collective-permute-start.20 = (f32[512,128]{1,0:T(8,128)S(1)}, f32[512,128]{1,0:T(8,128)S(1)}, u32[]{:S(2)}, u32[]{:S(2)}) collective-permute-start(f32[512,128]{1,0:T(8,128)S(1)} %get-tuple-element.159), channel_id=1, source_target_pairs={{0,2},{1,3},{2,0},{3,1},{4,6},{5,7},{6,4},{7,5},{8,10},{9,11},{10,... | collective-permute-start | bytes 786440 | tf_op jit(solution)/shard_map/ppermute | solution.py:344
  73.2 3.0 %close_blocks.7 = (f32[512,128]{1,0:T(8,128)S(1)}, f32[512,128]{1,0:T(8,128)S(1)}, f32[80,128]{1,0:T(8,128)S(1)}, f32[80,128]{1,0:T(8,128)S(1)}) custom-call(s32[30]{0:T(128)S(1)} %dynamic-slice_bitcast_fusion.info, bf16[512,512]{1,0:T(8,128)(2,1)S(1)} %collective-permute-done.3.refs_0_, bf16[512,512]{1,0:T(8,128)(2,1)S(1)} %copy-done.3, ...), custom_call_target="tpu_custom_call" | custom-call | flops 2400000000 | tf_op jit(solution)/shard_map/close_blocks/pallas_call | solution.py:185
  76.7 6.2 %close_blocks.6 = (f32[512,128]{1,0:T(8,128)S(1)}, f32[256,128]{1,0:T(8,128)S(1)}, f32[256,128]{1,0:T(8,128)S(1)}, f32[80,128]{1,0:T(8,128)S(1)}, f32[80,128]{1,0:T(8,128)S(1)}) custom-call(s32[30]{0:T(128)S(1)} %dynamic-slice_bitcast_fusion.info, bf16[512,512]{1,0:T(8,128)(2,1)S(1)} %copy-done.1, ...), custom_call_target="tpu_custom_call" | custom-call | flops 6000000000 | tf_op jit(solution)/shard_map/close_blocks/pallas_call | solution.py:185
  83.6 1.6 %collective-permute-start.22 = (f32[4,80,128]{2,1,0:T(8,128)S(1)}, f32[4,80,128]{2,1,0:T(8,128)S(1)}, u32[]{:S(2)}, u32[]{:S(2)}) collective-permute-start(f32[4,80,128]{2,1,0:T(8,128)S(1)} %get-tuple-element.175), channel_id=1, source_target_pairs={{0,2},{1,3},{2,0},{3,1},{4,6},{5,7},{6,4},{7,5},{8,10},{9,11},{10,... | collective-permute-start | bytes 491528 | tf_op jit(solution)/shard_map/ppermute | solution.py:344
  85.7 1.5 %collective-permute-start.27 = (f32[256,128]{1,0:T(8,128)S(1)}, f32[256,128]{1,0:T(8,128)S(1)}, u32[]{:S(2)}, u32[]{:S(2)}) collective-permute-start(f32[256,128]{1,0:T(8,128)S(1)} %get-tuple-element.182), channel_id=1, source_target_pairs={{0,2},{1,3},{2,0},{3,1},{4,6},{5,7},{6,4},{7,5},{8,10},{9,11},{10,... | collective-permute-start | bytes 393224 | tf_op jit(solution)/shard_map/ppermute | solution.py:344
  87.4 3.4 %collective-permute-done.22.refs_5_.refs_6_ = f32[4,80,128]{2,1,0:T(8,128)S(1)} collective-permute-done((f32[4,80,128]{2,1,0:T(8,128)S(1)}, f32[4,80,128]{2,1,0:T(8,128)S(1)}, u32[]{:S(2)}, u32[]{:S(2)}) %collective-permute-start.22) | collective-permute-done | bytes 163872 | tf_op jit(solution)/shard_map/ppermute | solution.py:344
  96.2 6.6 %collective-permute-start.28 = (bf16[512,128]{1,0:T(8,128)(2,1)S(1)}, bf16[512,128]{1,0:T(8,128)(2,1)S(1)}, u32[]{:S(2)}, u32[]{:S(2)}) collective-permute-start(bf16[512,128]{1,0:T(8,128)(2,1)S(1)} %get-tuple-element.183), channel_id=1, source_target_pairs={{0,12},{1,0},{2,16},{3,28},{4,8},{5,4},{6,20},{7,24},{8,25},{9,21}... | collective-permute-start | bytes 393224 | tf_op jit(solution)/shard_map/ppermute | solution.py:592
  102.8 1.9 %collective-permute-start.29 = (bf16[512,128]{1,0:T(8,128)(2,1)S(1)}, bf16[512,128]{1,0:T(8,128)(2,1)S(1)}, u32[]{:S(2)}, u32[]{:S(2)}) collective-permute-start(bf16[512,128]{1,0:T(8,128)(2,1)S(1)} %get-tuple-element.184), channel_id=1, source_target_pairs={{0,0},{1,12},{2,28},{3,16},{4,4},{5,8},{6,24},{7,20},{8,21},{9,25}... | collective-permute-start | bytes 393224 | tf_op jit(solution)/shard_map/ppermute | solution.py:592
  104.7 3.3 %collective-permute-done.28.refs_2_ = bf16[512,128]{1,0:T(8,128)(2,1)S(1)} collective-permute-done((bf16[512,128]{1,0:T(8,128)(2,1)S(1)}, bf16[512,128]{1,0:T(8,128)(2,1)S(1)}, u32[]{:S(2)}, u32[]{:S(2)}) %collective-permute-start.28) | collective-permute-done | bytes 131104 | tf_op jit(solution)/shard_map/ppermute | solution.py:592
  108.1 4.6 %collective-permute-done.29.refs_3_ = bf16[512,128]{1,0:T(8,128)(2,1)S(1)} collective-permute-done((bf16[512,128]{1,0:T(8,128)(2,1)S(1)}, bf16[512,128]{1,0:T(8,128)(2,1)S(1)}, u32[]{:S(2)}, u32[]{:S(2)}) %collective-permute-start.29) | collective-permute-done | bytes 131104 | tf_op jit(solution)/shard_map/ppermute | solution.py:592
  (78 shorter events, 20.2 us)
Async XLA Ops:
  0.0 13.9 %collective-permute-start = (bf16[512,512]{1,0:T(8,128)(2,1)}, bf16[512,512]{1,0:T(8,128)(2,1)S(1)}, u32[]{:S(2)}, u32[]{:S(2)}) collective-permute-start(bf16[512,512]{1,0:T(8,128)(2,1)} %refs_0_.3), channel_id=1, source_target_pairs={{0,8},{8,16},{16,24},{24,28},{28,20},{20,12},{12,4},{4,0},{1,9},{9... | collective-permute-start | bytes 1572872 | tf_op jit(solution)/shard_map/ppermute | solution.py:539
  1.6 13.6 %collective-permute-start.1 = (bf16[512,512]{1,0:T(8,128)(2,1)}, bf16[512,512]{1,0:T(8,128)(2,1)S(1)}, u32[]{:S(2)}, u32[]{:S(2)}) collective-permute-start(bf16[512,512]{1,0:T(8,128)(2,1)} %refs_0_.3), channel_id=1, source_target_pairs={{8,0},{16,8},{24,16},{28,24},{20,28},{12,20},{4,12},{0,4},{9,1},{1... | collective-permute-start | bytes 1572872 | tf_op jit(solution)/shard_map/ppermute | solution.py:539
  2.0 13.1 %collective-permute-start.2 = (bf16[512,512]{1,0:T(8,128)(2,1)}, bf16[512,512]{1,0:T(8,128)(2,1)S(1)}, u32[]{:S(2)}, u32[]{:S(2)}) collective-permute-start(bf16[512,512]{1,0:T(8,128)(2,1)} %refs_0_.3), channel_id=1, source_target_pairs={{0,1},{1,0},{2,3},{3,2},{4,5},{5,4},{6,7},{7,6},{8,9},{9,8},{10,11... | collective-permute-start | bytes 1572872 | tf_op jit(solution)/shard_map/ppermute | solution.py:344
  4.3 27.8 %collective-permute-start.9 = (bf16[4,128,1024]{2,1,0:T(8,128)(2,1)}, bf16[4,128,1024]{2,1,0:T(8,128)(2,1)S(1)}, u32[]{:S(2)}, u32[]{:S(2)}) collective-permute-start(bf16[4,128,1024]{2,1,0:T(8,128)(2,1)} %cut_filters.3), channel_id=1, source_target_pairs={{0,2},{1,3},{2,0},{3,1},{4,6},{5,7},{6,4},{7,5},{8,10},{9,11},{10,... | collective-permute-start | bytes 3145736 | tf_op jit(solution)/shard_map/ppermute | solution.py:344
  15.2 12.5 %collective-permute-start.3 = (bf16[512,512]{1,0:T(8,128)(2,1)S(1)}, bf16[512,512]{1,0:T(8,128)(2,1)S(1)}, u32[]{:S(2)}, u32[]{:S(2)}) collective-permute-start(bf16[512,512]{1,0:T(8,128)(2,1)S(1)} %collective-permute-done.refs_1_.refs_0_), channel_id=1, source_target_pairs={{0,8},{8,16},{16,24},{24,28},{28,20},{20,12},{12,4},{4,0},{1,9},{9... | collective-permute-start | bytes 1572872 | tf_op jit(solution)/shard_map/ppermute | solution.py:539
  16.8 12.2 %collective-permute-start.4 = (bf16[512,512]{1,0:T(8,128)(2,1)S(1)}, bf16[512,512]{1,0:T(8,128)(2,1)S(1)}, u32[]{:S(2)}, u32[]{:S(2)}) collective-permute-start(bf16[512,512]{1,0:T(8,128)(2,1)S(1)} %collective-permute-done.1.refs_2_.refs_1_), channel_id=1, source_target_pairs={{8,0},{16,8},{24,16},{28,24},{20,28},{12,20},{4,12},{0,4},{9,1},{1... | collective-permute-start | bytes 1572872 | tf_op jit(solution)/shard_map/ppermute | solution.py:539
  17.3 14.7 %collective-permute-start.5 = (bf16[512,512]{1,0:T(8,128)(2,1)S(1)}, bf16[512,512]{1,0:T(8,128)(2,1)}, u32[]{:S(2)}, u32[]{:S(2)}) collective-permute-start(bf16[512,512]{1,0:T(8,128)(2,1)S(1)} %collective-permute-done.refs_1_.refs_0_), channel_id=1, source_target_pairs={{0,1},{1,0},{2,3},{3,2},{4,5},{5,4},{6,7},{7,6},{8,9},{9,8},{10,11... | collective-permute-start | bytes 1572872 | tf_op jit(solution)/shard_map/ppermute | solution.py:344
  17.4 14.6 %collective-permute-start.6 = (bf16[512,512]{1,0:T(8,128)(2,1)S(1)}, bf16[512,512]{1,0:T(8,128)(2,1)}, u32[]{:S(2)}, u32[]{:S(2)}) collective-permute-start(bf16[512,512]{1,0:T(8,128)(2,1)S(1)} %collective-permute-done.1.refs_2_.refs_1_), channel_id=1, source_target_pairs={{0,1},{1,0},{2,3},{3,2},{4,5},{5,4},{6,7},{7,6},{8,9},{9,8},{10,11... | collective-permute-start | bytes 1572872 | tf_op jit(solution)/shard_map/ppermute | solution.py:344
  32.1 13.6 %collective-permute-start.11 = (bf16[512,512]{1,0:T(8,128)(2,1)S(1)}, bf16[512,512]{1,0:T(8,128)(2,1)S(1)}, u32[]{:S(2)}, u32[]{:S(2)}) collective-permute-start(bf16[512,512]{1,0:T(8,128)(2,1)S(1)} %collective-permute-done.3.refs_0_), channel_id=1, source_target_pairs={{0,8},{8,16},{16,24},{24,28},{28,20},{20,12},{12,4},{4,0},{1,9},{9... | collective-permute-start | bytes 1572872 | tf_op jit(solution)/shard_map/ppermute | solution.py:539
  33.7 14.3 %collective-permute-start.13 = (bf16[512,512]{1,0:T(8,128)(2,1)S(1)}, bf16[512,512]{1,0:T(8,128)(2,1)S(1)}, u32[]{:S(2)}, u32[]{:S(2)}) collective-permute-start(bf16[512,512]{1,0:T(8,128)(2,1)S(1)} %collective-permute-done.3.refs_0_), channel_id=1, source_target_pairs={{0,1},{1,0},{2,3},{3,2},{4,5},{5,4},{6,7},{7,6},{8,9},{9,8},{10,11... | collective-permute-start | bytes 1572872 | tf_op jit(solution)/shard_map/ppermute | solution.py:344
  33.7 14.3 %collective-permute-start.12 = (bf16[512,512]{1,0:T(8,128)(2,1)S(1)}, bf16[512,512]{1,0:T(8,128)(2,1)S(1)}, u32[]{:S(2)}, u32[]{:S(2)}) collective-permute-start(bf16[512,512]{1,0:T(8,128)(2,1)S(1)} %copy-done.3), channel_id=1, source_target_pairs={{8,0},{16,8},{24,16},{28,24},{20,28},{12,20},{4,12},{0,4},{9,1},{1... | collective-permute-start | bytes 1572872 | tf_op jit(solution)/shard_map/ppermute | solution.py:539
  34.1 13.9 %collective-permute-start.14 = (bf16[512,512]{1,0:T(8,128)(2,1)S(1)}, bf16[512,512]{1,0:T(8,128)(2,1)S(1)}, u32[]{:S(2)}, u32[]{:S(2)}) collective-permute-start(bf16[512,512]{1,0:T(8,128)(2,1)S(1)} %copy-done.3), channel_id=1, source_target_pairs={{0,1},{1,0},{2,3},{3,2},{4,5},{5,4},{6,7},{7,6},{8,9},{9,8},{10,11... | collective-permute-start | bytes 1572872 | tf_op jit(solution)/shard_map/ppermute | solution.py:344
  34.4 25.9 %collective-permute-start.10 = (bf16[4,128,1024]{2,1,0:T(8,128)(2,1)S(1)}, bf16[4,128,1024]{2,1,0:T(8,128)(2,1)S(1)}, u32[]{:S(2)}, u32[]{:S(2)}) collective-permute-start(bf16[4,128,1024]{2,1,0:T(8,128)(2,1)S(1)} %copy-done.6), channel_id=1, source_target_pairs={{0,3},{1,2},{2,1},{3,0},{4,7},{5,6},{6,5},{7,4},{8,11},{9,10},{10,... | collective-permute-start | bytes 3145736 | tf_op jit(solution)/shard_map/ppermute | solution.py:344
  48.1 9.6 %collective-permute-start.17 = (bf16[512,512]{1,0:T(8,128)(2,1)S(1)}, bf16[512,512]{1,0:T(8,128)(2,1)S(1)}, u32[]{:S(2)}, u32[]{:S(2)}) collective-permute-start(bf16[512,512]{1,0:T(8,128)(2,1)S(1)} %collective-permute-done.11.refs_0_), channel_id=1, source_target_pairs={{0,1},{1,0},{2,3},{3,2},{4,5},{5,4},{6,7},{7,6},{8,9},{9,8},{10,11... | collective-permute-start | bytes 1572872 | tf_op jit(solution)/shard_map/ppermute | solution.py:344
  48.7 11.6 %collective-permute-start.15 = (bf16[256,512]{1,0:T(8,128)(2,1)S(1)}, bf16[256,512]{1,0:T(8,128)(2,1)S(1)}, u32[]{:S(2)}, u32[]{:S(2)}) collective-permute-start(bf16[256,512]{1,0:T(8,128)(2,1)S(1)} %slice.6), channel_id=1, source_target_pairs={{0,8},{8,16},{16,24},{24,28},{28,20},{20,12},{12,4},{4,0},{1,9},{9... | collective-permute-start | bytes 786440 | tf_op jit(solution)/shard_map/ppermute | solution.py:542
  50.2 10.1 %collective-permute-start.16 = (bf16[256,512]{1,0:T(8,128)(2,1)S(1)}, bf16[256,512]{1,0:T(8,128)(2,1)S(1)}, u32[]{:S(2)}, u32[]{:S(2)}) collective-permute-start(bf16[256,512]{1,0:T(8,128)(2,1)S(1)} %slice.7), channel_id=1, source_target_pairs={{8,0},{16,8},{24,16},{28,24},{20,28},{12,20},{4,12},{0,4},{9,1},{1... | collective-permute-start | bytes 786440 | tf_op jit(solution)/shard_map/ppermute | solution.py:543
  63.8 21.9 %collective-permute-start.19 = (f32[512,128]{1,0:T(8,128)S(1)}, f32[512,128]{1,0:T(8,128)S(1)}, u32[]{:S(2)}, u32[]{:S(2)}) collective-permute-start(f32[512,128]{1,0:T(8,128)S(1)} %get-tuple-element.158), channel_id=1, source_target_pairs={{0,2},{1,3},{2,0},{3,1},{4,6},{5,7},{6,4},{7,5},{8,10},{9,11},{10,... | collective-permute-start | bytes 786440 | tf_op jit(solution)/shard_map/ppermute | solution.py:344
  64.4 12.3 %collective-permute-start.21 = (bf16[512,512]{1,0:T(8,128)(2,1)S(1)}, bf16[512,512]{1,0:T(8,128)(2,1)S(1)}, u32[]{:S(2)}, u32[]{:S(2)}) collective-permute-start(bf16[512,512]{1,0:T(8,128)(2,1)S(1)} %constant_dynamic-update-slice_fusion.refs_1_), channel_id=1, source_target_pairs={{0,1},{1,0},{2,3},{3,2},{4,5},{5,4},{6,7},{7,6},{8,9},{9,8},{10,11... | collective-permute-start | bytes 1572872 | tf_op jit(solution)/shard_map/ppermute | solution.py:344
  71.6 15.8 %collective-permute-start.20 = (f32[512,128]{1,0:T(8,128)S(1)}, f32[512,128]{1,0:T(8,128)S(1)}, u32[]{:S(2)}, u32[]{:S(2)}) collective-permute-start(f32[512,128]{1,0:T(8,128)S(1)} %get-tuple-element.159), channel_id=1, source_target_pairs={{0,2},{1,3},{2,0},{3,1},{4,6},{5,7},{6,4},{7,5},{8,10},{9,11},{10,... | collective-permute-start | bytes 786440 | tf_op jit(solution)/shard_map/ppermute | solution.py:344
  76.2 18.3 %collective-permute-start.25 = (f32[512,128]{1,0:T(8,128)S(1)}, f32[512,128]{1,0:T(8,128)S(1)}, u32[]{:S(2)}, u32[]{:S(2)}) collective-permute-start(f32[512,128]{1,0:T(8,128)S(1)} %get-tuple-element.180), channel_id=1, source_target_pairs={{0,2},{1,3},{2,0},{3,1},{4,6},{5,7},{6,4},{7,5},{8,10},{9,11},{10,... | collective-permute-start | bytes 786440 | tf_op jit(solution)/shard_map/ppermute | solution.py:344
  91.7 13.0 %collective-permute-start.23 = (bf16[512,128]{1,0:T(8,128)(2,1)S(1)}, bf16[512,128]{1,0:T(8,128)(2,1)S(1)}, u32[]{:S(2)}, u32[]{:S(2)}) collective-permute-start(bf16[512,128]{1,0:T(8,128)(2,1)S(1)} %get-tuple-element.176), channel_id=1, source_target_pairs={{0,8},{1,20},{2,4},{3,24},{4,12},{5,16},{6,0},{7,28},{8,1},{9,29},... | collective-permute-start | bytes 393224 | tf_op jit(solution)/shard_map/ppermute | solution.py:592
  93.1 11.6 %collective-permute-start.24 = (bf16[512,128]{1,0:T(8,128)(2,1)S(1)}, bf16[512,128]{1,0:T(8,128)(2,1)S(1)}, u32[]{:S(2)}, u32[]{:S(2)}) collective-permute-start(bf16[512,128]{1,0:T(8,128)(2,1)S(1)} %get-tuple-element.177), channel_id=1, source_target_pairs={{0,20},{1,8},{2,24},{3,4},{4,16},{5,12},{6,28},{7,0},{8,29},{9,1},... | collective-permute-start | bytes 393224 | tf_op jit(solution)/shard_map/ppermute | solution.py:592
  96.2 11.9 %collective-permute-start.28 = (bf16[512,128]{1,0:T(8,128)(2,1)S(1)}, bf16[512,128]{1,0:T(8,128)(2,1)S(1)}, u32[]{:S(2)}, u32[]{:S(2)}) collective-permute-start(bf16[512,128]{1,0:T(8,128)(2,1)S(1)} %get-tuple-element.183), channel_id=1, source_target_pairs={{0,12},{1,0},{2,16},{3,28},{4,8},{5,4},{6,20},{7,24},{8,25},{9,21}... | collective-permute-start | bytes 393224 | tf_op jit(solution)/shard_map/ppermute | solution.py:592
  102.8 9.8 %collective-permute-start.29 = (bf16[512,128]{1,0:T(8,128)(2,1)S(1)}, bf16[512,128]{1,0:T(8,128)(2,1)S(1)}, u32[]{:S(2)}, u32[]{:S(2)}) collective-permute-start(bf16[512,128]{1,0:T(8,128)(2,1)S(1)} %get-tuple-element.184), channel_id=1, source_target_pairs={{0,0},{1,12},{2,28},{3,16},{4,4},{5,8},{6,24},{7,20},{8,21},{9,25}... | collective-permute-start | bytes 393224 | tf_op jit(solution)/shard_map/ppermute | solution.py:592
  (13 other events, 108.2 us)

commit v5 on v4

--- a/solution.py
+++ b/solution.py
@@ -189,7 +189,7 @@
         out_shape=shapes,
         scratch_shapes=scratch,
         input_output_aliases=aliases,
-        compiler_params=params(24 if closing else 16),
+        compiler_params=params(14),
         cost_estimate=pl.CostEstimate(flops=int(units * 0.6e9), bytes_accessed=0, transcendentals=0),
         name="close_blocks" if closing else "add_blocks",
     )(info, *mine, *other, *mats, table, *old, *ends)
@@ -575,7 +575,7 @@
     other.append(swap(mine[-1]))
 
     kept, sent, states = [None] * len(pairs), [None] * len(pairs), [None] * count
-    for pair in [*sorted(pairs)[1:], sorted(pairs)[0]]:
+    for pair in pairs:
         use = {s: [n for n in range(5) if n not in done_sets.get(s, ())] for s in pair}
         keep, *send = run(list(pair), use, pairs.index(pair))
         send, state = send[:-2], send[-2:]

time: 114 us -> 114 us (level)
  no operation moved by 1% of the time
where the time goes in v5:
time: 114 us
  Pallas kernels  50.9 us (45%)
  waiting for transfers between devices  32.9 us (29%)
  starting transfers between devices  27.7 us (24%)
  local copies, waits for them, and re-layouts  1.89 us (2%)
    pallas_call x7, Pallas kernels, add_blocks(): pl.pallas_call(functools.partial(blocks_kernel, blocks, sets, work, info_...  39.2 us
    ppermute x3, waiting for transfers between devices, per_device(): lax.ppermute(going_right, 'ctx', right)  15.7 us
    ppermute x4, starting transfers between devices, per_device(): lax.ppermute(v, ('ctx', 'grp'), moves)  11.2 us
    ppermute x18, starting transfers between devices, shift_of(): lax.ppermute(x, 'grp', [(rank(w, h), rank(w + by_way, h ^ by_core)) for w...  8.36 us
    ppermute x4, waiting for transfers between devices, per_device(): lax.ppermute(v, ('ctx', 'grp'), moves)  7.92 us
    pallas_call x2, Pallas kernels, cut(): pl.pallas_call(functools.partial(cut_kernel, to), in_specs=[ANY], out_spe...  5.82 us
    ppermute x3, waiting for transfers between devices, per_device(): lax.ppermute(going_left, 'ctx', left)  4.96 us
    ppermute x3, starting transfers between devices, per_device(): lax.ppermute(going_right, 'ctx', right)  4.78 us
  transfers between devices with their start and end apart: 30, of which 10 were waited for; matrix products, arithmetic and copies ran while one was open for 1% of the time, Pallas kernels for 40%

profile of v5, /device:TPU:4, one launch (start us, length us, event | category | flops | bytes accessed | tf_op | source)
XLA Modules:
  0.0 114.0 jit_solution(4841192439968073990)
XLA Ops:
  0.0 1.6 %collective-permute-start = (bf16[512,512]{1,0:T(8,128)(2,1)}, bf16[512,512]{1,0:T(8,128)(2,1)S(1)}, u32[]{:S(2)}, u32[]{:S(2)}) collective-permute-start(bf16[512,512]{1,0:T(8,128)(2,1)} %refs_0_.3), channel_id=1, source_target_pairs={{0,8},{8,16},{16,24},{24,28},{28,20},{20,12},{12,4},{4,0},{1,9},{9... | collective-permute-start | bytes 1572872 | tf_op jit(solution)/shard_map/ppermute | solution.py:539
  2.0 2.2 %cut_filters.3 = bf16[4,128,1024]{2,1,0:T(8,128)(2,1)} custom-call(bf16[4,256,2048]{2,1,0:T(8,128)(2,1)} %mats.3), custom_call_target="tpu_custom_call" | custom-call | tf_op jit(solution)/shard_map/cut_filters/pallas_call | solution.py:83
  4.4 3.6 %cut_filters.2 = (bf16[2,128,1024]{2,1,0:T(8,128)(2,1)}, bf16[2,128,1024]{2,1,0:T(8,128)(2,1)}, bf16[4,128,1024]{2,1,0:T(8,128)(2,1)}, bf16[4,128,1024]{2,1,0:T(8,128)(2,1)}) custom-call(bf16[4,256,2048]{2,1,0:T(8,128)(2,1)} %mats.3), custom_call_target="tpu_custom_call" | custom-call | tf_op jit(solution)/shard_map/cut_filters/pallas_call | solution.py:83
  8.7 5.2 %collective-permute-done.refs_1_.refs_0_ = bf16[512,512]{1,0:T(8,128)(2,1)S(1)} collective-permute-done((bf16[512,512]{1,0:T(8,128)(2,1)}, bf16[512,512]{1,0:T(8,128)(2,1)S(1)}, u32[]{:S(2)}, u32[]{:S(2)}) %collective-permute-start) | collective-permute-done | bytes 524320 | tf_op jit(solution)/shard_map/ppermute | solution.py:539
  15.2 1.6 %collective-permute-start.3 = (bf16[512,512]{1,0:T(8,128)(2,1)S(1)}, bf16[512,512]{1,0:T(8,128)(2,1)S(1)}, u32[]{:S(2)}, u32[]{:S(2)}) collective-permute-start(bf16[512,512]{1,0:T(8,128)(2,1)S(1)} %collective-permute-done.refs_1_.refs_0_), channel_id=1, source_target_pairs={{0,8},{8,16},{16,24},{24,28},{28,20},{20,12},{12,4},{4,0},{1,9},{9... | collective-permute-start | bytes 1572872 | tf_op jit(solution)/shard_map/ppermute | solution.py:539
  17.9 9.7 %collective-permute-done.3.refs_0_ = bf16[512,512]{1,0:T(8,128)(2,1)S(1)} collective-permute-done((bf16[512,512]{1,0:T(8,128)(2,1)S(1)}, bf16[512,512]{1,0:T(8,128)(2,1)S(1)}, u32[]{:S(2)}, u32[]{:S(2)}) %collective-permute-start.3) | collective-permute-done | bytes 524320 | tf_op jit(solution)/shard_map/ppermute | solution.py:539
  30.1 1.9 %pole_tables.1.refs_10_.refs_8_.refs_5_.refs_9_ = bf16[8,208,512]{2,1,0:T(8,128)(2,1)S(1)} custom-call(f32[80,18]{1,0:T(8,128)S(1)} %copy.14.poles_ref), custom_call_target="tpu_custom_call" | custom-call | flops 4000000000 | tf_op jit(solution)/shard_map/pole_tables/pallas_call | solution.py:55
  32.1 1.6 %collective-permute-start.11 = (bf16[512,512]{1,0:T(8,128)(2,1)S(1)}, bf16[512,512]{1,0:T(8,128)(2,1)S(1)}, u32[]{:S(2)}, u32[]{:S(2)}) collective-permute-start(bf16[512,512]{1,0:T(8,128)(2,1)S(1)} %collective-permute-done.3.refs_0_), channel_id=1, source_target_pairs={{0,8},{8,16},{16,24},{24,28},{28,20},{20,12},{12,4},{4,0},{1,9},{9... | collective-permute-start | bytes 1572872 | tf_op jit(solution)/shard_map/ppermute | solution.py:539
  34.8 10.1 %add_blocks.3 = (f32[208,512]{1,0:T(8,128)S(1)}, f32[208,512]{1,0:T(8,128)S(1)}, f32[208,512]{1,0:T(8,128)S(1)}) custom-call(s32[30]{0:T(128)S(1)} %dynamic-slice_bitcast_fusion.info, bf16[512,512]{1,0:T(8,128)(2,1)S(1)} %copy-done.1, bf16[512,512]{1,0:T(8,128)(2,1)S(1)} %collective-permute-done.refs_1_.refs_0_, ...), custom_call_target="tpu_custom_call" | custom-call | flops 10800000000 | tf_op jit(solution)/shard_map/add_blocks/pallas_call | solution.py:185
  45.7 2.4 %collective-permute-done.12.refs_1_ = bf16[512,512]{1,0:T(8,128)(2,1)S(1)} collective-permute-done((bf16[512,512]{1,0:T(8,128)(2,1)S(1)}, bf16[512,512]{1,0:T(8,128)(2,1)S(1)}, u32[]{:S(2)}, u32[]{:S(2)}) %collective-permute-start.12) | collective-permute-done | bytes 524320 | tf_op jit(solution)/shard_map/ppermute | solution.py:539
  50.8 6.9 %add_blocks.4 = (f32[208,512]{1,0:T(8,128)S(1)}, f32[208,512]{1,0:T(8,128)S(1)}) custom-call(s32[30]{0:T(128)S(1)} %dynamic-slice_bitcast_fusion.info, bf16[512,512]{1,0:T(8,128)(2,1)S(1)} %collective-permute-done.3.refs_0_, bf16[512,512]{1,0:T(8,128)(2,1)S(1)} %copy-done.3, bf16[512,512]{1,0:T(8,128)(2,1)S(1)} %collective-permute-done.13.refs_2_, ...), custom_call_target="tpu_custom_call" | custom-call | flops 7200000000 | tf_op jit(solution)/shard_map/add_blocks/pallas_call | solution.py:185
  57.7 2.6 %add_blocks.5 = (f32[208,512]{1,0:T(8,128)S(1)}, f32[208,512]{1,0:T(8,128)S(1)}) custom-call(s32[30]{0:T(128)S(1)} %dynamic-slice_bitcast_fusion.info, bf16[512,512]{1,0:T(8,128)(2,1)S(1)} %collective-permute-done.11.refs_0_, bf16[512,512]{1,0:T(8,128)(2,1)S(1)} %collective-permute-done.12.refs_1_, bf16[512,512]{1,0:T(8,128)(2,1)S(1)} %collective-permute-done.17.refs_2_, ...), custom_call_target="tpu_custom_call" | custom-call | flops 2400000000 | tf_op jit(solution)/shard_map/add_blocks/pallas_call | solution.py:185
  60.3 3.4 %close_blocks.4 = (f32[512,128]{1,0:T(8,128)S(1)}, f32[512,128]{1,0:T(8,128)S(1)}, f32[80,128]{1,0:T(8,128)S(1)}, f32[80,128]{1,0:T(8,128)S(1)}) custom-call(s32[30]{0:T(128)S(1)} %dynamic-slice_bitcast_fusion.info, bf16[512,512]{1,0:T(8,128)(2,1)S(1)} %collective-permute-done.refs_1_.refs_0_, bf16[512,512]{1,0:T(8,128)(2,1)S(1)} %collective-permute-done.1.refs_2_.refs_1_, ...), custom_call_target="tpu_custom_call" | custom-call | flops 2400000000 | tf_op jit(solution)/shard_map/close_blocks/pallas_call | solution.py:185
  64.5 7.1 %close_blocks.5 = (f32[512,128]{1,0:T(8,128)S(1)}, f32[512,128]{1,0:T(8,128)S(1)}, f32[80,128]{1,0:T(8,128)S(1)}, f32[80,128]{1,0:T(8,128)S(1)}) custom-call(s32[30]{0:T(128)S(1)} %dynamic-slice_bitcast_fusion.info, bf16[512,512]{1,0:T(8,128)(2,1)S(1)} %collective-permute-done.11.refs_0_, bf16[512,512]{1,0:T(8,128)(2,1)S(1)} %collective-permute-done.12.refs_1_, ...), custom_call_target="tpu_custom_call" | custom-call | flops 7200000000 | tf_op jit(solution)/shard_map/close_blocks/pallas_call | solution.py:185
  71.6 1.6 %collective-permute-start.20 = (f32[512,128]{1,0:T(8,128)S(1)}, f32[512,128]{1,0:T(8,128)S(1)}, u32[]{:S(2)}, u32[]{:S(2)}) collective-permute-start(f32[512,128]{1,0:T(8,128)S(1)} %get-tuple-element.159), channel_id=1, source_target_pairs={{0,2},{1,3},{2,0},{3,1},{4,6},{5,7},{6,4},{7,5},{8,10},{9,11},{10,... | collective-permute-start | bytes 786440 | tf_op jit(solution)/shard_map/ppermute | solution.py:344
  73.2 3.0 %close_blocks.7 = (f32[512,128]{1,0:T(8,128)S(1)}, f32[512,128]{1,0:T(8,128)S(1)}, f32[80,128]{1,0:T(8,128)S(1)}, f32[80,128]{1,0:T(8,128)S(1)}) custom-call(s32[30]{0:T(128)S(1)} %dynamic-slice_bitcast_fusion.info, bf16[512,512]{1,0:T(8,128)(2,1)S(1)} %collective-permute-done.3.refs_0_, bf16[512,512]{1,0:T(8,128)(2,1)S(1)} %copy-done.3, ...), custom_call_target="tpu_custom_call" | custom-call | flops 2400000000 | tf_op jit(solution)/shard_map/close_blocks/pallas_call | solution.py:185
  76.7 6.2 %close_blocks.6 = (f32[512,128]{1,0:T(8,128)S(1)}, f32[256,128]{1,0:T(8,128)S(1)}, f32[256,128]{1,0:T(8,128)S(1)}, f32[80,128]{1,0:T(8,128)S(1)}, f32[80,128]{1,0:T(8,128)S(1)}) custom-call(s32[30]{0:T(128)S(1)} %dynamic-slice_bitcast_fusion.info, bf16[512,512]{1,0:T(8,128)(2,1)S(1)} %copy-done.1, ...), custom_call_target="tpu_custom_call" | custom-call | flops 6000000000 | tf_op jit(solution)/shard_map/close_blocks/pallas_call | solution.py:185
  83.6 1.6 %collective-permute-start.22 = (f32[4,80,128]{2,1,0:T(8,128)S(1)}, f32[4,80,128]{2,1,0:T(8,128)S(1)}, u32[]{:S(2)}, u32[]{:S(2)}) collective-permute-start(f32[4,80,128]{2,1,0:T(8,128)S(1)} %get-tuple-element.175), channel_id=1, source_target_pairs={{0,2},{1,3},{2,0},{3,1},{4,6},{5,7},{6,4},{7,5},{8,10},{9,11},{10,... | collective-permute-start | bytes 491528 | tf_op jit(solution)/shard_map/ppermute | solution.py:344
  85.7 1.5 %collective-permute-start.27 = (f32[256,128]{1,0:T(8,128)S(1)}, f32[256,128]{1,0:T(8,128)S(1)}, u32[]{:S(2)}, u32[]{:S(2)}) collective-permute-start(f32[256,128]{1,0:T(8,128)S(1)} %get-tuple-element.182), channel_id=1, source_target_pairs={{0,2},{1,3},{2,0},{3,1},{4,6},{5,7},{6,4},{7,5},{8,10},{9,11},{10,... | collective-permute-start | bytes 393224 | tf_op jit(solution)/shard_map/ppermute | solution.py:344
  87.4 3.4 %collective-permute-done.22.refs_5_.refs_6_ = f32[4,80,128]{2,1,0:T(8,128)S(1)} collective-permute-done((f32[4,80,128]{2,1,0:T(8,128)S(1)}, f32[4,80,128]{2,1,0:T(8,128)S(1)}, u32[]{:S(2)}, u32[]{:S(2)}) %collective-permute-start.22) | collective-permute-done | bytes 163872 | tf_op jit(solution)/shard_map/ppermute | solution.py:344
  96.2 6.5 %collective-permute-start.28 = (bf16[512,128]{1,0:T(8,128)(2,1)S(1)}, bf16[512,128]{1,0:T(8,128)(2,1)S(1)}, u32[]{:S(2)}, u32[]{:S(2)}) collective-permute-start(bf16[512,128]{1,0:T(8,128)(2,1)S(1)} %get-tuple-element.183), channel_id=1, source_target_pairs={{0,12},{1,0},{2,16},{3,28},{4,8},{5,4},{6,20},{7,24},{8,25},{9,21}... | collective-permute-start | bytes 393224 | tf_op jit(solution)/shard_map/ppermute | solution.py:592
  102.7 1.9 %collective-permute-start.29 = (bf16[512,128]{1,0:T(8,128)(2,1)S(1)}, bf16[512,128]{1,0:T(8,128)(2,1)S(1)}, u32[]{:S(2)}, u32[]{:S(2)}) collective-permute-start(bf16[512,128]{1,0:T(8,128)(2,1)S(1)} %get-tuple-element.184), channel_id=1, source_target_pairs={{0,0},{1,12},{2,28},{3,16},{4,4},{5,8},{6,24},{7,20},{8,21},{9,25}... | collective-permute-start | bytes 393224 | tf_op jit(solution)/shard_map/ppermute | solution.py:592
  104.7 3.4 %collective-permute-done.28.refs_2_ = bf16[512,128]{1,0:T(8,128)(2,1)S(1)} collective-permute-done((bf16[512,128]{1,0:T(8,128)(2,1)S(1)}, bf16[512,128]{1,0:T(8,128)(2,1)S(1)}, u32[]{:S(2)}, u32[]{:S(2)}) %collective-permute-start.28) | collective-permute-done | bytes 131104 | tf_op jit(solution)/shard_map/ppermute | solution.py:592
  108.1 4.6 %collective-permute-done.29.refs_3_ = bf16[512,128]{1,0:T(8,128)(2,1)S(1)} collective-permute-done((bf16[512,128]{1,0:T(8,128)(2,1)S(1)}, bf16[512,128]{1,0:T(8,128)(2,1)S(1)}, u32[]{:S(2)}, u32[]{:S(2)}) %collective-permute-start.29) | collective-permute-done | bytes 131104 | tf_op jit(solution)/shard_map/ppermute | solution.py:592
  (78 shorter events, 20.2 us)
Async XLA Ops:
  0.0 13.9 %collective-permute-start = (bf16[512,512]{1,0:T(8,128)(2,1)}, bf16[512,512]{1,0:T(8,128)(2,1)S(1)}, u32[]{:S(2)}, u32[]{:S(2)}) collective-permute-start(bf16[512,512]{1,0:T(8,128)(2,1)} %refs_0_.3), channel_id=1, source_target_pairs={{0,8},{8,16},{16,24},{24,28},{28,20},{20,12},{12,4},{4,0},{1,9},{9... | collective-permute-start | bytes 1572872 | tf_op jit(solution)/shard_map/ppermute | solution.py:539
  1.6 13.6 %collective-permute-start.1 = (bf16[512,512]{1,0:T(8,128)(2,1)}, bf16[512,512]{1,0:T(8,128)(2,1)S(1)}, u32[]{:S(2)}, u32[]{:S(2)}) collective-permute-start(bf16[512,512]{1,0:T(8,128)(2,1)} %refs_0_.3), channel_id=1, source_target_pairs={{8,0},{16,8},{24,16},{28,24},{20,28},{12,20},{4,12},{0,4},{9,1},{1... | collective-permute-start | bytes 1572872 | tf_op jit(solution)/shard_map/ppermute | solution.py:539
  2.0 13.1 %collective-permute-start.2 = (bf16[512,512]{1,0:T(8,128)(2,1)}, bf16[512,512]{1,0:T(8,128)(2,1)S(1)}, u32[]{:S(2)}, u32[]{:S(2)}) collective-permute-start(bf16[512,512]{1,0:T(8,128)(2,1)} %refs_0_.3), channel_id=1, source_target_pairs={{0,1},{1,0},{2,3},{3,2},{4,5},{5,4},{6,7},{7,6},{8,9},{9,8},{10,11... | collective-permute-start | bytes 1572872 | tf_op jit(solution)/shard_map/ppermute | solution.py:344
  4.3 27.8 %collective-permute-start.9 = (bf16[4,128,1024]{2,1,0:T(8,128)(2,1)}, bf16[4,128,1024]{2,1,0:T(8,128)(2,1)S(1)}, u32[]{:S(2)}, u32[]{:S(2)}) collective-permute-start(bf16[4,128,1024]{2,1,0:T(8,128)(2,1)} %cut_filters.3), channel_id=1, source_target_pairs={{0,2},{1,3},{2,0},{3,1},{4,6},{5,7},{6,4},{7,5},{8,10},{9,11},{10,... | collective-permute-start | bytes 3145736 | tf_op jit(solution)/shard_map/ppermute | solution.py:344
  15.2 12.5 %collective-permute-start.3 = (bf16[512,512]{1,0:T(8,128)(2,1)S(1)}, bf16[512,512]{1,0:T(8,128)(2,1)S(1)}, u32[]{:S(2)}, u32[]{:S(2)}) collective-permute-start(bf16[512,512]{1,0:T(8,128)(2,1)S(1)} %collective-permute-done.refs_1_.refs_0_), channel_id=1, source_target_pairs={{0,8},{8,16},{16,24},{24,28},{28,20},{20,12},{12,4},{4,0},{1,9},{9... | collective-permute-start | bytes 1572872 | tf_op jit(solution)/shard_map/ppermute | solution.py:539
  16.8 12.2 %collective-permute-start.4 = (bf16[512,512]{1,0:T(8,128)(2,1)S(1)}, bf16[512,512]{1,0:T(8,128)(2,1)S(1)}, u32[]{:S(2)}, u32[]{:S(2)}) collective-permute-start(bf16[512,512]{1,0:T(8,128)(2,1)S(1)} %collective-permute-done.1.refs_2_.refs_1_), channel_id=1, source_target_pairs={{8,0},{16,8},{24,16},{28,24},{20,28},{12,20},{4,12},{0,4},{9,1},{1... | collective-permute-start | bytes 1572872 | tf_op jit(solution)/shard_map/ppermute | solution.py:539
  17.3 14.7 %collective-permute-start.5 = (bf16[512,512]{1,0:T(8,128)(2,1)S(1)}, bf16[512,512]{1,0:T(8,128)(2,1)}, u32[]{:S(2)}, u32[]{:S(2)}) collective-permute-start(bf16[512,512]{1,0:T(8,128)(2,1)S(1)} %collective-permute-done.refs_1_.refs_0_), channel_id=1, source_target_pairs={{0,1},{1,0},{2,3},{3,2},{4,5},{5,4},{6,7},{7,6},{8,9},{9,8},{10,11... | collective-permute-start | bytes 1572872 | tf_op jit(solution)/shard_map/ppermute | solution.py:344
  17.4 14.6 %collective-permute-start.6 = (bf16[512,512]{1,0:T(8,128)(2,1)S(1)}, bf16[512,512]{1,0:T(8,128)(2,1)}, u32[]{:S(2)}, u32[]{:S(2)}) collective-permute-start(bf16[512,512]{1,0:T(8,128)(2,1)S(1)} %collective-permute-done.1.refs_2_.refs_1_), channel_id=1, source_target_pairs={{0,1},{1,0},{2,3},{3,2},{4,5},{5,4},{6,7},{7,6},{8,9},{9,8},{10,11... | collective-permute-start | bytes 1572872 | tf_op jit(solution)/shard_map/ppermute | solution.py:344
  32.1 13.6 %collective-permute-start.11 = (bf16[512,512]{1,0:T(8,128)(2,1)S(1)}, bf16[512,512]{1,0:T(8,128)(2,1)S(1)}, u32[]{:S(2)}, u32[]{:S(2)}) collective-permute-start(bf16[512,512]{1,0:T(8,128)(2,1)S(1)} %collective-permute-done.3.refs_0_), channel_id=1, source_target_pairs={{0,8},{8,16},{16,24},{24,28},{28,20},{20,12},{12,4},{4,0},{1,9},{9... | collective-permute-start | bytes 1572872 | tf_op jit(solution)/shard_map/ppermute | solution.py:539
  33.7 14.3 %collective-permute-start.13 = (bf16[512,512]{1,0:T(8,128)(2,1)S(1)}, bf16[512,512]{1,0:T(8,128)(2,1)S(1)}, u32[]{:S(2)}, u32[]{:S(2)}) collective-permute-start(bf16[512,512]{1,0:T(8,128)(2,1)S(1)} %collective-permute-done.3.refs_0_), channel_id=1, source_target_pairs={{0,1},{1,0},{2,3},{3,2},{4,5},{5,4},{6,7},{7,6},{8,9},{9,8},{10,11... | collective-permute-start | bytes 1572872 | tf_op jit(solution)/shard_map/ppermute | solution.py:344
  33.7 14.3 %collective-permute-start.12 = (bf16[512,512]{1,0:T(8,128)(2,1)S(1)}, bf16[512,512]{1,0:T(8,128)(2,1)S(1)}, u32[]{:S(2)}, u32[]{:S(2)}) collective-permute-start(bf16[512,512]{1,0:T(8,128)(2,1)S(1)} %copy-done.3), channel_id=1, source_target_pairs={{8,0},{16,8},{24,16},{28,24},{20,28},{12,20},{4,12},{0,4},{9,1},{1... | collective-permute-start | bytes 1572872 | tf_op jit(solution)/shard_map/ppermute | solution.py:539
  34.1 13.9 %collective-permute-start.14 = (bf16[512,512]{1,0:T(8,128)(2,1)S(1)}, bf16[512,512]{1,0:T(8,128)(2,1)S(1)}, u32[]{:S(2)}, u32[]{:S(2)}) collective-permute-start(bf16[512,512]{1,0:T(8,128)(2,1)S(1)} %copy-done.3), channel_id=1, source_target_pairs={{0,1},{1,0},{2,3},{3,2},{4,5},{5,4},{6,7},{7,6},{8,9},{9,8},{10,11... | collective-permute-start | bytes 1572872 | tf_op jit(solution)/shard_map/ppermute | solution.py:344
  34.4 25.9 %collective-permute-start.10 = (bf16[4,128,1024]{2,1,0:T(8,128)(2,1)S(1)}, bf16[4,128,1024]{2,1,0:T(8,128)(2,1)S(1)}, u32[]{:S(2)}, u32[]{:S(2)}) collective-permute-start(bf16[4,128,1024]{2,1,0:T(8,128)(2,1)S(1)} %copy-done.6), channel_id=1, source_target_pairs={{0,3},{1,2},{2,1},{3,0},{4,7},{5,6},{6,5},{7,4},{8,11},{9,10},{10,... | collective-permute-start | bytes 3145736 | tf_op jit(solution)/shard_map/ppermute | solution.py:344
  48.1 9.6 %collective-permute-start.17 = (bf16[512,512]{1,0:T(8,128)(2,1)S(1)}, bf16[512,512]{1,0:T(8,128)(2,1)S(1)}, u32[]{:S(2)}, u32[]{:S(2)}) collective-permute-start(bf16[512,512]{1,0:T(8,128)(2,1)S(1)} %collective-permute-done.11.refs_0_), channel_id=1, source_target_pairs={{0,1},{1,0},{2,3},{3,2},{4,5},{5,4},{6,7},{7,6},{8,9},{9,8},{10,11... | collective-permute-start | bytes 1572872 | tf_op jit(solution)/shard_map/ppermute | solution.py:344
  48.7 11.6 %collective-permute-start.15 = (bf16[256,512]{1,0:T(8,128)(2,1)S(1)}, bf16[256,512]{1,0:T(8,128)(2,1)S(1)}, u32[]{:S(2)}, u32[]{:S(2)}) collective-permute-start(bf16[256,512]{1,0:T(8,128)(2,1)S(1)} %slice.6), channel_id=1, source_target_pairs={{0,8},{8,16},{16,24},{24,28},{28,20},{20,12},{12,4},{4,0},{1,9},{9... | collective-permute-start | bytes 786440 | tf_op jit(solution)/shard_map/ppermute | solution.py:542
  50.2 10.1 %collective-permute-start.16 = (bf16[256,512]{1,0:T(8,128)(2,1)S(1)}, bf16[256,512]{1,0:T(8,128)(2,1)S(1)}, u32[]{:S(2)}, u32[]{:S(2)}) collective-permute-start(bf16[256,512]{1,0:T(8,128)(2,1)S(1)} %slice.7), channel_id=1, source_target_pairs={{8,0},{16,8},{24,16},{28,24},{20,28},{12,20},{4,12},{0,4},{9,1},{1... | collective-permute-start | bytes 786440 | tf_op jit(solution)/shard_map/ppermute | solution.py:543
  63.8 21.9 %collective-permute-start.19 = (f32[512,128]{1,0:T(8,128)S(1)}, f32[512,128]{1,0:T(8,128)S(1)}, u32[]{:S(2)}, u32[]{:S(2)}) collective-permute-start(f32[512,128]{1,0:T(8,128)S(1)} %get-tuple-element.158), channel_id=1, source_target_pairs={{0,2},{1,3},{2,0},{3,1},{4,6},{5,7},{6,4},{7,5},{8,10},{9,11},{10,... | collective-permute-start | bytes 786440 | tf_op jit(solution)/shard_map/ppermute | solution.py:344
  64.4 12.3 %collective-permute-start.21 = (bf16[512,512]{1,0:T(8,128)(2,1)S(1)}, bf16[512,512]{1,0:T(8,128)(2,1)S(1)}, u32[]{:S(2)}, u32[]{:S(2)}) collective-permute-start(bf16[512,512]{1,0:T(8,128)(2,1)S(1)} %constant_dynamic-update-slice_fusion.refs_1_), channel_id=1, source_target_pairs={{0,1},{1,0},{2,3},{3,2},{4,5},{5,4},{6,7},{7,6},{8,9},{9,8},{10,11... | collective-permute-start | bytes 1572872 | tf_op jit(solution)/shard_map/ppermute | solution.py:344
  71.6 15.8 %collective-permute-start.20 = (f32[512,128]{1,0:T(8,128)S(1)}, f32[512,128]{1,0:T(8,128)S(1)}, u32[]{:S(2)}, u32[]{:S(2)}) collective-permute-start(f32[512,128]{1,0:T(8,128)S(1)} %get-tuple-element.159), channel_id=1, source_target_pairs={{0,2},{1,3},{2,0},{3,1},{4,6},{5,7},{6,4},{7,5},{8,10},{9,11},{10,... | collective-permute-start | bytes 786440 | tf_op jit(solution)/shard_map/ppermute | solution.py:344
  76.2 18.2 %collective-permute-start.25 = (f32[512,128]{1,0:T(8,128)S(1)}, f32[512,128]{1,0:T(8,128)S(1)}, u32[]{:S(2)}, u32[]{:S(2)}) collective-permute-start(f32[512,128]{1,0:T(8,128)S(1)} %get-tuple-element.180), channel_id=1, source_target_pairs={{0,2},{1,3},{2,0},{3,1},{4,6},{5,7},{6,4},{7,5},{8,10},{9,11},{10,... | collective-permute-start | bytes 786440 | tf_op jit(solution)/shard_map/ppermute | solution.py:344
  91.7 13.0 %collective-permute-start.23 = (bf16[512,128]{1,0:T(8,128)(2,1)S(1)}, bf16[512,128]{1,0:T(8,128)(2,1)S(1)}, u32[]{:S(2)}, u32[]{:S(2)}) collective-permute-start(bf16[512,128]{1,0:T(8,128)(2,1)S(1)} %get-tuple-element.176), channel_id=1, source_target_pairs={{0,8},{1,20},{2,4},{3,24},{4,12},{5,16},{6,0},{7,28},{8,1},{9,29},... | collective-permute-start | bytes 393224 | tf_op jit(solution)/shard_map/ppermute | solution.py:592
  93.1 11.6 %collective-permute-start.24 = (bf16[512,128]{1,0:T(8,128)(2,1)S(1)}, bf16[512,128]{1,0:T(8,128)(2,1)S(1)}, u32[]{:S(2)}, u32[]{:S(2)}) collective-permute-start(bf16[512,128]{1,0:T(8,128)(2,1)S(1)} %get-tuple-element.177), channel_id=1, source_target_pairs={{0,20},{1,8},{2,24},{3,4},{4,16},{5,12},{6,28},{7,0},{8,29},{9,1},... | collective-permute-start | bytes 393224 | tf_op jit(solution)/shard_map/ppermute | solution.py:592
  96.2 11.9 %collective-permute-start.28 = (bf16[512,128]{1,0:T(8,128)(2,1)S(1)}, bf16[512,128]{1,0:T(8,128)(2,1)S(1)}, u32[]{:S(2)}, u32[]{:S(2)}) collective-permute-start(bf16[512,128]{1,0:T(8,128)(2,1)S(1)} %get-tuple-element.183), channel_id=1, source_target_pairs={{0,12},{1,0},{2,16},{3,28},{4,8},{5,4},{6,20},{7,24},{8,25},{9,21}... | collective-permute-start | bytes 393224 | tf_op jit(solution)/shard_map/ppermute | solution.py:592
  102.7 9.9 %collective-permute-start.29 = (bf16[512,128]{1,0:T(8,128)(2,1)S(1)}, bf16[512,128]{1,0:T(8,128)(2,1)S(1)}, u32[]{:S(2)}, u32[]{:S(2)}) collective-permute-start(bf16[512,128]{1,0:T(8,128)(2,1)S(1)} %get-tuple-element.184), channel_id=1, source_target_pairs={{0,0},{1,12},{2,28},{3,16},{4,4},{5,8},{6,24},{7,20},{8,21},{9,25}... | collective-permute-start | bytes 393224 | tf_op jit(solution)/shard_map/ppermute | solution.py:592
  (13 other events, 108.2 us)

commit v6 on v5

--- a/solution.py
+++ b/solution.py
@@ -190,7 +190,7 @@
         scratch_shapes=scratch,
         input_output_aliases=aliases,
         compiler_params=params(14),
-        cost_estimate=pl.CostEstimate(flops=int(units * 0.6e9), bytes_accessed=0, transcendentals=0),
+        cost_estimate=pl.CostEstimate(flops=int(units * 1.0e9), bytes_accessed=0, transcendentals=0),
         name="close_blocks" if closing else "add_blocks",
     )(info, *mine, *other, *mats, table, *old, *ends)
 

time: 114 us -> 114 us (level)
  no operation moved by 1% of the time
where the time goes in v6:
time: 114 us
  Pallas kernels  50.9 us (45%)
  waiting for transfers between devices  32.9 us (29%)
  starting transfers between devices  27.7 us (24%)
  local copies, waits for them, and re-layouts  1.89 us (2%)
    pallas_call x7, Pallas kernels, add_blocks(): pl.pallas_call(functools.partial(blocks_kernel, blocks, sets, work, info_...  39.2 us
    ppermute x3, waiting for transfers between devices, per_device(): lax.ppermute(going_right, 'ctx', right)  15.7 us
    ppermute x4, starting transfers between devices, per_device(): lax.ppermute(v, ('ctx', 'grp'), moves)  11.2 us
    ppermute x18, starting transfers between devices, shift_of(): lax.ppermute(x, 'grp', [(rank(w, h), rank(w + by_way, h ^ by_core)) for w...  8.36 us
    ppermute x4, waiting for transfers between devices, per_device(): lax.ppermute(v, ('ctx', 'grp'), moves)  7.92 us
    pallas_call x2, Pallas kernels, cut(): pl.pallas_call(functools.partial(cut_kernel, to), in_specs=[ANY], out_spe...  5.82 us
    ppermute x3, waiting for transfers between devices, per_device(): lax.ppermute(going_left, 'ctx', left)  4.96 us
    ppermute x3, starting transfers between devices, per_device(): lax.ppermute(going_right, 'ctx', right)  4.78 us
  transfers between devices with their start and end apart: 30, of which 10 were waited for; matrix products, arithmetic and copies ran while one was open for 1% of the time, Pallas kernels for 40%

profile of v6, /device:TPU:4, one launch (start us, length us, event | category | flops | bytes accessed | tf_op | source)
XLA Modules:
  0.0 114.0 jit_solution(4841192439968073990)
XLA Ops:
  0.0 1.6 %collective-permute-start = (bf16[512,512]{1,0:T(8,128)(2,1)}, bf16[512,512]{1,0:T(8,128)(2,1)S(1)}, u32[]{:S(2)}, u32[]{:S(2)}) collective-permute-start(bf16[512,512]{1,0:T(8,128)(2,1)} %refs_0_.3), channel_id=1, source_target_pairs={{0,8},{8,16},{16,24},{24,28},{28,20},{20,12},{12,4},{4,0},{1,9},{9... | collective-permute-start | bytes 1572872 | tf_op jit(solution)/shard_map/ppermute | solution.py:539
  2.0 2.2 %cut_filters.3 = bf16[4,128,1024]{2,1,0:T(8,128)(2,1)} custom-call(bf16[4,256,2048]{2,1,0:T(8,128)(2,1)} %mats.3), custom_call_target="tpu_custom_call" | custom-call | tf_op jit(solution)/shard_map/cut_filters/pallas_call | solution.py:83
  4.4 3.6 %cut_filters.2 = (bf16[2,128,1024]{2,1,0:T(8,128)(2,1)}, bf16[2,128,1024]{2,1,0:T(8,128)(2,1)}, bf16[4,128,1024]{2,1,0:T(8,128)(2,1)}, bf16[4,128,1024]{2,1,0:T(8,128)(2,1)}) custom-call(bf16[4,256,2048]{2,1,0:T(8,128)(2,1)} %mats.3), custom_call_target="tpu_custom_call" | custom-call | tf_op jit(solution)/shard_map/cut_filters/pallas_call | solution.py:83
  8.7 5.2 %collective-permute-done.refs_1_.refs_0_ = bf16[512,512]{1,0:T(8,128)(2,1)S(1)} collective-permute-done((bf16[512,512]{1,0:T(8,128)(2,1)}, bf16[512,512]{1,0:T(8,128)(2,1)S(1)}, u32[]{:S(2)}, u32[]{:S(2)}) %collective-permute-start) | collective-permute-done | bytes 524320 | tf_op jit(solution)/shard_map/ppermute | solution.py:539
  15.2 1.6 %collective-permute-start.3 = (bf16[512,512]{1,0:T(8,128)(2,1)S(1)}, bf16[512,512]{1,0:T(8,128)(2,1)S(1)}, u32[]{:S(2)}, u32[]{:S(2)}) collective-permute-start(bf16[512,512]{1,0:T(8,128)(2,1)S(1)} %collective-permute-done.refs_1_.refs_0_), channel_id=1, source_target_pairs={{0,8},{8,16},{16,24},{24,28},{28,20},{20,12},{12,4},{4,0},{1,9},{9... | collective-permute-start | bytes 1572872 | tf_op jit(solution)/shard_map/ppermute | solution.py:539
  17.9 9.7 %collective-permute-done.3.refs_0_ = bf16[512,512]{1,0:T(8,128)(2,1)S(1)} collective-permute-done((bf16[512,512]{1,0:T(8,128)(2,1)S(1)}, bf16[512,512]{1,0:T(8,128)(2,1)S(1)}, u32[]{:S(2)}, u32[]{:S(2)}) %collective-permute-start.3) | collective-permute-done | bytes 524320 | tf_op jit(solution)/shard_map/ppermute | solution.py:539
  30.1 1.9 %pole_tables.1.refs_10_.refs_8_.refs_5_.refs_9_ = bf16[8,208,512]{2,1,0:T(8,128)(2,1)S(1)} custom-call(f32[80,18]{1,0:T(8,128)S(1)} %copy.14.poles_ref), custom_call_target="tpu_custom_call" | custom-call | flops 4000000000 | tf_op jit(solution)/shard_map/pole_tables/pallas_call | solution.py:55
  32.1 1.6 %collective-permute-start.11 = (bf16[512,512]{1,0:T(8,128)(2,1)S(1)}, bf16[512,512]{1,0:T(8,128)(2,1)S(1)}, u32[]{:S(2)}, u32[]{:S(2)}) collective-permute-start(bf16[512,512]{1,0:T(8,128)(2,1)S(1)} %collective-permute-done.3.refs_0_), channel_id=1, source_target_pairs={{0,8},{8,16},{16,24},{24,28},{28,20},{20,12},{12,4},{4,0},{1,9},{9... | collective-permute-start | bytes 1572872 | tf_op jit(solution)/shard_map/ppermute | solution.py:539
  34.8 10.1 %add_blocks.3 = (f32[208,512]{1,0:T(8,128)S(1)}, f32[208,512]{1,0:T(8,128)S(1)}, f32[208,512]{1,0:T(8,128)S(1)}) custom-call(s32[30]{0:T(128)S(1)} %dynamic-slice_bitcast_fusion.info, bf16[512,512]{1,0:T(8,128)(2,1)S(1)} %copy-done.1, bf16[512,512]{1,0:T(8,128)(2,1)S(1)} %collective-permute-done.refs_1_.refs_0_, ...), custom_call_target="tpu_custom_call" | custom-call | flops 17999998976 | tf_op jit(solution)/shard_map/add_blocks/pallas_call | solution.py:185
  45.7 2.4 %collective-permute-done.12.refs_1_ = bf16[512,512]{1,0:T(8,128)(2,1)S(1)} collective-permute-done((bf16[512,512]{1,0:T(8,128)(2,1)S(1)}, bf16[512,512]{1,0:T(8,128)(2,1)S(1)}, u32[]{:S(2)}, u32[]{:S(2)}) %collective-permute-start.12) | collective-permute-done | bytes 524320 | tf_op jit(solution)/shard_map/ppermute | solution.py:539
  50.8 6.9 %add_blocks.4 = (f32[208,512]{1,0:T(8,128)S(1)}, f32[208,512]{1,0:T(8,128)S(1)}) custom-call(s32[30]{0:T(128)S(1)} %dynamic-slice_bitcast_fusion.info, bf16[512,512]{1,0:T(8,128)(2,1)S(1)} %collective-permute-done.3.refs_0_, bf16[512,512]{1,0:T(8,128)(2,1)S(1)} %copy-done.3, bf16[512,512]{1,0:T(8,128)(2,1)S(1)} %collective-permute-done.13.refs_2_, ...), custom_call_target="tpu_custom_call" | custom-call | flops 12000000000 | tf_op jit(solution)/shard_map/add_blocks/pallas_call | solution.py:185
  57.7 2.6 %add_blocks.5 = (f32[208,512]{1,0:T(8,128)S(1)}, f32[208,512]{1,0:T(8,128)S(1)}) custom-call(s32[30]{0:T(128)S(1)} %dynamic-slice_bitcast_fusion.info, bf16[512,512]{1,0:T(8,128)(2,1)S(1)} %collective-permute-done.11.refs_0_, bf16[512,512]{1,0:T(8,128)(2,1)S(1)} %collective-permute-done.12.refs_1_, bf16[512,512]{1,0:T(8,128)(2,1)S(1)} %collective-permute-done.17.refs_2_, ...), custom_call_target="tpu_custom_call" | custom-call | flops 4000000000 | tf_op jit(solution)/shard_map/add_blocks/pallas_call | solution.py:185
  60.3 3.4 %close_blocks.4 = (f32[512,128]{1,0:T(8,128)S(1)}, f32[512,128]{1,0:T(8,128)S(1)}, f32[80,128]{1,0:T(8,128)S(1)}, f32[80,128]{1,0:T(8,128)S(1)}) custom-call(s32[30]{0:T(128)S(1)} %dynamic-slice_bitcast_fusion.info, bf16[512,512]{1,0:T(8,128)(2,1)S(1)} %collective-permute-done.refs_1_.refs_0_, bf16[512,512]{1,0:T(8,128)(2,1)S(1)} %collective-permute-done.1.refs_2_.refs_1_, ...), custom_call_target="tpu_custom_call" | custom-call | flops 4000000000 | tf_op jit(solution)/shard_map/close_blocks/pallas_call | solution.py:185
  64.5 7.1 %close_blocks.5 = (f32[512,128]{1,0:T(8,128)S(1)}, f32[512,128]{1,0:T(8,128)S(1)}, f32[80,128]{1,0:T(8,128)S(1)}, f32[80,128]{1,0:T(8,128)S(1)}) custom-call(s32[30]{0:T(128)S(1)} %dynamic-slice_bitcast_fusion.info, bf16[512,512]{1,0:T(8,128)(2,1)S(1)} %collective-permute-done.11.refs_0_, bf16[512,512]{1,0:T(8,128)(2,1)S(1)} %collective-permute-done.12.refs_1_, ...), custom_call_target="tpu_custom_call" | custom-call | flops 12000000000 | tf_op jit(solution)/shard_map/close_blocks/pallas_call | solution.py:185
  71.6 1.6 %collective-permute-start.20 = (f32[512,128]{1,0:T(8,128)S(1)}, f32[512,128]{1,0:T(8,128)S(1)}, u32[]{:S(2)}, u32[]{:S(2)}) collective-permute-start(f32[512,128]{1,0:T(8,128)S(1)} %get-tuple-element.159), channel_id=1, source_target_pairs={{0,2},{1,3},{2,0},{3,1},{4,6},{5,7},{6,4},{7,5},{8,10},{9,11},{10,... | collective-permute-start | bytes 786440 | tf_op jit(solution)/shard_map/ppermute | solution.py:344
  73.2 3.0 %close_blocks.7 = (f32[512,128]{1,0:T(8,128)S(1)}, f32[512,128]{1,0:T(8,128)S(1)}, f32[80,128]{1,0:T(8,128)S(1)}, f32[80,128]{1,0:T(8,128)S(1)}) custom-call(s32[30]{0:T(128)S(1)} %dynamic-slice_bitcast_fusion.info, bf16[512,512]{1,0:T(8,128)(2,1)S(1)} %collective-permute-done.3.refs_0_, bf16[512,512]{1,0:T(8,128)(2,1)S(1)} %copy-done.3, ...), custom_call_target="tpu_custom_call" | custom-call | flops 4000000000 | tf_op jit(solution)/shard_map/close_blocks/pallas_call | solution.py:185
  76.7 6.2 %close_blocks.6 = (f32[512,128]{1,0:T(8,128)S(1)}, f32[256,128]{1,0:T(8,128)S(1)}, f32[256,128]{1,0:T(8,128)S(1)}, f32[80,128]{1,0:T(8,128)S(1)}, f32[80,128]{1,0:T(8,128)S(1)}) custom-call(s32[30]{0:T(128)S(1)} %dynamic-slice_bitcast_fusion.info, bf16[512,512]{1,0:T(8,128)(2,1)S(1)} %copy-done.1, ...), custom_call_target="tpu_custom_call" | custom-call | flops 10000000000 | tf_op jit(solution)/shard_map/close_blocks/pallas_call | solution.py:185
  83.6 1.6 %collective-permute-start.22 = (f32[4,80,128]{2,1,0:T(8,128)S(1)}, f32[4,80,128]{2,1,0:T(8,128)S(1)}, u32[]{:S(2)}, u32[]{:S(2)}) collective-permute-start(f32[4,80,128]{2,1,0:T(8,128)S(1)} %get-tuple-element.175), channel_id=1, source_target_pairs={{0,2},{1,3},{2,0},{3,1},{4,6},{5,7},{6,4},{7,5},{8,10},{9,11},{10,... | collective-permute-start | bytes 491528 | tf_op jit(solution)/shard_map/ppermute | solution.py:344
  85.7 1.5 %collective-permute-start.27 = (f32[256,128]{1,0:T(8,128)S(1)}, f32[256,128]{1,0:T(8,128)S(1)}, u32[]{:S(2)}, u32[]{:S(2)}) collective-permute-start(f32[256,128]{1,0:T(8,128)S(1)} %get-tuple-element.182), channel_id=1, source_target_pairs={{0,2},{1,3},{2,0},{3,1},{4,6},{5,7},{6,4},{7,5},{8,10},{9,11},{10,... | collective-permute-start | bytes 393224 | tf_op jit(solution)/shard_map/ppermute | solution.py:344
  87.4 3.4 %collective-permute-done.22.refs_5_.refs_6_ = f32[4,80,128]{2,1,0:T(8,128)S(1)} collective-permute-done((f32[4,80,128]{2,1,0:T(8,128)S(1)}, f32[4,80,128]{2,1,0:T(8,128)S(1)}, u32[]{:S(2)}, u32[]{:S(2)}) %collective-permute-start.22) | collective-permute-done | bytes 163872 | tf_op jit(solution)/shard_map/ppermute | solution.py:344
  96.2 6.5 %collective-permute-start.28 = (bf16[512,128]{1,0:T(8,128)(2,1)S(1)}, bf16[512,128]{1,0:T(8,128)(2,1)S(1)}, u32[]{:S(2)}, u32[]{:S(2)}) collective-permute-start(bf16[512,128]{1,0:T(8,128)(2,1)S(1)} %get-tuple-element.183), channel_id=1, source_target_pairs={{0,12},{1,0},{2,16},{3,28},{4,8},{5,4},{6,20},{7,24},{8,25},{9,21}... | collective-permute-start | bytes 393224 | tf_op jit(solution)/shard_map/ppermute | solution.py:592
  102.7 1.9 %collective-permute-start.29 = (bf16[512,128]{1,0:T(8,128)(2,1)S(1)}, bf16[512,128]{1,0:T(8,128)(2,1)S(1)}, u32[]{:S(2)}, u32[]{:S(2)}) collective-permute-start(bf16[512,128]{1,0:T(8,128)(2,1)S(1)} %get-tuple-element.184), channel_id=1, source_target_pairs={{0,0},{1,12},{2,28},{3,16},{4,4},{5,8},{6,24},{7,20},{8,21},{9,25}... | collective-permute-start | bytes 393224 | tf_op jit(solution)/shard_map/ppermute | solution.py:592
  104.7 3.4 %collective-permute-done.28.refs_2_ = bf16[512,128]{1,0:T(8,128)(2,1)S(1)} collective-permute-done((bf16[512,128]{1,0:T(8,128)(2,1)S(1)}, bf16[512,128]{1,0:T(8,128)(2,1)S(1)}, u32[]{:S(2)}, u32[]{:S(2)}) %collective-permute-start.28) | collective-permute-done | bytes 131104 | tf_op jit(solution)/shard_map/ppermute | solution.py:592
  108.1 4.6 %collective-permute-done.29.refs_3_ = bf16[512,128]{1,0:T(8,128)(2,1)S(1)} collective-permute-done((bf16[512,128]{1,0:T(8,128)(2,1)S(1)}, bf16[512,128]{1,0:T(8,128)(2,1)S(1)}, u32[]{:S(2)}, u32[]{:S(2)}) %collective-permute-start.29) | collective-permute-done | bytes 131104 | tf_op jit(solution)/shard_map/ppermute | solution.py:592
  (78 shorter events, 20.2 us)
Async XLA Ops:
  0.0 13.9 %collective-permute-start = (bf16[512,512]{1,0:T(8,128)(2,1)}, bf16[512,512]{1,0:T(8,128)(2,1)S(1)}, u32[]{:S(2)}, u32[]{:S(2)}) collective-permute-start(bf16[512,512]{1,0:T(8,128)(2,1)} %refs_0_.3), channel_id=1, source_target_pairs={{0,8},{8,16},{16,24},{24,28},{28,20},{20,12},{12,4},{4,0},{1,9},{9... | collective-permute-start | bytes 1572872 | tf_op jit(solution)/shard_map/ppermute | solution.py:539
  1.6 13.6 %collective-permute-start.1 = (bf16[512,512]{1,0:T(8,128)(2,1)}, bf16[512,512]{1,0:T(8,128)(2,1)S(1)}, u32[]{:S(2)}, u32[]{:S(2)}) collective-permute-start(bf16[512,512]{1,0:T(8,128)(2,1)} %refs_0_.3), channel_id=1, source_target_pairs={{8,0},{16,8},{24,16},{28,24},{20,28},{12,20},{4,12},{0,4},{9,1},{1... | collective-permute-start | bytes 1572872 | tf_op jit(solution)/shard_map/ppermute | solution.py:539
  2.0 13.1 %collective-permute-start.2 = (bf16[512,512]{1,0:T(8,128)(2,1)}, bf16[512,512]{1,0:T(8,128)(2,1)S(1)}, u32[]{:S(2)}, u32[]{:S(2)}) collective-permute-start(bf16[512,512]{1,0:T(8,128)(2,1)} %refs_0_.3), channel_id=1, source_target_pairs={{0,1},{1,0},{2,3},{3,2},{4,5},{5,4},{6,7},{7,6},{8,9},{9,8},{10,11... | collective-permute-start | bytes 1572872 | tf_op jit(solution)/shard_map/ppermute | solution.py:344
  4.3 27.8 %collective-permute-start.9 = (bf16[4,128,1024]{2,1,0:T(8,128)(2,1)}, bf16[4,128,1024]{2,1,0:T(8,128)(2,1)S(1)}, u32[]{:S(2)}, u32[]{:S(2)}) collective-permute-start(bf16[4,128,1024]{2,1,0:T(8,128)(2,1)} %cut_filters.3), channel_id=1, source_target_pairs={{0,2},{1,3},{2,0},{3,1},{4,6},{5,7},{6,4},{7,5},{8,10},{9,11},{10,... | collective-permute-start | bytes 3145736 | tf_op jit(solution)/shard_map/ppermute | solution.py:344
  15.2 12.5 %collective-permute-start.3 = (bf16[512,512]{1,0:T(8,128)(2,1)S(1)}, bf16[512,512]{1,0:T(8,128)(2,1)S(1)}, u32[]{:S(2)}, u32[]{:S(2)}) collective-permute-start(bf16[512,512]{1,0:T(8,128)(2,1)S(1)} %collective-permute-done.refs_1_.refs_0_), channel_id=1, source_target_pairs={{0,8},{8,16},{16,24},{24,28},{28,20},{20,12},{12,4},{4,0},{1,9},{9... | collective-permute-start | bytes 1572872 | tf_op jit(solution)/shard_map/ppermute | solution.py:539
  16.8 12.2 %collective-permute-start.4 = (bf16[512,512]{1,0:T(8,128)(2,1)S(1)}, bf16[512,512]{1,0:T(8,128)(2,1)S(1)}, u32[]{:S(2)}, u32[]{:S(2)}) collective-permute-start(bf16[512,512]{1,0:T(8,128)(2,1)S(1)} %collective-permute-done.1.refs_2_.refs_1_), channel_id=1, source_target_pairs={{8,0},{16,8},{24,16},{28,24},{20,28},{12,20},{4,12},{0,4},{9,1},{1... | collective-permute-start | bytes 1572872 | tf_op jit(solution)/shard_map/ppermute | solution.py:539
  17.3 14.7 %collective-permute-start.5 = (bf16[512,512]{1,0:T(8,128)(2,1)S(1)}, bf16[512,512]{1,0:T(8,128)(2,1)}, u32[]{:S(2)}, u32[]{:S(2)}) collective-permute-start(bf16[512,512]{1,0:T(8,128)(2,1)S(1)} %collective-permute-done.refs_1_.refs_0_), channel_id=1, source_target_pairs={{0,1},{1,0},{2,3},{3,2},{4,5},{5,4},{6,7},{7,6},{8,9},{9,8},{10,11... | collective-permute-start | bytes 1572872 | tf_op jit(solution)/shard_map/ppermute | solution.py:344
  17.4 14.6 %collective-permute-start.6 = (bf16[512,512]{1,0:T(8,128)(2,1)S(1)}, bf16[512,512]{1,0:T(8,128)(2,1)}, u32[]{:S(2)}, u32[]{:S(2)}) collective-permute-start(bf16[512,512]{1,0:T(8,128)(2,1)S(1)} %collective-permute-done.1.refs_2_.refs_1_), channel_id=1, source_target_pairs={{0,1},{1,0},{2,3},{3,2},{4,5},{5,4},{6,7},{7,6},{8,9},{9,8},{10,11... | collective-permute-start | bytes 1572872 | tf_op jit(solution)/shard_map/ppermute | solution.py:344
  32.1 13.6 %collective-permute-start.11 = (bf16[512,512]{1,0:T(8,128)(2,1)S(1)}, bf16[512,512]{1,0:T(8,128)(2,1)S(1)}, u32[]{:S(2)}, u32[]{:S(2)}) collective-permute-start(bf16[512,512]{1,0:T(8,128)(2,1)S(1)} %collective-permute-done.3.refs_0_), channel_id=1, source_target_pairs={{0,8},{8,16},{16,24},{24,28},{28,20},{20,12},{12,4},{4,0},{1,9},{9... | collective-permute-start | bytes 1572872 | tf_op jit(solution)/shard_map/ppermute | solution.py:539
  33.7 14.3 %collective-permute-start.13 = (bf16[512,512]{1,0:T(8,128)(2,1)S(1)}, bf16[512,512]{1,0:T(8,128)(2,1)S(1)}, u32[]{:S(2)}, u32[]{:S(2)}) collective-permute-start(bf16[512,512]{1,0:T(8,128)(2,1)S(1)} %collective-permute-done.3.refs_0_), channel_id=1, source_target_pairs={{0,1},{1,0},{2,3},{3,2},{4,5},{5,4},{6,7},{7,6},{8,9},{9,8},{10,11... | collective-permute-start | bytes 1572872 | tf_op jit(solution)/shard_map/ppermute | solution.py:344
  33.7 14.3 %collective-permute-start.12 = (bf16[512,512]{1,0:T(8,128)(2,1)S(1)}, bf16[512,512]{1,0:T(8,128)(2,1)S(1)}, u32[]{:S(2)}, u32[]{:S(2)}) collective-permute-start(bf16[512,512]{1,0:T(8,128)(2,1)S(1)} %copy-done.3), channel_id=1, source_target_pairs={{8,0},{16,8},{24,16},{28,24},{20,28},{12,20},{4,12},{0,4},{9,1},{1... | collective-permute-start | bytes 1572872 | tf_op jit(solution)/shard_map/ppermute | solution.py:539
  34.1 13.9 %collective-permute-start.14 = (bf16[512,512]{1,0:T(8,128)(2,1)S(1)}, bf16[512,512]{1,0:T(8,128)(2,1)S(1)}, u32[]{:S(2)}, u32[]{:S(2)}) collective-permute-start(bf16[512,512]{1,0:T(8,128)(2,1)S(1)} %copy-done.3), channel_id=1, source_target_pairs={{0,1},{1,0},{2,3},{3,2},{4,5},{5,4},{6,7},{7,6},{8,9},{9,8},{10,11... | collective-permute-start | bytes 1572872 | tf_op jit(solution)/shard_map/ppermute | solution.py:344
  34.4 25.9 %collective-permute-start.10 = (bf16[4,128,1024]{2,1,0:T(8,128)(2,1)S(1)}, bf16[4,128,1024]{2,1,0:T(8,128)(2,1)S(1)}, u32[]{:S(2)}, u32[]{:S(2)}) collective-permute-start(bf16[4,128,1024]{2,1,0:T(8,128)(2,1)S(1)} %copy-done.6), channel_id=1, source_target_pairs={{0,3},{1,2},{2,1},{3,0},{4,7},{5,6},{6,5},{7,4},{8,11},{9,10},{10,... | collective-permute-start | bytes 3145736 | tf_op jit(solution)/shard_map/ppermute | solution.py:344
  48.1 9.6 %collective-permute-start.17 = (bf16[512,512]{1,0:T(8,128)(2,1)S(1)}, bf16[512,512]{1,0:T(8,128)(2,1)S(1)}, u32[]{:S(2)}, u32[]{:S(2)}) collective-permute-start(bf16[512,512]{1,0:T(8,128)(2,1)S(1)} %collective-permute-done.11.refs_0_), channel_id=1, source_target_pairs={{0,1},{1,0},{2,3},{3,2},{4,5},{5,4},{6,7},{7,6},{8,9},{9,8},{10,11... | collective-permute-start | bytes 1572872 | tf_op jit(solution)/shard_map/ppermute | solution.py:344
  48.7 11.6 %collective-permute-start.15 = (bf16[256,512]{1,0:T(8,128)(2,1)S(1)}, bf16[256,512]{1,0:T(8,128)(2,1)S(1)}, u32[]{:S(2)}, u32[]{:S(2)}) collective-permute-start(bf16[256,512]{1,0:T(8,128)(2,1)S(1)} %slice.6), channel_id=1, source_target_pairs={{0,8},{8,16},{16,24},{24,28},{28,20},{20,12},{12,4},{4,0},{1,9},{9... | collective-permute-start | bytes 786440 | tf_op jit(solution)/shard_map/ppermute | solution.py:542
  50.2 10.1 %collective-permute-start.16 = (bf16[256,512]{1,0:T(8,128)(2,1)S(1)}, bf16[256,512]{1,0:T(8,128)(2,1)S(1)}, u32[]{:S(2)}, u32[]{:S(2)}) collective-permute-start(bf16[256,512]{1,0:T(8,128)(2,1)S(1)} %slice.7), channel_id=1, source_target_pairs={{8,0},{16,8},{24,16},{28,24},{20,28},{12,20},{4,12},{0,4},{9,1},{1... | collective-permute-start | bytes 786440 | tf_op jit(solution)/shard_map/ppermute | solution.py:543
  63.8 21.9 %collective-permute-start.19 = (f32[512,128]{1,0:T(8,128)S(1)}, f32[512,128]{1,0:T(8,128)S(1)}, u32[]{:S(2)}, u32[]{:S(2)}) collective-permute-start(f32[512,128]{1,0:T(8,128)S(1)} %get-tuple-element.158), channel_id=1, source_target_pairs={{0,2},{1,3},{2,0},{3,1},{4,6},{5,7},{6,4},{7,5},{8,10},{9,11},{10,... | collective-permute-start | bytes 786440 | tf_op jit(solution)/shard_map/ppermute | solution.py:344
  64.4 12.3 %collective-permute-start.21 = (bf16[512,512]{1,0:T(8,128)(2,1)S(1)}, bf16[512,512]{1,0:T(8,128)(2,1)S(1)}, u32[]{:S(2)}, u32[]{:S(2)}) collective-permute-start(bf16[512,512]{1,0:T(8,128)(2,1)S(1)} %constant_dynamic-update-slice_fusion.refs_1_), channel_id=1, source_target_pairs={{0,1},{1,0},{2,3},{3,2},{4,5},{5,4},{6,7},{7,6},{8,9},{9,8},{10,11... | collective-permute-start | bytes 1572872 | tf_op jit(solution)/shard_map/ppermute | solution.py:344
  71.6 15.8 %collective-permute-start.20 = (f32[512,128]{1,0:T(8,128)S(1)}, f32[512,128]{1,0:T(8,128)S(1)}, u32[]{:S(2)}, u32[]{:S(2)}) collective-permute-start(f32[512,128]{1,0:T(8,128)S(1)} %get-tuple-element.159), channel_id=1, source_target_pairs={{0,2},{1,3},{2,0},{3,1},{4,6},{5,7},{6,4},{7,5},{8,10},{9,11},{10,... | collective-permute-start | bytes 786440 | tf_op jit(solution)/shard_map/ppermute | solution.py:344
  76.2 18.2 %collective-permute-start.25 = (f32[512,128]{1,0:T(8,128)S(1)}, f32[512,128]{1,0:T(8,128)S(1)}, u32[]{:S(2)}, u32[]{:S(2)}) collective-permute-start(f32[512,128]{1,0:T(8,128)S(1)} %get-tuple-element.180), channel_id=1, source_target_pairs={{0,2},{1,3},{2,0},{3,1},{4,6},{5,7},{6,4},{7,5},{8,10},{9,11},{10,... | collective-permute-start | bytes 786440 | tf_op jit(solution)/shard_map/ppermute | solution.py:344
  91.7 13.0 %collective-permute-start.23 = (bf16[512,128]{1,0:T(8,128)(2,1)S(1)}, bf16[512,128]{1,0:T(8,128)(2,1)S(1)}, u32[]{:S(2)}, u32[]{:S(2)}) collective-permute-start(bf16[512,128]{1,0:T(8,128)(2,1)S(1)} %get-tuple-element.176), channel_id=1, source_target_pairs={{0,8},{1,20},{2,4},{3,24},{4,12},{5,16},{6,0},{7,28},{8,1},{9,29},... | collective-permute-start | bytes 393224 | tf_op jit(solution)/shard_map/ppermute | solution.py:592
  93.1 11.6 %collective-permute-start.24 = (bf16[512,128]{1,0:T(8,128)(2,1)S(1)}, bf16[512,128]{1,0:T(8,128)(2,1)S(1)}, u32[]{:S(2)}, u32[]{:S(2)}) collective-permute-start(bf16[512,128]{1,0:T(8,128)(2,1)S(1)} %get-tuple-element.177), channel_id=1, source_target_pairs={{0,20},{1,8},{2,24},{3,4},{4,16},{5,12},{6,28},{7,0},{8,29},{9,1},... | collective-permute-start | bytes 393224 | tf_op jit(solution)/shard_map/ppermute | solution.py:592
  96.2 11.9 %collective-permute-start.28 = (bf16[512,128]{1,0:T(8,128)(2,1)S(1)}, bf16[512,128]{1,0:T(8,128)(2,1)S(1)}, u32[]{:S(2)}, u32[]{:S(2)}) collective-permute-start(bf16[512,128]{1,0:T(8,128)(2,1)S(1)} %get-tuple-element.183), channel_id=1, source_target_pairs={{0,12},{1,0},{2,16},{3,28},{4,8},{5,4},{6,20},{7,24},{8,25},{9,21}... | collective-permute-start | bytes 393224 | tf_op jit(solution)/shard_map/ppermute | solution.py:592
  102.7 9.9 %collective-permute-start.29 = (bf16[512,128]{1,0:T(8,128)(2,1)S(1)}, bf16[512,128]{1,0:T(8,128)(2,1)S(1)}, u32[]{:S(2)}, u32[]{:S(2)}) collective-permute-start(bf16[512,128]{1,0:T(8,128)(2,1)S(1)} %get-tuple-element.184), channel_id=1, source_target_pairs={{0,0},{1,12},{2,28},{3,16},{4,4},{5,8},{6,24},{7,20},{8,21},{9,25}... | collective-permute-start | bytes 393224 | tf_op jit(solution)/shard_map/ppermute | solution.py:592
  (13 other events, 108.2 us)
